TPU v7x, 32 devices: a whole 2x2x4 slice. The times are simulated.
32 devices in a mesh: grp: 2 (over x), row: 16 (over z, y, core).
Axes of the slice: x: 2, y: 2, z: 4, core: 2. Of those that a mesh axis runs over, the one named last changes fastest.
Arguments:
- amp_exch: bfloat16 [256, 256, 256], P(('grp', 'row')), parts along dimension 0, may hold values from -250 to 250
- pno_energy: float32 [256, 256], P(('grp', 'row')), parts along dimension 0, may hold values from 0.3 to 3
- pair_gap: float32 [256], P(('grp', 'row')), parts along dimension 0, may hold values from 0.5 to 1.5
- fock: float32 [256, 8], P(('grp', 'row')), parts along dimension 0, may hold values from -0.4 to 0.4
- intersection: bfloat16 [256, 8, 256, 256], P(('grp', 'row')), parts along dimension 0, may hold values from -0.375 to 0.375
- nbr_slot: int32 [256, 8], P(('grp', 'row')), parts along dimension 0, may hold values from 4 to 19, as said below
- nbr_live: int32 [256, 8], P(('grp', 'row')), parts along dimension 0, may hold values from 0 to 1, as said below
- pair_live: int32 [256], P(('grp', 'row')), parts along dimension 0, may hold values 0 or 1
Outputs:
- amplitudes: float32 [256, 256, 256], P(('grp', 'row')), parts along dimension 0
- residual_norms: float32 [4], P('grp'), parts along dimension 0
There are 2 independent parts, one for each index of `grp`. A program takes and returns all parts, laid end to end along the dimension named above; each array names one. Nothing has to cross between parts.
Inputs may be any that keep to these rules, and one draw needn't show every extreme that they name: `nbr_slot`: an entry names a slot among the last 4 of the previous device, any slot of this device, or among the first 4 of the next device; both ends are named in every draw. `nbr_live`: the share of live entries differs from device to device.
All inputs are finite; a program needn't handle non-finite values. No bound on the sum of `pair_live` on one device may be relied on, other than what follows from the above.
Results may differ from a plain program's by a relative error of at most 0.0029.
Values may be sent and summed in bfloat16 or wider, within the bound.
No kernel may reach another device: no remote copies, remote signals or barrier semaphores. Data moves between devices by JAX's collectives and lax.ppermute only.
A program may use at most 64 MiB of HBM per device.

v0:
```python
import jax
import jax.numpy as jnp
from jax import lax
from jax.sharding import PartitionSpec as P

PAIR_DEV = 8
ITERS = 2


def with_halo(array, sides, width):
    for axis, dim in sides:
        count, length = (lax.axis_size(axis), array.shape[dim])
        up = [(i, (i + 1) % count) for i in range(count - 1)]
        down = [(j, i) for i, j in up]
        last = lax.slice_in_dim(array, length - width, length, axis=dim)
        initial = lax.slice_in_dim(array, 0, width, axis=dim)
        before = lax.ppermute(last, axis, up)
        after = lax.ppermute(initial, axis, down)
        array = jnp.concatenate([before, array, after], axis=dim)
    return array


def on_device(amp_exch, pno_energy, pair_gap, fock, intersection, nbr_slot, nbr_live, pair_live):
    slots = amp_exch.shape[0]
    orbitals = amp_exch.shape[1]
    denominator = pno_energy[:, :, None] + pno_energy[:, None, :] + pair_gap[:, None, None]
    coupling = fock * nbr_live.astype(jnp.float32)
    live_pairs = pair_live.astype(jnp.float32)[:, None, None]
    exchange = amp_exch.astype(jnp.float32)
    amplitudes = -live_pairs * exchange / denominator
    global_sums = []
    for sweep in range(ITERS):
        rounded = amplitudes.astype(jnp.bfloat16)
        extended = with_halo(rounded, (("row", 0),), PAIR_DEV)
        sources = extended[nbr_slot]
        half_done = jnp.einsum(
            "pnab,pnbc->pnac", intersection, sources, preferred_element_type=jnp.float32
        ).astype(jnp.bfloat16)
        transformed = jnp.einsum(
            "pnac,pndc->pnad", half_done, intersection, preferred_element_type=jnp.float32
        )
        coupled = jnp.sum(coupling[:, :, None, None] * transformed, axis=1)
        residual = live_pairs * (exchange + denominator * amplitudes - coupled)
        squared = jnp.sum(residual * residual)
        global_sums.append(lax.psum(squared, "row"))
        amplitudes = amplitudes - residual / denominator
    square_sums = jnp.stack(global_sums)
    total_pairs = slots * lax.axis_size("row")
    residual_norms = jnp.sqrt(square_sums / (total_pairs * orbitals * orbitals))
    return (amplitudes, residual_norms)


def solution(mesh):
    return jax.shard_map(
        on_device,
        mesh=mesh,
        in_specs=(
            P(("grp", "row"), None, None),
            P(("grp", "row"), None),
            P(("grp", "row")),
            P(("grp", "row"), None),
            P(("grp", "row"), None, None, None),
            P(("grp", "row"), None),
            P(("grp", "row"), None),
            P(("grp", "row")),
        ),
        out_specs=(P(("grp", "row"), None, None), P("grp")),
        check_vma=False,
    )
```

profile of v0, /device:TPU:0, one launch (start us, length us, event | category | flops | bytes accessed | tf_op | source)
XLA Modules:
  0.0 139.8 jit_solution(4962342072897085214)
XLA Ops:
  0.6 0.0 copy-start.11
  0.6 0.0 copy-start.10
  0.7 0.0 copy-start.9
  0.7 0.0 copy-start.8
  0.7 0.7 convert_negate_fusion
  1.4 1.8 %fusion.12 = bf16[8,256,256]{2,1,0:T(8,128)(2,1)S(1)} fusion(f32[8]{0:T(128)} %param.10, f32[8,256]{1,0:T(8,128)} %param.9, bf16[8,256,256]{2,1,0:T(8,128)(2,1)} %param.8, f32[8]{0:T(128)S(1)} %convert_negate_fusion), kind=kLoop, calls=%fused_computation.29 | loop fusion | flops 3145728 | bytes 2105408 | tf_op jit(solution)/shard_map/convert_element_type | solution.py:33
  3.2 0.0 copy-start.4
  3.2 1.3 collective-permute-start.1
  4.5 4.0 %collective-permute-start = (bf16[8,256,256]{2,1,0:T(8,128)(2,1)S(1)}, bf16[8,256,256]{2,1,0:T(8,128)(2,1)}, u32[]{:S(2)}, u32[]{:S(2)}) collective-permute-start(bf16[8,256,256]{2,1,0:T(8,128)(2,1)S(1)} %fusion.12), channel_id=1, source_target_pairs={{0,1},{1,2},{2,3},{3,4},{4,5},{5,6},{6,7},{7,8},{8,9},{9,10},{10,1... | collective-permute-start | bytes 3145736 | tf_op jit(solution)/shard_map/ppermute | solution.py:17
  8.5 0.0 copy-done.11
  8.5 0.0 copy-done.10
  8.6 0.1 reshape.13
  8.6 0.0 copy-done.9
  8.6 0.0 copy-done.8
  8.7 0.0 collective-permute-done.1
  8.7 0.0 copy-done.4
  8.7 0.0 copy-start.5
  8.7 1.0 copy-done.5
  9.7 0.3 collective-permute-done
  9.9 2.0 %pad_maximum_fusion = bf16[24,256,256]{2,1,0:T(8,128)(2,1)S(1)} fusion(bf16[8,256,256]{2,1,0:T(8,128)(2,1)} %copy-done.5, bf16[8,256,256]{2,1,0:T(8,128)(2,1)} %copy-done.4, bf16[8,256,256]{2,1,0:T(8,128)(2,1)} %collective-permute-done), kind=kLoop, calls=%fused_computation.8 | loop fusion | flops 3145728 | bytes 6291456 | tf_op jit(solution)/shard_map/concatenate | solution.py:19
  12.0 5.5 %gather_fusion = bf16[64,256,256]{2,1,0:T(8,128)(2,1)} fusion(bf16[24,256,256]{2,1,0:T(8,128)(2,1)S(1)} %pad_maximum_fusion, s32[1024]{0:T(1024)S(1)} %pad_clamp_fusion), kind=kCustom, calls=%fused_computation | custom fusion | bytes 16777472 | tf_op jit(solution)/shard_map/gather | solution.py:35
  17.4 0.0 copy-start
  17.4 0.0 copy-start.6
  17.4 0.0 copy-start.7
  17.4 13.2 %multiply_reduce_fusion.1 = f32[8,256,256]{2,1,0:T(8,128)S(1)} fusion(bf16[8,8,256,256]{3,2,1,0:T(8,128)(2,1)} %param.12, bf16[8,8,256,256]{3,2,1,0:T(8,128)(2,1)} %bitcast.11, f32[8,8]{1,0:T(8,128)S(1)} %convert_multiply_fusion.1), kind=kOutput, calls=%fused_computation.3 | convolution fusion | flops 4307025920 | bytes 18874624 | tf_op jit(solution)/shard_map/pnac,pndc->pnad/dot_general | solution.py:39
  30.6 0.0 copy-done
  30.6 0.0 copy-done.6
  30.6 0.0 copy-done.7
  30.6 0.0 copy-start.2
  30.6 2.1 %fusion.13 = (bf16[8,256,256]{2,1,0:T(8,128)(2,1)S(1)}, f32[8,256,256]{2,1,0:T(8,128)}) fusion(f32[8,256,256]{2,1,0:T(8,128)S(1)} %multiply_reduce_fusion.1, f32[8]{0:T(128)S(1)} %convert_element_type.23, f32[8]{0:T(128)S(1)} %copy-done.7, f32[8,256]{1,0:T(8,128)S(1)} %copy-done.6, bf16[8,256,256]{2,1,0:T(8,128)(2,1)S(1)} %copy-done, f32[8]{0:T(128)S(1)} %convert_negate_fusion), kind=kLoop, calls=%fused_computation.30 | loop fusion | flops 6291456 | bytes 6299744 | tf_op jit(solution)/shard_map/convert_element_type | solution.py:33
  32.7 0.0 copy-done.2
  32.7 1.3 collective-permute-start.3
  34.0 24.7 %collective-permute-start.2 = (bf16[8,256,256]{2,1,0:T(8,128)(2,1)S(1)}, bf16[8,256,256]{2,1,0:T(8,128)(2,1)S(1)}, u32[]{:S(2)}, u32[]{:S(2)}) collective-permute-start(bf16[8,256,256]{2,1,0:T(8,128)(2,1)S(1)} %get-tuple-element.6), channel_id=1, source_target_pairs={{0,1},{1,2},{2,3},{3,4},{4,5},{5,6},{6,7},{7,8},{8,9},{9,10},{10,1... | collective-permute-start | bytes 3145736 | tf_op jit(solution)/shard_map/ppermute | solution.py:17
  58.7 0.1 collective-permute-done.3
  58.9 2.1 %collective-permute-done.2 = bf16[8,256,256]{2,1,0:T(8,128)(2,1)S(1)} collective-permute-done((bf16[8,256,256]{2,1,0:T(8,128)(2,1)S(1)}, bf16[8,256,256]{2,1,0:T(8,128)(2,1)S(1)}, u32[]{:S(2)}, u32[]{:S(2)}) %collective-permute-start.2) | collective-permute-done | bytes 1048608 | tf_op jit(solution)/shard_map/ppermute | solution.py:17
  60.9 0.4 pad_maximum_fusion.1
  61.3 5.5 %gather_fusion.1 = bf16[64,256,256]{2,1,0:T(8,128)(2,1)} fusion(bf16[24,256,256]{2,1,0:T(8,128)(2,1)S(1)} %pad_maximum_fusion.1, s32[1024]{0:T(1024)S(1)} %pad_clamp_fusion), kind=kCustom, calls=%fused_computation.1 | custom fusion | bytes 16777472 | tf_op jit(solution)/shard_map/gather | solution.py:35
  66.8 0.0 copy-start.1
  66.8 0.0 copy-start.3
  66.8 14.5 %multiply_reduce_fusion = f32[8,256,256]{2,1,0:T(8,128)} fusion(bf16[8,8,256,256]{3,2,1,0:T(8,128)(2,1)} %param.12, bf16[8,8,256,256]{3,2,1,0:T(8,128)(2,1)} %bitcast.10, f32[8,8]{1,0:T(8,128)S(1)} %convert_multiply_fusion.1), kind=kOutput, calls=%fused_computation.2 | convolution fusion | flops 4307025920 | bytes 18874624 | tf_op jit(solution)/shard_map/pnac,pndc->pnad/dot_general | solution.py:39
  81.2 0.0 copy-done.1
  81.2 0.0 copy-done.3
  81.2 4.8 %multiply_reduce_fusion.3 = (f32[]{:T(128)}, f32[]{:T(128)}, f32[8,256,256]{2,1,0:T(8,128)}) fusion(f32[8,256,256]{2,1,0:T(8,128)S(1)} %copy-done.3, f32[8]{0:T(128)S(1)} %copy-done.7, f32[8,256]{1,0:T(8,128)S(1)} %copy-done.6, bf16[8,256,256]{2,1,0:T(8,128)(2,1)S(1)} %copy-done.1, f32[8]{0:T(128)S(1)} %convert_element_type.23, f32[8]{0:T(128)S(1)} %convert_negate_fusion, ...), kind=kLoop, calls=%fused_computation.19 | loop fusion | flops 9961470 | bytes 9445480 | tf_op jit(solution)/shard_map/reduce_sum | solution.py:44
  86.0 52.0 %all-reduce = (f32[1]{0:T(128)}, f32[1]{0:T(128)}) all-reduce(f32[1]{0:T(128)} %bitcast.3, f32[1]{0:T(128)} %bitcast.2), channel_id=1, replica_groups=mesh['grp'=2,'row'=16] {'row'}, use_global_device_ids=true, to_apply=%region_5.0 | all-reduce | flops 2 | bytes 16 | tf_op jit(solution)/shard_map/psum | solution.py:45
  138.0 1.8 %fusion.11 = f32[2]{0:T(128)} fusion(f32[1]{0:T(128)} %get-tuple-element.4, f32[1]{0:T(128)} %get-tuple-element.5), kind=kLoop, calls=%fused_computation.27 | loop fusion | flops 4 | bytes 16 | tf_op jit(solution)/shard_map/sqrt | solution.py:49
  (4 shorter events, 0.0 us)
Async XLA Ops:
  0.6 7.9 %copy-start.11 = (s32[8]{0:T(128)S(1)}, s32[8]{0:T(128)}, u32[]{:S(2)}) copy-start(s32[8]{0:T(128)} %param.15) | copy-start | bytes 100
  0.6 7.9 %copy-start.10 = (s32[8,8]{1,0:T(8,128)S(1)}, s32[8,8]{1,0:T(8,128)}, u32[]{:S(2)}) copy-start(s32[8,8]{1,0:T(8,128)} %param.13) | copy-start | bytes 772
  0.7 8.0 %copy-start.9 = (s32[8,8]{1,0:T(8,128)S(1)}, s32[8,8]{1,0:T(8,128)}, u32[]{:S(2)}) copy-start(s32[8,8]{1,0:T(8,128)} %param.14) | copy-start | bytes 772
  0.7 8.0 %copy-start.8 = (f32[8,8]{1,0:T(8,128)S(1)}, f32[8,8]{1,0:T(8,128)}, u32[]{:S(2)}) copy-start(f32[8,8]{1,0:T(8,128)} %param.11) | copy-start | bytes 772
  3.2 5.5 %copy-start.4 = (bf16[8,256,256]{2,1,0:T(8,128)(2,1)}, bf16[8,256,256]{2,1,0:T(8,128)(2,1)S(1)}, u32[]{:S(2)}) copy-start(bf16[8,256,256]{2,1,0:T(8,128)(2,1)S(1)} %fusion.12) | copy-start | bytes 3145732
  3.2 5.5 %collective-permute-start.1 = (bf16[8,256,256]{2,1,0:T(8,128)(2,1)S(1)}, bf16[8,256,256]{2,1,0:T(8,128)(2,1)S(1)}, u32[]{:S(2)}, u32[]{:S(2)}) collective-permute-start(bf16[8,256,256]{2,1,0:T(8,128)(2,1)S(1)} %fusion.12), channel_id=1, source_target_pairs={{1,0},{2,1},{3,2},{4,3},{5,4},{6,5},{7,6},{8,7},{9,8},{10,9},{11,1... | collective-permute-start | bytes 3145736 | tf_op jit(solution)/shard_map/ppermute | solution.py:18
  4.5 5.4 %collective-permute-start = (bf16[8,256,256]{2,1,0:T(8,128)(2,1)S(1)}, bf16[8,256,256]{2,1,0:T(8,128)(2,1)}, u32[]{:S(2)}, u32[]{:S(2)}) collective-permute-start(bf16[8,256,256]{2,1,0:T(8,128)(2,1)S(1)} %fusion.12), channel_id=1, source_target_pairs={{0,1},{1,2},{2,3},{3,4},{4,5},{5,6},{6,7},{7,8},{8,9},{9,10},{10,1... | collective-permute-start | bytes 3145736 | tf_op jit(solution)/shard_map/ppermute | solution.py:17
  8.7 1.0 copy-start.5
  17.4 13.2 %copy-start = (bf16[8,256,256]{2,1,0:T(8,128)(2,1)S(1)}, bf16[8,256,256]{2,1,0:T(8,128)(2,1)}, u32[]{:S(2)}) copy-start(bf16[8,256,256]{2,1,0:T(8,128)(2,1)} %param.8) | copy-start | bytes 3145732
  17.4 13.2 %copy-start.6 = (f32[8,256]{1,0:T(8,128)S(1)}, f32[8,256]{1,0:T(8,128)}, u32[]{:S(2)}) copy-start(f32[8,256]{1,0:T(8,128)} %param.9) | copy-start | bytes 24580
  17.4 13.2 %copy-start.7 = (f32[8]{0:T(128)S(1)}, f32[8]{0:T(128)}, u32[]{:S(2)}) copy-start(f32[8]{0:T(128)} %param.10) | copy-start | bytes 100
  30.6 2.1 %copy-start.2 = (f32[8,256,256]{2,1,0:T(8,128)}, f32[8,256,256]{2,1,0:T(8,128)S(1)}, u32[]{:S(2)}) copy-start(f32[8,256,256]{2,1,0:T(8,128)S(1)} %multiply_reduce_fusion.1) | copy-start | bytes 6291460
  32.7 26.2 %collective-permute-start.3 = (bf16[8,256,256]{2,1,0:T(8,128)(2,1)S(1)}, bf16[8,256,256]{2,1,0:T(8,128)(2,1)S(1)}, u32[]{:S(2)}, u32[]{:S(2)}) collective-permute-start(bf16[8,256,256]{2,1,0:T(8,128)(2,1)S(1)} %get-tuple-element.6), channel_id=1, source_target_pairs={{1,0},{2,1},{3,2},{4,3},{5,4},{6,5},{7,6},{8,7},{9,8},{10,9},{11,1... | collective-permute-start | bytes 3145736 | tf_op jit(solution)/shard_map/ppermute | solution.py:18
  34.0 26.9 %collective-permute-start.2 = (bf16[8,256,256]{2,1,0:T(8,128)(2,1)S(1)}, bf16[8,256,256]{2,1,0:T(8,128)(2,1)S(1)}, u32[]{:S(2)}, u32[]{:S(2)}) collective-permute-start(bf16[8,256,256]{2,1,0:T(8,128)(2,1)S(1)} %get-tuple-element.6), channel_id=1, source_target_pairs={{0,1},{1,2},{2,3},{3,4},{4,5},{5,6},{6,7},{7,8},{8,9},{9,10},{10,1... | collective-permute-start | bytes 3145736 | tf_op jit(solution)/shard_map/ppermute | solution.py:17
  66.8 14.5 %copy-start.1 = (bf16[8,256,256]{2,1,0:T(8,128)(2,1)S(1)}, bf16[8,256,256]{2,1,0:T(8,128)(2,1)}, u32[]{:S(2)}) copy-start(bf16[8,256,256]{2,1,0:T(8,128)(2,1)} %param.8) | copy-start | bytes 3145732
  66.8 14.5 %copy-start.3 = (f32[8,256,256]{2,1,0:T(8,128)S(1)}, f32[8,256,256]{2,1,0:T(8,128)}, u32[]{:S(2)}) copy-start(f32[8,256,256]{2,1,0:T(8,128)} %copy-done.2) | copy-start | bytes 6291460
where the time goes:
time: 140 us
  blocking collectives  52 us (37%)
  starting transfers between devices  31.3 us (22%)
  matrix products  27.6 us (20%)
  other arithmetic  13.6 us (10%)
  local copies, waits for them, and re-layouts  12 us (9%)
  waiting for transfers between devices  2.47 us (2%)
    psum x1, blocking collectives, on_device(): global_sums.append(lax.psum(squared, 'row'))  52 us
    ppermute x2, starting transfers between devices, with_halo(): before = lax.ppermute(last, axis, up)  28.8 us
    dot_general x2, matrix products, on_device(): jnp.einsum('pnac,pndc->pnad', half_done, intersection, preferred_element_...  27.6 us
    gather x2, local copies, waits for them, and re-layouts, on_device(): sources = extended[nbr_slot]  10.9 us
    reduce_sum x1, other arithmetic, on_device(): squared = jnp.sum(residual * residual)  4.77 us
    convert_element_type x2, other arithmetic, on_device(): rounded = amplitudes.astype(jnp.bfloat16)  3.87 us
  transfers between devices with their start and end apart: 4, of which 3 were waited for; matrix products, arithmetic and copies ran while one was open for 0% of the time, Pallas kernels for 0%

commit v1 on v0

v1 whole, which is shorter than its diff:
```python
import functools

import jax
import jax.numpy as jnp
from jax import lax
from jax.experimental import pallas as pl
from jax.experimental.pallas import tpu as pltpu
from jax.sharding import PartitionSpec as P

F32 = jnp.float32
BF16 = jnp.bfloat16
VM = pl.BlockSpec(memory_space=pltpu.VMEM)
SM = pl.BlockSpec(memory_space=pltpu.SMEM)
AN = pl.BlockSpec(memory_space=pl.ANY)
CAP = 72
UNROLL = 4
MIB = 1 << 20


def base_slot():
    return lax.rem(lax.axis_index("row"), 2) * 4


def params(mib, **kw):
    return pltpu.CompilerParams(vmem_limit_bytes=mib * MIB, **kw)


def cost(flops, nbytes):
    return pl.CostEstimate(flops=flops, bytes_accessed=nbytes, transcendentals=0)


def vmem(x):
    return pltpu.with_memory_space_constraint(x, pltpu.VMEM)


def denominators(energy, gap, slots):
    rows = [energy[pl.ds(p, 1), :] for p in slots]
    fill = [jnp.zeros_like(rows[0])] * (8 - len(rows))
    cols = jnp.transpose(jnp.concatenate(rows + fill, axis=0))
    return [cols[:, i : i + 1] + rows[i] + gap[p] for i, p in enumerate(slots)]


def start_tiles(first, exch, energy, gap, live, out, buf, sem):
    base = base_slot()
    slots = [(q + base) & 7 for q in range(first, first + 4)]
    copies = [pltpu.make_async_copy(exch.at[p], buf.at[i], sem.at[i]) for i, p in enumerate(slots)]
    for c in copies:
        c.start()
    dens = denominators(energy, gap, slots)
    for i, p in enumerate(slots):
        copies[i].wait()
        out[i] = (-live[p].astype(F32) * buf[i].astype(F32) / dens[i]).astype(BF16)


def first_kernel(exch, energy, gap, live, out, buf, sem):
    start_tiles(0, exch, energy, gap, live, out, buf, sem)


def second_kernel(exch, energy, gap, live, fock, nslot, nlive, out, lists, coefs, counts, buf, sem):
    start_tiles(4, exch, energy, gap, live, out, buf, sem)
    base = base_slot()
    odd = base != 0

    def entry(i, carry):
        na, nxa, nxb = carry
        q, n = i >> 3, i & 7
        p = (q + base) & 7
        v = nslot[p, n]
        on = (nlive[p, n] != 0) & (live[p] != 0)
        one = jnp.where(on, 1, 0)
        prev, nxt = v < 8, v >= 16
        across = (prev & jnp.logical_not(odd)) | (nxt & odd)
        near = (prev & odd) | (nxt & jnp.logical_not(odd))
        index = jnp.where(prev, v - 4, v - 16)
        src = jnp.where(across, index, jnp.where(near, 8 + index, (v - 8 + base) & 7))
        code = (src << 9) | (q << 6) | (p << 3) | n
        pos = jnp.where(across, jnp.where(q < 4, CAP + nxa, 2 * CAP + nxb), na)
        lists[pos] = code
        coefs[pos] = fock[p, n] * nlive[p, n].astype(F32)
        na = na + jnp.where(across, 0, one)
        nxa = nxa + jnp.where(across & (q < 4), one, 0)
        nxb = nxb + jnp.where(across & (q >= 4), one, 0)
        return na, nxa, nxb

    zero = jnp.int32(0)
    ends = lax.fori_loop(0, 64, entry, (zero, zero, zero))
    for k, e in enumerate(ends):
        counts[k] = e
        for u in range(UNROLL):
            lists[k * CAP + e + u] = 0
            coefs[k * CAP + e + u] = 0.0


def run_list(which, lists, coefs, counts, inter, src, acc):
    off = which * CAP
    chunks = (counts[which] + (UNROLL - 1)) // UNROLL

    def chunk(i, _):
        halves = []
        for u in range(UNROLL):
            code = lists[off + i * UNROLL + u]
            n, p, q, s = code & 7, (code >> 3) & 7, (code >> 6) & 7, code >> 9
            x = inter[p, n]
            h = jnp.dot(x, src[s], preferred_element_type=F32).astype(BF16)
            halves.append((coefs[off + i * UNROLL + u], q, x, h))
        for c, q, x, h in halves:
            t = lax.dot_general(h, x, (((1,), (1,)), ((), ())), preferred_element_type=F32)
            acc[q] = acc[q] - c * t
        return 0

    lax.fori_loop(0, chunks, chunk, 0)


def near_kernel_1(lists, coefs, counts, gap, live, inter, exch, energy, x, i, ih, acc, amps, recip, src):
    base = base_slot()
    slots = [(q + base) & 7 for q in range(8)]
    dens = denominators(energy, gap, slots)
    for q, p in enumerate(slots):
        ex = exch[p].astype(F32)
        a0 = -live[p].astype(F32) * ex / dens[q]
        amps[q] = a0
        recip[q] = 1.0 / dens[q]
        acc[q] = ex + dens[q] * a0
    src[0:4] = x[...]
    src[4:8] = i[...]
    src[8:12] = ih[...]
    run_list(0, lists, coefs, counts, inter, src, acc)


def across_kernel(first, lists, coefs, counts, live, inter, xh, recip, acc_in, amps_in, out, acc, amps):
    del acc_in, amps_in
    base = base_slot()
    run_list(1 if first == 0 else 2, lists, coefs, counts, inter, xh, acc)
    for j in range(4):
        q = first + j
        res = live[(q + base) & 7].astype(F32) * acc[q]
        a1 = amps[q] - res * recip[q]
        amps[q] = a1
        out[j] = a1.astype(BF16)


def squares(res):
    s = jnp.sum((res * res).reshape(32, 8, 256), axis=0)
    return s[:, :128] + s[:, 128:]


def near_kernel_2(lists, coefs, counts, gap, live, inter, exch, energy, x, i, ih, amps, acc_in, acc, sq, src):
    del acc_in
    base = base_slot()
    slots = [(q + base) & 7 for q in range(8)]
    dens = denominators(energy, gap, slots)
    total = jnp.zeros((8, 128), F32)
    for q, p in enumerate(slots):
        total = total + squares(live[p].astype(F32) * acc[q])
        acc[q] = exch[p].astype(F32) + dens[q] * amps[q]
    sq[...] = total
    src[0:4] = x[...]
    src[4:8] = i[...]
    src[8:12] = ih[...]
    run_list(0, lists, coefs, counts, inter, src, acc)


def last_kernel(lists, coefs, counts, live, inter, xh, recip, amps, sq1, acc_in, out, sums, acc, buf, sem):
    del acc_in
    base = base_slot()
    total = jnp.zeros((8, 128), F32)
    copies = []
    for half in range(2):
        run_list(1 + half, lists, coefs, counts, inter, xh, acc)
        for q in range(4 * half, 4 * half + 4):
            p = (q + base) & 7
            res = live[p].astype(F32) * acc[q]
            total = total + squares(res)
            buf[q] = amps[q] - res * recip[q]
            copies.append(pltpu.make_async_copy(buf.at[q], out.at[p], sem.at[q]))
            copies[-1].start()
    first = jnp.sum(sq1[...], axis=0, keepdims=True)
    second = jnp.sum(total, axis=0, keepdims=True)
    row = lax.broadcasted_iota(jnp.int32, (8, 128), 0)
    sums[...] = jnp.where(row == 0, first, jnp.where(row == 1, second, 0.0))
    for c in copies:
        c.wait()


def on_device(amp_exch, pno_energy, pair_gap, fock, intersection, nbr_slot, nbr_live, pair_live):
    count = lax.axis_size("row")
    v = amp_exch.shape[-1]
    tiles4 = pltpu.VMEM((4, v, v), BF16)
    tiles8 = pltpu.VMEM((8, v, v), F32)
    stage = [pltpu.VMEM((4, v, v), BF16), pltpu.SemaphoreType.DMA((4,))]
    same_chip = [(i, i ^ 1) for i in range(count) if (i ^ 1) < count]
    other_chip = [(i, i + 1) for i in range(1, count - 1, 2)]
    other_chip += [(j, i) for i, j in other_chip]

    x0 = pl.pallas_call(
        first_kernel, out_shape=tiles4, in_specs=[AN, VM, SM, SM], out_specs=VM, scratch_shapes=stage,
        compiler_params=params(8), cost_estimate=cost(10**6, 10**6), name="first",
    )(amp_exch, pno_energy, pair_gap, pair_live)
    xh = lax.ppermute(x0, "row", other_chip)
    i0, lists, coefs, counts = pl.pallas_call(
        second_kernel,
        out_shape=[tiles4, pltpu.SMEM((3 * CAP,), jnp.int32), pltpu.SMEM((3 * CAP,), F32), pltpu.SMEM((3,), jnp.int32)],
        in_specs=[AN, VM] + [SM] * 5, out_specs=[VM, SM, SM, SM], scratch_shapes=stage,
        compiler_params=params(8), cost_estimate=cost(10**6, 10**6), name="second",
    )(amp_exch, pno_energy, pair_gap, pair_live, fock, nbr_slot, nbr_live)
    ih = lax.ppermute(i0, "row", same_chip)
    inter, exch = vmem(intersection), vmem(amp_exch)
    meta = (lists, coefs, counts)
    gathered = [pltpu.VMEM((12, v, v), BF16)]
    acc, amps, recip = pl.pallas_call(
        near_kernel_1, out_shape=[tiles8] * 3, in_specs=[SM] * 5 + [VM] * 6, out_specs=[VM] * 3, scratch_shapes=gathered,
        compiler_params=params(16), cost_estimate=cost(3 * 10**9, 10**7), name="near1",
    )(*meta, pair_gap, pair_live, inter, exch, pno_energy, vmem(x0), vmem(i0), vmem(ih))

    def across(first, halo, acc, amps):
        return pl.pallas_call(
            functools.partial(across_kernel, first), out_shape=[tiles4, tiles8, tiles8],
            in_specs=[SM] * 4 + [VM] * 5, out_specs=[VM] * 3, input_output_aliases={7: 1, 8: 2},
            compiler_params=params(8), cost_estimate=cost(10**9, 10**6), name=f"across{first}",
        )(*meta, pair_live, inter, vmem(halo), vmem(recip), vmem(acc), vmem(amps))

    x1, acc, amps = across(0, xh, acc, amps)
    xh1 = lax.ppermute(x1, "row", other_chip)
    i1, acc, amps = across(4, xh, acc, amps)
    ih1 = lax.ppermute(i1, "row", same_chip)
    acc, sq = pl.pallas_call(
        near_kernel_2, out_shape=[tiles8, pltpu.VMEM((8, 128), F32)], in_specs=[SM] * 5 + [VM] * 8, out_specs=[VM] * 2,
        scratch_shapes=gathered, input_output_aliases={12: 0},
        compiler_params=params(16), cost_estimate=cost(3 * 10**9, 10**7), name="near2",
    )(*meta, pair_gap, pair_live, inter, exch, pno_energy, vmem(x1), vmem(i1), vmem(ih1), vmem(amps), vmem(acc))
    out, sums, _ = pl.pallas_call(
        last_kernel, out_shape=[jax.ShapeDtypeStruct((8, v, v), F32), pltpu.VMEM((8, 128), F32), tiles8],
        in_specs=[SM] * 4 + [VM] * 6, out_specs=[AN, VM, VM], input_output_aliases={9: 2},
        scratch_shapes=[pltpu.VMEM((8, v, v), F32), pltpu.SemaphoreType.DMA((8,))],
        compiler_params=params(16), cost_estimate=cost(10**9, 10**6), name="last",
    )(*meta, pair_live, inter, vmem(xh1), vmem(recip), vmem(amps), vmem(sq), vmem(acc))
    step = 1
    while step < count:
        sums = sums + lax.ppermute(sums, "row", [(i, i ^ step) for i in range(count)])
        step *= 2
    norms = jnp.sqrt(jnp.sum(sums[:2], axis=1) / (amp_exch.shape[0] * count * v * v))
    return out, norms


def solution(mesh):
    whole = P(("grp", "row"))
    return jax.shard_map(
        on_device, mesh=mesh, in_specs=(whole,) * 8, out_specs=(whole, P("grp")), check_vma=False
    )
```

time: 140 us -> 66.7 us (0.48)
  blocking collectives: 52 us -> 0 us
  matrix products: 27.6 us -> 0 us
  Pallas kernels: 0 us -> 21.2 us
  other arithmetic: 13.6 us -> 0.65 us
  waiting for transfers between devices: 2.47 us -> 7.05 us
  local copies, waits for them, and re-layouts: 12 us -> 8.68 us
  starting transfers between devices: 31.3 us -> 28.1 us
    psum x1 -> x0, blocking collectives: 52 us -> none  [on_device(): global_sums.append(lax.psum(squared, 'row'))]
    dot_general x2 -> x0, matrix products: 27.6 us -> none  [on_device(): jnp.einsum('pnac,pndc->pnad', half_done, intersection, preferred_element_...]
    pallas_call x0 -> x7, Pallas kernels: none -> 21.2 us  [the longest x1 5.1 us: on_device(): pl.pallas_call(near_kernel_1, out_shape=[tiles8] * 3, in_specs=[SM] * 5 +...]
    gather x2 -> x0, local copies, waits for them, and re-layouts: 10.9 us -> none  [on_device(): sources = extended[nbr_slot]]
    unnamed x24 -> x26, local copies, waits for them, and re-layouts: 1.01 us -> 8.68 us
    reduce_sum x1, other arithmetic: 4.77 us -> 0.12 us  [on_device(): jnp.sum(sums[:2], axis=1) / (amp_exch.shape[0] * count * v * v)]
    ppermute x4 -> x8, waiting for transfers between devices: 2.47 us -> 7.05 us  [the longest x4 6.19 us: on_device(): lax.ppermute(sums, 'row', [(i, i ^ step) for i in range(count)])]
    convert_element_type x3 -> x0, other arithmetic: 3.88 us -> none  [the longest x2 3.87 us: on_device(): rounded = amplitudes.astype(jnp.bfloat16)]
  transfers between devices with their start and end apart: 4 -> 8, of which waited for: 3 -> 5; matrix products, arithmetic and copies ran while one was open for 0% -> 0% of each run, Pallas kernels for 0% -> 18%
where the time goes in v1:
time: 66.7 us; the launch traced here: 66.4 us
  starting transfers between devices  28.1 us (42%)
  Pallas kernels  21.2 us (32%)
  local copies, waits for them, and re-layouts  8.68 us (13%)
  waiting for transfers between devices  7.05 us (11%)
  between operations  0.79 us (1%)
    ppermute x4, starting transfers between devices, on_device(): lax.ppermute(sums, 'row', [(i, i ^ step) for i in range(count)])  18 us
    unnamed x26, local copies, waits for them, and re-layouts  8.68 us
    ppermute x1, starting transfers between devices, on_device(): ih1 = lax.ppermute(i1, 'row', same_chip)  8.26 us
    ppermute x4, waiting for transfers between devices, on_device(): lax.ppermute(sums, 'row', [(i, i ^ step) for i in range(count)])  6.19 us
    pallas_call x1, Pallas kernels, on_device(): pl.pallas_call(near_kernel_1, out_shape=[tiles8] * 3, in_specs=[SM] * 5 +...  5.1 us
    pallas_call x1, Pallas kernels, on_device(): pl.pallas_call(near_kernel_2, out_shape=[tiles8, pltpu.VMEM((8, 128), F32...  5.07 us
    pallas_call x1, Pallas kernels, on_device(): pl.pallas_call(second_kernel, out_shape=[tiles4, pltpu.SMEM((3 * CAP,), j...  3.41 us
    pallas_call x1, Pallas kernels, on_device(): pl.pallas_call(last_kernel, out_shape=[jax.ShapeDtypeStruct((8, v, v), F3...  3.05 us
  transfers between devices with their start and end apart: 8, of which 5 were waited for; matrix products, arithmetic and copies ran while one was open for 0% of the time, Pallas kernels for 18%

profile of v1, /device:TPU:0, one launch (start us, length us, event | category | flops | bytes accessed | tf_op | source)
XLA Modules:
  0.0 66.4 jit_solution(1321087628773841522)
XLA Ops:
  0.6 0.0 copy-start.2
  0.6 1.2 %copy-done.2 = bf16[8,256,256]{2,1,0:T(8,128)(2,1)S(1)} copy-done((bf16[8,256,256]{2,1,0:T(8,128)(2,1)S(1)}, bf16[8,256,256]{2,1,0:T(8,128)(2,1)}, u32[]{:S(2)}) %copy-start.2) | copy-done | bytes 1048600
  1.9 0.0 copy-start.4
  1.9 0.7 %copy-done.4 = f32[8,256]{1,0:T(8,128)S(1)} copy-done((f32[8,256]{1,0:T(8,128)S(1)}, f32[8,256]{1,0:T(8,128)}, u32[]{:S(2)}) %copy-start.4) | copy-done | bytes 8216
  2.6 0.0 copy-start.6
  2.6 0.7 copy-done.6
  3.2 0.0 copy-start.8
  3.2 0.7 copy-done.8
  3.9 0.0 copy-start.10
  3.9 0.7 %copy-done.10 = f32[8,8]{1,0:T(8,128)S(1)} copy-done((f32[8,8]{1,0:T(8,128)S(1)}, f32[8,8]{1,0:T(8,128)}, u32[]{:S(2)}) %copy-start.10) | copy-done | bytes 280
  4.6 0.0 copy-start.11
  4.6 0.7 %copy-done.11 = s32[8,8]{1,0:T(8,128)S(1)} copy-done((s32[8,8]{1,0:T(8,128)S(1)}, s32[8,8]{1,0:T(8,128)}, u32[]{:S(2)}) %copy-start.11) | copy-done | bytes 280
  5.2 0.0 copy-start.12
  5.2 0.7 %copy-done.12 = s32[8,8]{1,0:T(8,128)S(1)} copy-done((s32[8,8]{1,0:T(8,128)S(1)}, s32[8,8]{1,0:T(8,128)}, u32[]{:S(2)}) %copy-start.12) | copy-done | bytes 280
  5.9 0.0 copy-start.3
  5.9 0.0 copy-start.5
  5.9 0.0 copy-start.7
  5.9 0.0 copy-start.9
  5.9 3.4 %second.1 = (bf16[4,256,256]{2,1,0:T(8,128)(2,1)S(1)}, s32[216]{0:T(256)S(4)}, f32[216]{0:T(256)S(4)}, s32[3]{0:T(128)S(4)}) custom-call(bf16[8,256,256]{2,1,0:T(8,128)(2,1)S(1)} %copy-done.2, f32[8,256]{1,0:T(8,128)S(1)} %copy-done.4, f32[8]{0:T(128)S(1)} %copy-done.8, s32[8]{0:T(128)S(1)} %copy-done.6, f32[8,8]{1,0:T(8,128)S(1)} %copy-done.10, ...), custom_call_target="tpu_custom_call" | custom-call | flops 1000000 | bytes 1000000 | tf_op jit(solution)/shard_map/second/pallas_call | solution.py:200
  9.4 0.5 collective-permute-start.1
  9.9 1.8 %first.1.x = bf16[4,256,256]{2,1,0:T(8,128)(2,1)S(1)} custom-call(bf16[8,256,256]{2,1,0:T(8,128)(2,1)S(1)} %copy-done.2, f32[8,256]{1,0:T(8,128)S(1)} %copy-done.4, f32[8]{0:T(128)S(1)} %copy-done.8, s32[8]{0:T(128)S(1)} %copy-done.6), custom_call_target="tpu_custom_call" | custom-call | flops 1000000 | bytes 1000000 | tf_op jit(solution)/shard_map/first/pallas_call | solution.py:195
  11.7 0.7 %collective-permute-start = (bf16[4,256,256]{2,1,0:T(8,128)(2,1)S(1)}, bf16[4,256,256]{2,1,0:T(8,128)(2,1)S(1)}, u32[]{:S(2)}, u32[]{:S(2)}) collective-permute-start(bf16[4,256,256]{2,1,0:T(8,128)(2,1)S(1)} %first.1.x), channel_id=1, source_target_pairs={{1,2},{3,4},{5,6},{7,8},{9,10},{11,12},{13,14},{2,1},{4,3},{6,5},{... | collective-permute-start | bytes 1572872 | tf_op jit(solution)/shard_map/ppermute | solution.py:199
  12.4 0.0 collective-permute-done.1.ih
  12.4 0.0 copy-done.3
  12.5 0.0 copy-done.5
  12.5 0.0 copy-done.7
  12.5 0.0 copy-done.9
  12.5 0.0 copy-start
  12.5 3.4 %copy-done = bf16[8,8,256,256]{3,2,1,0:T(8,128)(2,1)S(1)} copy-done((bf16[8,8,256,256]{3,2,1,0:T(8,128)(2,1)S(1)}, bf16[8,8,256,256]{3,2,1,0:T(8,128)(2,1)}, u32[]{:S(2)}) %copy-start) | copy-done | bytes 8388632
  15.9 0.0 copy-start.1
  15.9 5.1 %near1.1 = (f32[8,256,256]{2,1,0:T(8,128)S(1)}, f32[8,256,256]{2,1,0:T(8,128)S(1)}, f32[8,256,256]{2,1,0:T(8,128)S(1)}) custom-call(s32[216]{0:T(256)S(4)} %get-tuple-element.19.lists, f32[216]{0:T(256)S(4)} %get-tuple-element.20.coefs, s32[3]{0:T(128)S(4)} %get-tuple-element.21.counts, f32[8]{0:T(128)S(1)} %copy-done.9, s32[8]{0:T(128)S(1)} %copy-done.7, ...), custom_call_target="tpu_custom_call" | custom-call | flops 3000000000 | bytes 10000000 | tf_op jit(solution)/shard_map/near1/pallas_call | solution.py:210
  21.0 0.0 collective-permute-done.xh
  21.0 0.0 copy-done.1
  21.0 1.3 %across0.1 = (bf16[4,256,256]{2,1,0:T(8,128)(2,1)S(1)}, f32[8,256,256]{2,1,0:T(8,128)S(1)}, f32[8,256,256]{2,1,0:T(8,128)S(1)}) custom-call(s32[216]{0:T(256)S(4)} %get-tuple-element.19.lists, f32[216]{0:T(256)S(4)} %get-tuple-element.20.coefs, s32[3]{0:T(128)S(4)} %get-tuple-element.21.counts, ...), custom_call_target="tpu_custom_call", output_to_operand_aliasing={{1}: (7, {}), {2}: (8, {})} | custom-call | flops 1000000000 | bytes 1000000 | tf_op jit(solution)/shard_map/across0/pallas_call | solution.py:216
  22.4 1.3 %across4.1 = (bf16[4,256,256]{2,1,0:T(8,128)(2,1)S(1)}, f32[8,256,256]{2,1,0:T(8,128)S(1)}, f32[8,256,256]{2,1,0:T(8,128)S(1)}) custom-call(s32[216]{0:T(256)S(4)} %get-tuple-element.19.lists, f32[216]{0:T(256)S(4)} %get-tuple-element.20.coefs, s32[3]{0:T(128)S(4)} %get-tuple-element.21.counts, ...), custom_call_target="tpu_custom_call", output_to_operand_aliasing={{1}: (7, {}), {2}: (8, {})} | custom-call | flops 1000000000 | bytes 1000000 | tf_op jit(solution)/shard_map/across4/pallas_call | solution.py:216
  23.7 8.3 %collective-permute-start.3 = (bf16[4,256,256]{2,1,0:T(8,128)(2,1)S(1)}, bf16[4,256,256]{2,1,0:T(8,128)(2,1)S(1)}, u32[]{:S(2)}, u32[]{:S(2)}) collective-permute-start(bf16[4,256,256]{2,1,0:T(8,128)(2,1)S(1)} %get-tuple-element.30.i), channel_id=1, source_target_pairs={{0,1},{1,0},{2,3},{3,2},{4,5},{5,4},{6,7},{7,6},{8,9},{9,8},{10,11... | collective-permute-start | bytes 1572872 | tf_op jit(solution)/shard_map/ppermute | solution.py:225
  32.0 0.7 %collective-permute-start.2 = (bf16[4,256,256]{2,1,0:T(8,128)(2,1)S(1)}, bf16[4,256,256]{2,1,0:T(8,128)(2,1)S(1)}, u32[]{:S(2)}, u32[]{:S(2)}) collective-permute-start(bf16[4,256,256]{2,1,0:T(8,128)(2,1)S(1)} %get-tuple-element.26.x), channel_id=1, source_target_pairs={{1,2},{3,4},{5,6},{7,8},{9,10},{11,12},{13,14},{2,1},{4,3},{6,5},{... | collective-permute-start | bytes 1572872 | tf_op jit(solution)/shard_map/ppermute | solution.py:223
  32.6 0.8 %collective-permute-done.3.ih = bf16[4,256,256]{2,1,0:T(8,128)(2,1)S(1)} collective-permute-done((bf16[4,256,256]{2,1,0:T(8,128)(2,1)S(1)}, bf16[4,256,256]{2,1,0:T(8,128)(2,1)S(1)}, u32[]{:S(2)}, u32[]{:S(2)}) %collective-permute-start.3) | collective-permute-done | bytes 524320 | tf_op jit(solution)/shard_map/ppermute | solution.py:225
  33.5 5.1 %near2.1 = (f32[8,256,256]{2,1,0:T(8,128)S(1)}, f32[8,128]{1,0:T(8,128)S(1)}) custom-call(s32[216]{0:T(256)S(4)} %get-tuple-element.19.lists, f32[216]{0:T(256)S(4)} %get-tuple-element.20.coefs, s32[3]{0:T(128)S(4)} %get-tuple-element.21.counts, f32[8]{0:T(128)S(1)} %copy-done.9, s32[8]{0:T(128)S(1)} %copy-done.7, ...), custom_call_target="tpu_custom_call", output_to_operand_aliasing={{0}: (12, {})} | custom-call | flops 3000000000 | bytes 10000000 | tf_op jit(solution)/shard_map/near2/pallas_call | solution.py:226
  38.6 0.0 collective-permute-done.2.xh
  38.6 3.0 %last.1 = (f32[8,256,256]{2,1,0:T(8,128)}, f32[8,128]{1,0:T(8,128)S(1)}, f32[8,256,256]{2,1,0:T(8,128)S(1)}) custom-call(s32[216]{0:T(256)S(4)} %get-tuple-element.19.lists, f32[216]{0:T(256)S(4)} %get-tuple-element.20.coefs, s32[3]{0:T(128)S(4)} %get-tuple-element.21.counts, s32[8]{0:T(128)S(1)} %copy-done.7, ...), custom_call_target="tpu_custom_call", output_to_operand_aliasing={{2}: (9, {})} | custom-call | flops 1000000000 | bytes 1000000 | tf_op jit(solution)/shard_map/last/pallas_call | solution.py:231
  41.6 10.8 %collective-permute-start.4 = (f32[8,128]{1,0:T(8,128)S(1)}, f32[8,128]{1,0:T(8,128)S(1)}, u32[]{:S(2)}, u32[]{:S(2)}) collective-permute-start(f32[8,128]{1,0:T(8,128)S(1)} %get-tuple-element.35), channel_id=1, source_target_pairs={{0,1},{1,0},{2,3},{3,2},{4,5},{5,4},{6,7},{7,6},{8,9},{9,8},{10,11... | collective-permute-start | bytes 12296 | tf_op jit(solution)/shard_map/ppermute | solution.py:239
  52.5 0.8 %collective-permute-done.4 = f32[8,128]{1,0:T(8,128)S(1)} collective-permute-done((f32[8,128]{1,0:T(8,128)S(1)}, f32[8,128]{1,0:T(8,128)S(1)}, u32[]{:S(2)}, u32[]{:S(2)}) %collective-permute-start.4) | collective-permute-done | bytes 4128 | tf_op jit(solution)/shard_map/ppermute | solution.py:239
  53.3 2.8 %collective-permute-start.5 = (f32[8,128]{1,0:T(8,128)S(1)}, f32[8,128]{1,0:T(8,128)S(1)}, u32[]{:S(2)}, u32[]{:S(2)}) collective-permute-start(f32[8,128]{1,0:T(8,128)S(1)} %add.12), channel_id=1, source_target_pairs={{0,2},{1,3},{2,0},{3,1},{4,6},{5,7},{6,4},{7,5},{8,10},{9,11},{10,... | collective-permute-start | bytes 12296 | tf_op jit(solution)/shard_map/ppermute | solution.py:239
  56.1 1.6 %collective-permute-done.5 = f32[8,128]{1,0:T(8,128)S(1)} collective-permute-done((f32[8,128]{1,0:T(8,128)S(1)}, f32[8,128]{1,0:T(8,128)S(1)}, u32[]{:S(2)}, u32[]{:S(2)}) %collective-permute-start.5) | collective-permute-done | bytes 4128 | tf_op jit(solution)/shard_map/ppermute | solution.py:239
  57.7 2.0 %collective-permute-start.6 = (f32[8,128]{1,0:T(8,128)S(1)}, f32[8,128]{1,0:T(8,128)S(1)}, u32[]{:S(2)}, u32[]{:S(2)}) collective-permute-start(f32[8,128]{1,0:T(8,128)S(1)} %add.13), channel_id=1, source_target_pairs={{0,4},{1,5},{2,6},{3,7},{4,0},{5,1},{6,2},{7,3},{8,12},{9,13},{10,... | collective-permute-start | bytes 12296 | tf_op jit(solution)/shard_map/ppermute | solution.py:239
  59.7 1.6 %collective-permute-done.6 = f32[8,128]{1,0:T(8,128)S(1)} collective-permute-done((f32[8,128]{1,0:T(8,128)S(1)}, f32[8,128]{1,0:T(8,128)S(1)}, u32[]{:S(2)}, u32[]{:S(2)}) %collective-permute-start.6) | collective-permute-done | bytes 4128 | tf_op jit(solution)/shard_map/ppermute | solution.py:239
  61.3 2.3 %collective-permute-start.7 = (f32[8,128]{1,0:T(8,128)S(1)}, f32[8,128]{1,0:T(8,128)S(1)}, u32[]{:S(2)}, u32[]{:S(2)}) collective-permute-start(f32[8,128]{1,0:T(8,128)S(1)} %add.14), channel_id=1, source_target_pairs={{0,8},{1,9},{2,10},{3,11},{4,12},{5,13},{6,14},{7,15},{8,0},{9,1},... | collective-permute-start | bytes 12296 | tf_op jit(solution)/shard_map/ppermute | solution.py:239
  63.6 2.2 %collective-permute-done.7 = f32[8,128]{1,0:T(8,128)S(1)} collective-permute-done((f32[8,128]{1,0:T(8,128)S(1)}, f32[8,128]{1,0:T(8,128)S(1)}, u32[]{:S(2)}, u32[]{:S(2)}) %collective-permute-start.7) | collective-permute-done | bytes 4128 | tf_op jit(solution)/shard_map/ppermute | solution.py:239
  65.8 0.1 slice_reduce_fusion
  65.9 0.5 multiply_sqrt_fusion
  (4 shorter events, 0.0 us)
Async XLA Ops:
  0.6 1.2 %copy-start.2 = (bf16[8,256,256]{2,1,0:T(8,128)(2,1)S(1)}, bf16[8,256,256]{2,1,0:T(8,128)(2,1)}, u32[]{:S(2)}) copy-start(bf16[8,256,256]{2,1,0:T(8,128)(2,1)} %exch.7) | copy-start | bytes 3145732
  1.9 0.7 %copy-start.4 = (f32[8,256]{1,0:T(8,128)S(1)}, f32[8,256]{1,0:T(8,128)}, u32[]{:S(2)}) copy-start(f32[8,256]{1,0:T(8,128)} %energy.7) | copy-start | bytes 24580
  2.6 0.7 copy-start.6
  3.2 0.7 copy-start.8
  3.9 0.7 %copy-start.10 = (f32[8,8]{1,0:T(8,128)S(1)}, f32[8,8]{1,0:T(8,128)}, u32[]{:S(2)}) copy-start(f32[8,8]{1,0:T(8,128)} %fock.1) | copy-start | bytes 772
  4.6 0.7 %copy-start.11 = (s32[8,8]{1,0:T(8,128)S(1)}, s32[8,8]{1,0:T(8,128)}, u32[]{:S(2)}) copy-start(s32[8,8]{1,0:T(8,128)} %nslot.1) | copy-start | bytes 772
  5.2 0.7 %copy-start.12 = (s32[8,8]{1,0:T(8,128)S(1)}, s32[8,8]{1,0:T(8,128)}, u32[]{:S(2)}) copy-start(s32[8,8]{1,0:T(8,128)} %nlive.1) | copy-start | bytes 772
  5.9 6.5 %copy-start.3 = (bf16[8,256,256]{2,1,0:T(8,128)(2,1)S(1)}, bf16[8,256,256]{2,1,0:T(8,128)(2,1)}, u32[]{:S(2)}) copy-start(bf16[8,256,256]{2,1,0:T(8,128)(2,1)} %exch.7) | copy-start | bytes 3145732
  5.9 6.5 %copy-start.5 = (f32[8,256]{1,0:T(8,128)S(1)}, f32[8,256]{1,0:T(8,128)}, u32[]{:S(2)}) copy-start(f32[8,256]{1,0:T(8,128)} %energy.7) | copy-start | bytes 24580
  5.9 6.5 %copy-start.7 = (s32[8]{0:T(128)S(1)}, s32[8]{0:T(128)}, u32[]{:S(2)}) copy-start(s32[8]{0:T(128)} %live.13) | copy-start | bytes 100
  5.9 6.5 %copy-start.9 = (f32[8]{0:T(128)S(1)}, f32[8]{0:T(128)}, u32[]{:S(2)}) copy-start(f32[8]{0:T(128)} %gap.7) | copy-start | bytes 100
  9.4 3.1 %collective-permute-start.1 = (bf16[4,256,256]{2,1,0:T(8,128)(2,1)S(1)}, bf16[4,256,256]{2,1,0:T(8,128)(2,1)S(1)}, u32[]{:S(2)}, u32[]{:S(2)}) collective-permute-start(bf16[4,256,256]{2,1,0:T(8,128)(2,1)S(1)} %get-tuple-element.22.i), channel_id=1, source_target_pairs={{0,1},{1,0},{2,3},{3,2},{4,5},{5,4},{6,7},{7,6},{8,9},{9,8},{10,11... | collective-permute-start | bytes 1572872 | tf_op jit(solution)/shard_map/ppermute | solution.py:206
  11.7 9.3 %collective-permute-start = (bf16[4,256,256]{2,1,0:T(8,128)(2,1)S(1)}, bf16[4,256,256]{2,1,0:T(8,128)(2,1)S(1)}, u32[]{:S(2)}, u32[]{:S(2)}) collective-permute-start(bf16[4,256,256]{2,1,0:T(8,128)(2,1)S(1)} %first.1.x), channel_id=1, source_target_pairs={{1,2},{3,4},{5,6},{7,8},{9,10},{11,12},{13,14},{2,1},{4,3},{6,5},{... | collective-permute-start | bytes 1572872 | tf_op jit(solution)/shard_map/ppermute | solution.py:199
  12.5 3.4 %copy-start = (bf16[8,8,256,256]{3,2,1,0:T(8,128)(2,1)S(1)}, bf16[8,8,256,256]{3,2,1,0:T(8,128)(2,1)}, u32[]{:S(2)}) copy-start(bf16[8,8,256,256]{3,2,1,0:T(8,128)(2,1)} %inter.9) | copy-start | bytes 25165828
  15.9 5.1 %copy-start.1 = (bf16[8,8,256,256]{3,2,1,0:T(8,128)(2,1)S(1)}, bf16[8,8,256,256]{3,2,1,0:T(8,128)(2,1)}, u32[]{:S(2)}) copy-start(bf16[8,8,256,256]{3,2,1,0:T(8,128)(2,1)} %inter.9) | copy-start | bytes 25165828
  23.7 9.8 %collective-permute-start.3 = (bf16[4,256,256]{2,1,0:T(8,128)(2,1)S(1)}, bf16[4,256,256]{2,1,0:T(8,128)(2,1)S(1)}, u32[]{:S(2)}, u32[]{:S(2)}) collective-permute-start(bf16[4,256,256]{2,1,0:T(8,128)(2,1)S(1)} %get-tuple-element.30.i), channel_id=1, source_target_pairs={{0,1},{1,0},{2,3},{3,2},{4,5},{5,4},{6,7},{7,6},{8,9},{9,8},{10,11... | collective-permute-start | bytes 1572872 | tf_op jit(solution)/shard_map/ppermute | solution.py:225
  32.0 6.6 %collective-permute-start.2 = (bf16[4,256,256]{2,1,0:T(8,128)(2,1)S(1)}, bf16[4,256,256]{2,1,0:T(8,128)(2,1)S(1)}, u32[]{:S(2)}, u32[]{:S(2)}) collective-permute-start(bf16[4,256,256]{2,1,0:T(8,128)(2,1)S(1)} %get-tuple-element.26.x), channel_id=1, source_target_pairs={{1,2},{3,4},{5,6},{7,8},{9,10},{11,12},{13,14},{2,1},{4,3},{6,5},{... | collective-permute-start | bytes 1572872 | tf_op jit(solution)/shard_map/ppermute | solution.py:223
  41.6 11.7 %collective-permute-start.4 = (f32[8,128]{1,0:T(8,128)S(1)}, f32[8,128]{1,0:T(8,128)S(1)}, u32[]{:S(2)}, u32[]{:S(2)}) collective-permute-start(f32[8,128]{1,0:T(8,128)S(1)} %get-tuple-element.35), channel_id=1, source_target_pairs={{0,1},{1,0},{2,3},{3,2},{4,5},{5,4},{6,7},{7,6},{8,9},{9,8},{10,11... | collective-permute-start | bytes 12296 | tf_op jit(solution)/shard_map/ppermute | solution.py:239
  53.3 4.4 %collective-permute-start.5 = (f32[8,128]{1,0:T(8,128)S(1)}, f32[8,128]{1,0:T(8,128)S(1)}, u32[]{:S(2)}, u32[]{:S(2)}) collective-permute-start(f32[8,128]{1,0:T(8,128)S(1)} %add.12), channel_id=1, source_target_pairs={{0,2},{1,3},{2,0},{3,1},{4,6},{5,7},{6,4},{7,5},{8,10},{9,11},{10,... | collective-permute-start | bytes 12296 | tf_op jit(solution)/shard_map/ppermute | solution.py:239
  57.7 3.6 %collective-permute-start.6 = (f32[8,128]{1,0:T(8,128)S(1)}, f32[8,128]{1,0:T(8,128)S(1)}, u32[]{:S(2)}, u32[]{:S(2)}) collective-permute-start(f32[8,128]{1,0:T(8,128)S(1)} %add.13), channel_id=1, source_target_pairs={{0,4},{1,5},{2,6},{3,7},{4,0},{5,1},{6,2},{7,3},{8,12},{9,13},{10,... | collective-permute-start | bytes 12296 | tf_op jit(solution)/shard_map/ppermute | solution.py:239
  61.3 4.5 %collective-permute-start.7 = (f32[8,128]{1,0:T(8,128)S(1)}, f32[8,128]{1,0:T(8,128)S(1)}, u32[]{:S(2)}, u32[]{:S(2)}) collective-permute-start(f32[8,128]{1,0:T(8,128)S(1)} %add.14), channel_id=1, source_target_pairs={{0,8},{1,9},{2,10},{3,11},{4,12},{5,13},{6,14},{7,15},{8,0},{9,1},... | collective-permute-start | bytes 12296 | tf_op jit(solution)/shard_map/ppermute | solution.py:239

commit v2 on v1

v2 whole, which is shorter than its diff:
```python
import functools

import jax
import jax.numpy as jnp
from jax import lax
from jax.experimental import pallas as pl
from jax.experimental.pallas import tpu as pltpu
from jax.sharding import PartitionSpec as P

F32 = jnp.float32
BF16 = jnp.bfloat16
VM = pl.BlockSpec(memory_space=pltpu.VMEM)
SM = pl.BlockSpec(memory_space=pltpu.SMEM)
AN = pl.BlockSpec(memory_space=pl.ANY)
CAP = 72
NEAR, ACROSS = 8, 4
COUNTS, LIVE = 4 * CAP, 4 * CAP + 4
GAP = 4 * CAP
MIB = 1 << 20


def base_slot():
    return lax.rem(lax.axis_index("row"), 2) * 4


def slots_of(first, end):
    base = base_slot()
    return [(q + base) & 7 for q in range(first, end)]


def params(mib, **kw):
    return pltpu.CompilerParams(vmem_limit_bytes=mib * MIB, **kw)


COST = pl.CostEstimate(flops=1000, bytes_accessed=1000, transcendentals=0)


def vmem(x):
    return pltpu.with_memory_space_constraint(x, pltpu.VMEM)


def hbm(x):
    return pltpu.with_memory_space_constraint(x, pltpu.HBM)


def denominators(energy, gaps, slots):
    rows = [energy[pl.ds(p, 1), :] for p in slots]
    fill = [jnp.zeros_like(rows[0])] * (8 - len(rows))
    cols = jnp.transpose(jnp.concatenate(rows + fill, axis=0))
    return [cols[:, i : i + 1] + rows[i] + gaps[i] for i in range(len(slots))]


def start_all(pairs, sems):
    copies = [pltpu.make_async_copy(a, b, sems.at[i]) for i, (a, b) in enumerate(pairs)]
    for c in copies:
        c.start()
    return copies


def first_kernel(exch, energy, gap, live, out, buf, en, gp, lv, sem, sems):
    slots = slots_of(0, 4)
    small = start_all([(energy, en), (gap, gp), (live, lv)], sems)
    tiles = start_all([(exch.at[p], buf.at[i]) for i, p in enumerate(slots)], sem)
    for c in small:
        c.wait()
    dens = denominators(en, [gp[p] for p in slots], slots)
    for i, p in enumerate(slots):
        tiles[i].wait()
        out[i] = (-lv[p].astype(F32) * buf[i].astype(F32) / dens[i]).astype(BF16)


def second_kernel(
    exch, energy, gap, live, fock, nslot, nlive, inter_hbm, x, out_a, out_b, ex, en, lists, coefs, inter,
    gp, lv, fk, ns, nl, table, ends, sem, sems, slab_sem,
):
    del x
    slots = slots_of(4, 8)
    base = base_slot()
    small = start_all([(energy, en), (gap, gp), (live, lv), (fock, fk), (nslot, ns), (nlive, nl)], sems)
    order = slots + slots_of(0, 4)
    tiles = start_all([(exch.at[p], ex.at[p]) for p in order], sem)
    slabs = start_all([(inter_hbm.at[p], inter.at[p]) for p in range(8)], slab_sem)
    for c in small:
        c.wait()
    dens = denominators(en, [gp[p] for p in slots], slots)
    for i, p in enumerate(slots):
        tiles[i].wait()
        tile = (-lv[p].astype(F32) * ex[p].astype(F32) / dens[i]).astype(BF16)
        if i < 2:
            out_a[i] = tile
        else:
            out_b[i - 2] = tile

    for s in range(4):
        table[4 + s] = jnp.where(base == 0, (s << 9) | 3, ((8 + s) << 9) | 1)
        table[16 + s] = jnp.where(base == 0, ((8 + s) << 9) | 1, (s << 9) | 3)
    for s in range(8):
        table[8 + s] = (((s + base) & 7) << 9) | lv[s]
    for k in range(4):
        ends[k] = k * CAP

    def entry(i, _):
        q, n = i >> 3, i & 7
        p = (q + base) & 7
        what = table[ns[p, n]]
        which = (what & 2) + (q >> 2)
        pos = ends[which]
        lists[pos] = ((what >> 9) << 9) | (q << 6) | (p << 3) | n
        coefs[pos] = fk[p, n]
        ends[which] = pos + (nl[p, n] & lv[p] & what & 1)
        return 0

    lax.fori_loop(0, 64, entry, 0, unroll=4)
    for k in range(4):
        e = ends[k]
        lists[COUNTS + k] = e - k * CAP
        for u in range(NEAR if k < 2 else ACROSS):
            lists[e + u] = 0
            coefs[e + u] = 0.0
    for p in range(8):
        lists[LIVE + p] = lv[p]
        coefs[GAP + p] = gp[p]
    for c in tiles[4:] + slabs:
        c.wait()


def run_list(which, lists, coefs, inter, src, acc):
    unroll = NEAR if which < 2 else ACROSS
    off = which * CAP
    chunks = (lists[COUNTS + which] + (unroll - 1)) // unroll

    def chunk(i, _):
        halves = []
        for u in range(unroll):
            code = lists[off + i * unroll + u]
            n, p, q, s = code & 7, (code >> 3) & 7, (code >> 6) & 7, code >> 9
            x = inter[p, n]
            h = jnp.dot(x, src[s], preferred_element_type=F32).astype(BF16)
            halves.append((coefs[off + i * unroll + u], q, x, h))
        for c, q, x, h in halves:
            t = lax.dot_general(h, x, (((1,), (1,)), ((), ())), preferred_element_type=F32)
            acc[q] = acc[q] - c * t
        return 0

    lax.fori_loop(0, chunks, chunk, 0)


def gather(src, x, ia, ib, iha, ihb):
    src[0:4] = x[...]
    src[4:6] = ia[...]
    src[6:8] = ib[...]
    src[8:10] = iha[...]
    src[10:12] = ihb[...]


def near_kernel_1(lists, coefs, inter, exch, energy, x, ia, ib, iha, ihb, acc, amps, recip, src):
    slots = slots_of(0, 8)
    dens = denominators(energy, [coefs[GAP + p] for p in slots], slots)
    gather(src, x, ia, ib, iha, ihb)
    for q, p in enumerate(slots):
        ex = exch[p].astype(F32)
        a0 = -lists[LIVE + p].astype(F32) * ex / dens[q]
        amps[q] = a0
        recip[q] = 1.0 / dens[q]
        acc[q] = ex + dens[q] * a0
    for half in range(2):
        run_list(half, lists, coefs, inter, src, acc)


def across_kernel(half, lists, coefs, inter, xh, recip, acc_in, amps_in, *outs):
    del acc_in, amps_in
    *out, acc, amps = outs
    run_list(2 + half, lists, coefs, inter, xh, acc)
    for j, p in enumerate(slots_of(4 * half, 4 * half + 4)):
        q = 4 * half + j
        res = lists[LIVE + p].astype(F32) * acc[q]
        a1 = amps[q] - res * recip[q]
        amps[q] = a1
        each = 4 // len(out)
        out[j // each][j % each] = a1.astype(BF16)


def squares(res):
    s = jnp.sum((res * res).reshape(32, 8, 256), axis=0)
    return s[:, :128] + s[:, 128:]


def near_kernel_2(lists, coefs, inter, exch, energy, x, ia, ib, iha, ihb, amps, acc_in, acc, sq, src):
    del acc_in
    slots = slots_of(0, 8)
    dens = denominators(energy, [coefs[GAP + p] for p in slots], slots)
    total = jnp.zeros((8, 128), F32)
    for q, p in enumerate(slots):
        total = total + squares(lists[LIVE + p].astype(F32) * acc[q])
        acc[q] = exch[p].astype(F32) + dens[q] * amps[q]
    sq[...] = total
    gather(src, x, ia, ib, iha, ihb)
    for half in range(2):
        run_list(half, lists, coefs, inter, src, acc)


def last_kernel(lists, coefs, inter, xh, recip, amps, sq1, acc_in, out, sums, acc, buf, sem):
    del acc_in
    total = jnp.zeros((8, 128), F32)
    copies = []
    slots = slots_of(0, 8)
    for half in range(2):
        run_list(2 + half, lists, coefs, inter, xh, acc)
        for q in range(4 * half, 4 * half + 4):
            p = slots[q]
            res = lists[LIVE + p].astype(F32) * acc[q]
            total = total + squares(res)
            buf[q] = amps[q] - res * recip[q]
            copies.append(pltpu.make_async_copy(buf.at[q], out.at[p], sem.at[q]))
            copies[-1].start()
    lane = lax.broadcasted_iota(jnp.int32, sums.shape, 1)
    sums[...] = jnp.where(lane == 0, jnp.sum(sq1[...]), jnp.where(lane == 1, jnp.sum(total), 0.0))
    for c in copies:
        c.wait()


def on_device(amp_exch, pno_energy, pair_gap, fock, intersection, nbr_slot, nbr_live, pair_live):
    count = lax.axis_size("row")
    v = amp_exch.shape[-1]
    tiles4 = pltpu.VMEM((4, v, v), BF16)
    tiles8 = pltpu.VMEM((8, v, v), F32)
    dma = pltpu.SemaphoreType.DMA
    per_pair = [pltpu.SMEM((8,), F32), pltpu.SMEM((8,), jnp.int32)]
    same_chip = [(i, i ^ 1) for i in range(count) if (i ^ 1) < count]
    other_chip = [(i, i + 1) for i in range(1, count - 1, 2)]
    other_chip += [(j, i) for i, j in other_chip]
    big = [hbm(a) for a in (amp_exch, pno_energy, pair_gap, pair_live, fock, nbr_slot, nbr_live)]

    x0 = pl.pallas_call(
        first_kernel, out_shape=tiles4, in_specs=[AN] * 4, out_specs=VM,
        scratch_shapes=[pltpu.VMEM((4, v, v), BF16), pltpu.VMEM((8, v), F32)] + per_pair + [dma((4,)), dma((3,))],
        compiler_params=params(8), cost_estimate=COST, name="first",
    )(*big[:4])
    xh = lax.ppermute(x0, "row", other_chip)
    tiles2 = pltpu.VMEM((2, v, v), BF16)
    i0a, i0b, exch, energy, lists, coefs, inter = pl.pallas_call(
        second_kernel,
        out_shape=[tiles2, tiles2, pltpu.VMEM((8, v, v), BF16), pltpu.VMEM((8, v), F32),
                   pltpu.SMEM((LIVE + 8,), jnp.int32), pltpu.SMEM((GAP + 8,), F32), pltpu.VMEM(intersection.shape, BF16)],
        in_specs=[AN] * 9, out_specs=[VM] * 4 + [SM] * 2 + [VM],
        scratch_shapes=per_pair + [pltpu.SMEM((8, 8), F32)] + [pltpu.SMEM((8, 8), jnp.int32)] * 2
        + [pltpu.SMEM((24,), jnp.int32), pltpu.SMEM((4,), jnp.int32), dma((8,)), dma((6,)), dma((8,))],
        compiler_params=params(8), cost_estimate=COST, name="second",
    )(*big, hbm(intersection), x0)

    def swap(*halves):
        return [vmem(lax.ppermute(h, "row", same_chip)) for h in halves]

    meta = (lists, coefs)
    exch, energy, inter = vmem(exch), vmem(energy), vmem(inter)
    gathered = [pltpu.VMEM((12, v, v), BF16)]
    acc, amps, recip = pl.pallas_call(
        near_kernel_1, out_shape=[tiles8] * 3, in_specs=[SM] * 2 + [VM] * 8, out_specs=[VM] * 3, scratch_shapes=gathered,
        compiler_params=params(8), cost_estimate=COST, name="near1",
    )(*meta, inter, exch, energy, vmem(x0), vmem(i0a), vmem(i0b), *swap(i0a, i0b))

    def across(half, halo, acc, amps):
        shapes = [tiles2, tiles2] if half else [tiles4]
        k = len(shapes)
        return pl.pallas_call(
            functools.partial(across_kernel, half), out_shape=shapes + [tiles8, tiles8],
            in_specs=[SM] * 2 + [VM] * 5, out_specs=[VM] * (k + 2), input_output_aliases={5: k, 6: k + 1},
            compiler_params=params(8), cost_estimate=COST, name=f"across{half}",
        )(*meta, inter, vmem(halo), vmem(recip), vmem(acc), vmem(amps))

    x1, acc, amps = across(0, xh, acc, amps)
    xh1 = lax.ppermute(x1, "row", other_chip)
    i1a, i1b, acc, amps = across(1, xh, acc, amps)
    acc, sq = pl.pallas_call(
        near_kernel_2, out_shape=[tiles8, pltpu.VMEM((8, 128), F32)], in_specs=[SM] * 2 + [VM] * 10, out_specs=[VM] * 2,
        scratch_shapes=gathered, input_output_aliases={11: 0},
        compiler_params=params(8), cost_estimate=COST, name="near2",
    )(*meta, inter, exch, energy, vmem(x1), vmem(i1a), vmem(i1b), *swap(i1a, i1b), vmem(amps), vmem(acc))
    out, sums, _ = pl.pallas_call(
        last_kernel, out_shape=[jax.ShapeDtypeStruct((8, v, v), F32), pltpu.VMEM((count, 128), F32), tiles8],
        in_specs=[SM] * 2 + [VM] * 6, out_specs=[AN, VM, VM], input_output_aliases={7: 2},
        scratch_shapes=[pltpu.VMEM((8, v, v), F32), dma((8,))],
        compiler_params=params(8), cost_estimate=COST, name="last",
    )(*meta, inter, vmem(xh1), vmem(recip), vmem(amps), vmem(sq), vmem(acc))
    sums = lax.all_to_all(sums, "row", 0, 0, tiled=True)
    norms = jnp.sqrt(jnp.sum(sums[:, :2], axis=0) / (amp_exch.shape[0] * count * v * v))
    return out, norms


def solution(mesh):
    whole = P(("grp", "row"))
    return jax.shard_map(
        on_device, mesh=mesh, in_specs=(whole,) * 8, out_specs=(whole, P("grp")), check_vma=False
    )
```

time: 66.7 us -> 51.3 us (0.77)
  starting transfers between devices: 28.1 us -> 10.9 us
  blocking collectives: 0 us -> 16.4 us
  local copies, waits for them, and re-layouts: 8.68 us -> 0 us
  waiting for transfers between devices: 7.05 us -> 2.92 us
  Pallas kernels: 21.2 us -> 19.3 us
    ppermute x6 -> x4, starting transfers between devices: 26.7 us -> 9.56 us  [swap(): return [vmem(lax.ppermute(h, 'row', same_chip)) for h in halves]]
    all_to_all x0 -> x1, blocking collectives: none -> 16.4 us  [on_device(): sums = lax.all_to_all(sums, 'row', 0, 0, tiled=True)]
    unnamed x26 -> x0, local copies, waits for them, and re-layouts: 8.68 us -> none
    ppermute x6 -> x4, waiting for transfers between devices: 7.04 us -> 2.91 us  [swap(): return [vmem(lax.ppermute(h, 'row', same_chip)) for h in halves]]
    pallas_call x5, Pallas kernels: 13 us -> 11.9 us  [the longest x1 4.27 us: on_device(): pl.pallas_call(near_kernel_1, out_shape=[tiles8] * 3, in_specs=[SM] * 2 +...]
    pallas_call x1, Pallas kernels: 5.07 us -> 4.25 us  [on_device(): pl.pallas_call(near_kernel_2, out_shape=[tiles8, pltpu.VMEM((8, 128), F32...]
  transfers between devices with their start and end apart: 8 -> 6, of which waited for: 5 -> 4; matrix products, arithmetic and copies ran while one was open for 0% -> 0% of each run, Pallas kernels for 18% -> 27%
where the time goes in v2:
time: 51.3 us; the launch traced here: 50.9 us
  Pallas kernels  19.3 us (38%)
  blocking collectives  16.4 us (32%)
  starting transfers between devices  10.9 us (21%)
  waiting for transfers between devices  2.92 us (6%)
  between operations  0.71 us (1%)
  other arithmetic  0.54 us (1%)
    all_to_all x1, blocking collectives, on_device(): sums = lax.all_to_all(sums, 'row', 0, 0, tiled=True)  16.4 us
    ppermute x4, starting transfers between devices, swap(): return [vmem(lax.ppermute(h, 'row', same_chip)) for h in halves]  9.56 us
    pallas_call x1, Pallas kernels, on_device(): pl.pallas_call(near_kernel_1, out_shape=[tiles8] * 3, in_specs=[SM] * 2 +...  4.27 us
    pallas_call x1, Pallas kernels, on_device(): pl.pallas_call(near_kernel_2, out_shape=[tiles8, pltpu.VMEM((8, 128), F32...  4.25 us
    pallas_call x1, Pallas kernels, on_device(): pl.pallas_call(second_kernel, out_shape=[tiles2, tiles2, pltpu.VMEM((8, v...  3.93 us
    pallas_call x1, Pallas kernels, on_device(): pl.pallas_call(last_kernel, out_shape=[jax.ShapeDtypeStruct((8, v, v), F3...  3.21 us
    ppermute x4, waiting for transfers between devices, swap(): return [vmem(lax.ppermute(h, 'row', same_chip)) for h in halves]  2.91 us
    pallas_call x2, Pallas kernels, across(): pl.pallas_call(functools.partial(across_kernel, half), out_shape=shapes +...  2.22 us
  transfers between devices with their start and end apart: 6, of which 4 were waited for; matrix products, arithmetic and copies ran while one was open for 0% of the time, Pallas kernels for 27%

profile of v2, /device:TPU:0, one launch (start us, length us, event | category | flops | bytes accessed | tf_op | source)
XLA Modules:
  0.0 50.9 jit_solution(6173854957479659747)
XLA Ops:
  0.6 1.4 %first.1.x = bf16[4,256,256]{2,1,0:T(8,128)(2,1)S(1)} custom-call(bf16[8,256,256]{2,1,0:T(8,128)(2,1)} %exch.3, f32[8,256]{1,0:T(8,128)} %energy.3, f32[8]{0:T(128)} %gap.3, s32[8]{0:T(128)} %live.3), custom_call_target="tpu_custom_call" | custom-call | flops 1000 | bytes 1000 | tf_op jit(solution)/shard_map/first/pallas_call | solution.py:234
  2.1 0.7 %collective-permute-start = (bf16[4,256,256]{2,1,0:T(8,128)(2,1)S(1)}, bf16[4,256,256]{2,1,0:T(8,128)(2,1)S(1)}, u32[]{:S(2)}, u32[]{:S(2)}) collective-permute-start(bf16[4,256,256]{2,1,0:T(8,128)(2,1)S(1)} %first.1.x), channel_id=1, source_target_pairs={{1,2},{3,4},{5,6},{7,8},{9,10},{11,12},{13,14},{2,1},{4,3},{6,5},{... | collective-permute-start | bytes 1572872 | tf_op jit(solution)/shard_map/ppermute | solution.py:239
  2.8 3.9 %second.1 = (bf16[2,256,256]{2,1,0:T(8,128)(2,1)S(1)}, bf16[2,256,256]{2,1,0:T(8,128)(2,1)S(1)}, bf16[8,256,256]{2,1,0:T(8,128)(2,1)S(1)}, f32[8,256]{1,0:T(8,12...) custom-call(bf16[8,256,256]{2,1,0:T(8,128)(2,1)} %exch.3, f32[8,256]{1,0:T(8,128)} %energy.3, ...), custom_call_target="tpu_custom_call" | custom-call | flops 1000 | bytes 1000 | tf_op jit(solution)/shard_map/second/pallas_call | solution.py:241
  6.7 4.4 %collective-permute-start.1 = (bf16[2,256,256]{2,1,0:T(8,128)(2,1)S(1)}, bf16[2,256,256]{2,1,0:T(8,128)(2,1)S(1)}, u32[]{:S(2)}, u32[]{:S(2)}) collective-permute-start(bf16[2,256,256]{2,1,0:T(8,128)(2,1)S(1)} %get-tuple-element.28.ia), channel_id=1, source_target_pairs={{0,1},{1,0},{2,3},{3,2},{4,5},{5,4},{6,7},{7,6},{8,9},{9,8},{10,11... | collective-permute-start | bytes 786440 | tf_op jit(solution)/shard_map/ppermute | solution.py:252
  11.1 0.1 collective-permute-start.2
  11.2 1.1 %collective-permute-done.1.iha = bf16[2,256,256]{2,1,0:T(8,128)(2,1)S(1)} collective-permute-done((bf16[2,256,256]{2,1,0:T(8,128)(2,1)S(1)}, bf16[2,256,256]{2,1,0:T(8,128)(2,1)S(1)}, u32[]{:S(2)}, u32[]{:S(2)}) %collective-permute-start.1) | collective-permute-done | bytes 262176 | tf_op jit(solution)/shard_map/ppermute | solution.py:252
  12.2 0.4 collective-permute-done.2.ihb
  12.6 4.3 %near1.1 = (f32[8,256,256]{2,1,0:T(8,128)S(1)}, f32[8,256,256]{2,1,0:T(8,128)S(1)}, f32[8,256,256]{2,1,0:T(8,128)S(1)}) custom-call(s32[300]{0:T(512)S(4)} %get-tuple-element.23.lists, f32[296]{0:T(512)S(4)} %get-tuple-element.24.coefs, bf16[8,8,256,256]{3,2,1,0:T(8,128)(2,1)S(1)} %get-tuple-element.25.inter, ...), custom_call_target="tpu_custom_call" | custom-call | flops 1000 | bytes 1000 | tf_op jit(solution)/shard_map/near1/pallas_call | solution.py:257
  16.9 0.0 collective-permute-done.xh
  16.9 0.8 %across0.1 = (bf16[4,256,256]{2,1,0:T(8,128)(2,1)S(1)}, f32[8,256,256]{2,1,0:T(8,128)S(1)}, f32[8,256,256]{2,1,0:T(8,128)S(1)}) custom-call(s32[300]{0:T(512)S(4)} %get-tuple-element.23.lists, f32[296]{0:T(512)S(4)} %get-tuple-element.24.coefs, bf16[8,8,256,256]{3,2,1,0:T(8,128)(2,1)S(1)} %get-tuple-element.25.inter, ...), custom_call_target="tpu_custom_call", output_to_operand_aliasing={{1}: (5, {}), {2}: (6, {})} | custom-call | flops 1000 | bytes 1000 | tf_op jit(solution)/shard_map/across0/pallas_call | solution.py:265
  17.7 0.7 %collective-permute-start.3 = (bf16[4,256,256]{2,1,0:T(8,128)(2,1)S(1)}, bf16[4,256,256]{2,1,0:T(8,128)(2,1)S(1)}, u32[]{:S(2)}, u32[]{:S(2)}) collective-permute-start(bf16[4,256,256]{2,1,0:T(8,128)(2,1)S(1)} %get-tuple-element.33.x), channel_id=1, source_target_pairs={{1,2},{3,4},{5,6},{7,8},{9,10},{11,12},{13,14},{2,1},{4,3},{6,5},{... | collective-permute-start | bytes 1572872 | tf_op jit(solution)/shard_map/ppermute | solution.py:272
  18.4 1.4 %across1.1 = (bf16[2,256,256]{2,1,0:T(8,128)(2,1)S(1)}, bf16[2,256,256]{2,1,0:T(8,128)(2,1)S(1)}, f32[8,256,256]{2,1,0:T(8,128)S(1)}, f32[8,256,256]{2,1,0:T(8,128)S(1)}) custom-call(s32[300]{0:T(512)S(4)} %get-tuple-element.23.lists, f32[296]{0:T(512)S(4)} %get-tuple-element.24.coefs, ...), custom_call_target="tpu_custom_call", output_to_operand_aliasing={{2}: (5, {}), {3}: (6, {})} | custom-call | flops 1000 | bytes 1000 | tf_op jit(solution)/shard_map/across1/pallas_call | solution.py:265
  19.8 5.0 %collective-permute-start.4 = (bf16[2,256,256]{2,1,0:T(8,128)(2,1)S(1)}, bf16[2,256,256]{2,1,0:T(8,128)(2,1)S(1)}, u32[]{:S(2)}, u32[]{:S(2)}) collective-permute-start(bf16[2,256,256]{2,1,0:T(8,128)(2,1)S(1)} %get-tuple-element.37.ia), channel_id=1, source_target_pairs={{0,1},{1,0},{2,3},{3,2},{4,5},{5,4},{6,7},{7,6},{8,9},{9,8},{10,11... | collective-permute-start | bytes 786440 | tf_op jit(solution)/shard_map/ppermute | solution.py:252
  24.9 0.1 collective-permute-start.5
  24.9 1.1 %collective-permute-done.4.iha = bf16[2,256,256]{2,1,0:T(8,128)(2,1)S(1)} collective-permute-done((bf16[2,256,256]{2,1,0:T(8,128)(2,1)S(1)}, bf16[2,256,256]{2,1,0:T(8,128)(2,1)S(1)}, u32[]{:S(2)}, u32[]{:S(2)}) %collective-permute-start.4) | collective-permute-done | bytes 262176 | tf_op jit(solution)/shard_map/ppermute | solution.py:252
  26.0 0.4 collective-permute-done.5.ihb
  26.4 4.2 %near2.1 = (f32[8,256,256]{2,1,0:T(8,128)S(1)}, f32[8,128]{1,0:T(8,128)S(1)}) custom-call(s32[300]{0:T(512)S(4)} %get-tuple-element.23.lists, f32[296]{0:T(512)S(4)} %get-tuple-element.24.coefs, bf16[8,8,256,256]{3,2,1,0:T(8,128)(2,1)S(1)} %get-tuple-element.25.inter, ...), custom_call_target="tpu_custom_call", output_to_operand_aliasing={{0}: (11, {})} | custom-call | flops 1000 | bytes 1000 | tf_op jit(solution)/shard_map/near2/pallas_call | solution.py:274
  30.7 0.0 collective-permute-done.3.xh
  30.7 3.2 %last.1 = (f32[8,256,256]{2,1,0:T(8,128)}, f32[16,128]{1,0:T(8,128)S(1)}, f32[8,256,256]{2,1,0:T(8,128)S(1)}) custom-call(s32[300]{0:T(512)S(4)} %get-tuple-element.23.lists, f32[296]{0:T(512)S(4)} %get-tuple-element.24.coefs, bf16[8,8,256,256]{3,2,1,0:T(8,128)(2,1)S(1)} %get-tuple-element.25.inter, ...), custom_call_target="tpu_custom_call", output_to_operand_aliasing={{2}: (7, {})} | custom-call | flops 1000 | bytes 1000 | tf_op jit(solution)/shard_map/last/pallas_call | solution.py:279
  33.9 16.4 %all_to_all.12 = f32[16,1,128]{2,1,0:T(1,128)S(1)} all-to-all(f32[16,1,128]{2,1,0:T(1,128)S(1)} %bitcast.4), channel_id=1, replica_groups=mesh['grp'=2,'row'=16] {'row'}, dimensions={0} | all-to-all | bytes 16384 | tf_op jit(solution)/shard_map/all_to_all | solution.py:285
  50.3 0.5 %multiply_sqrt_fusion = f32[2]{0:T(128)} fusion(f32[2]{0:T(128)S(1)} %slice_reduce_fusion), kind=kLoop, calls=%fused_computation.1 | loop fusion | flops 2 | bytes 16 | tf_op jit(solution)/shard_map/sqrt | solution.py:286
  (1 shorter events, 0.0 us)
Async XLA Ops:
  2.1 14.8 %collective-permute-start = (bf16[4,256,256]{2,1,0:T(8,128)(2,1)S(1)}, bf16[4,256,256]{2,1,0:T(8,128)(2,1)S(1)}, u32[]{:S(2)}, u32[]{:S(2)}) collective-permute-start(bf16[4,256,256]{2,1,0:T(8,128)(2,1)S(1)} %first.1.x), channel_id=1, source_target_pairs={{1,2},{3,4},{5,6},{7,8},{9,10},{11,12},{13,14},{2,1},{4,3},{6,5},{... | collective-permute-start | bytes 1572872 | tf_op jit(solution)/shard_map/ppermute | solution.py:239
  6.7 5.5 %collective-permute-start.1 = (bf16[2,256,256]{2,1,0:T(8,128)(2,1)S(1)}, bf16[2,256,256]{2,1,0:T(8,128)(2,1)S(1)}, u32[]{:S(2)}, u32[]{:S(2)}) collective-permute-start(bf16[2,256,256]{2,1,0:T(8,128)(2,1)S(1)} %get-tuple-element.28.ia), channel_id=1, source_target_pairs={{0,1},{1,0},{2,3},{3,2},{4,5},{5,4},{6,7},{7,6},{8,9},{9,8},{10,11... | collective-permute-start | bytes 786440 | tf_op jit(solution)/shard_map/ppermute | solution.py:252
  11.1 1.5 %collective-permute-start.2 = (bf16[2,256,256]{2,1,0:T(8,128)(2,1)S(1)}, bf16[2,256,256]{2,1,0:T(8,128)(2,1)S(1)}, u32[]{:S(2)}, u32[]{:S(2)}) collective-permute-start(bf16[2,256,256]{2,1,0:T(8,128)(2,1)S(1)} %get-tuple-element.29.ib), channel_id=1, source_target_pairs={{0,1},{1,0},{2,3},{3,2},{4,5},{5,4},{6,7},{7,6},{8,9},{9,8},{10,11... | collective-permute-start | bytes 786440 | tf_op jit(solution)/shard_map/ppermute | solution.py:252
  17.7 13.0 %collective-permute-start.3 = (bf16[4,256,256]{2,1,0:T(8,128)(2,1)S(1)}, bf16[4,256,256]{2,1,0:T(8,128)(2,1)S(1)}, u32[]{:S(2)}, u32[]{:S(2)}) collective-permute-start(bf16[4,256,256]{2,1,0:T(8,128)(2,1)S(1)} %get-tuple-element.33.x), channel_id=1, source_target_pairs={{1,2},{3,4},{5,6},{7,8},{9,10},{11,12},{13,14},{2,1},{4,3},{6,5},{... | collective-permute-start | bytes 1572872 | tf_op jit(solution)/shard_map/ppermute | solution.py:272
  19.8 6.2 %collective-permute-start.4 = (bf16[2,256,256]{2,1,0:T(8,128)(2,1)S(1)}, bf16[2,256,256]{2,1,0:T(8,128)(2,1)S(1)}, u32[]{:S(2)}, u32[]{:S(2)}) collective-permute-start(bf16[2,256,256]{2,1,0:T(8,128)(2,1)S(1)} %get-tuple-element.37.ia), channel_id=1, source_target_pairs={{0,1},{1,0},{2,3},{3,2},{4,5},{5,4},{6,7},{7,6},{8,9},{9,8},{10,11... | collective-permute-start | bytes 786440 | tf_op jit(solution)/shard_map/ppermute | solution.py:252
  24.9 1.5 %collective-permute-start.5 = (bf16[2,256,256]{2,1,0:T(8,128)(2,1)S(1)}, bf16[2,256,256]{2,1,0:T(8,128)(2,1)S(1)}, u32[]{:S(2)}, u32[]{:S(2)}) collective-permute-start(bf16[2,256,256]{2,1,0:T(8,128)(2,1)S(1)} %get-tuple-element.38.ib), channel_id=1, source_target_pairs={{0,1},{1,0},{2,3},{3,2},{4,5},{5,4},{6,7},{7,6},{8,9},{9,8},{10,11... | collective-permute-start | bytes 786440 | tf_op jit(solution)/shard_map/ppermute | solution.py:252

commit v3 on v2

--- a/solution.py
+++ b/solution.py
@@ -13,7 +13,7 @@
 SM = pl.BlockSpec(memory_space=pltpu.SMEM)
 AN = pl.BlockSpec(memory_space=pl.ANY)
 CAP = 72
-NEAR, ACROSS = 8, 4
+LONG, SHORT = 16, 8
 COUNTS, LIVE = 4 * CAP, 4 * CAP + 4
 GAP = 4 * CAP
 MIB = 1 << 20
@@ -57,29 +57,32 @@
     return copies
 
 
-def first_kernel(exch, energy, gap, live, out, buf, en, gp, lv, sem, sems):
+def first_kernel(exch, energy, gap, live, inter_hbm, out, inter, buf, en, gp, lv, sem, sems, slab_sem):
     slots = slots_of(0, 4)
     small = start_all([(energy, en), (gap, gp), (live, lv)], sems)
     tiles = start_all([(exch.at[p], buf.at[i]) for i, p in enumerate(slots)], sem)
+    slabs = start_all([(inter_hbm.at[p], inter.at[p]) for p in slots[:1]], slab_sem)
     for c in small:
         c.wait()
     dens = denominators(en, [gp[p] for p in slots], slots)
     for i, p in enumerate(slots):
         tiles[i].wait()
         out[i] = (-lv[p].astype(F32) * buf[i].astype(F32) / dens[i]).astype(BF16)
+    for c in slabs:
+        c.wait()
 
 
 def second_kernel(
-    exch, energy, gap, live, fock, nslot, nlive, inter_hbm, x, out_a, out_b, ex, en, lists, coefs, inter,
+    exch, energy, gap, live, fock, nslot, nlive, inter_hbm, x, inter_in, out_a, out_b, ex, en, lists, coefs, inter,
     gp, lv, fk, ns, nl, table, ends, sem, sems, slab_sem,
 ):
-    del x
+    del x, inter_in
     slots = slots_of(4, 8)
     base = base_slot()
     small = start_all([(energy, en), (gap, gp), (live, lv), (fock, fk), (nslot, ns), (nlive, nl)], sems)
     order = slots + slots_of(0, 4)
     tiles = start_all([(exch.at[p], ex.at[p]) for p in order], sem)
-    slabs = start_all([(inter_hbm.at[p], inter.at[p]) for p in range(8)], slab_sem)
+    slabs = start_all([(inter_hbm.at[p], inter.at[p]) for p in order[5:]], slab_sem)
     for c in small:
         c.wait()
     dens = denominators(en, [gp[p] for p in slots], slots)
@@ -114,8 +117,8 @@
     for k in range(4):
         e = ends[k]
         lists[COUNTS + k] = e - k * CAP
-        for u in range(NEAR if k < 2 else ACROSS):
-            lists[e + u] = 0
+        for u in range(LONG):
+            lists[e + u] = base << 3
             coefs[e + u] = 0.0
     for p in range(8):
         lists[LIVE + p] = lv[p]
@@ -124,25 +127,26 @@
         c.wait()
 
 
-def run_list(which, lists, coefs, inter, src, acc):
-    unroll = NEAR if which < 2 else ACROSS
+def run_list(which, lists, coefs, inter, src, acc, steps=(LONG, SHORT)):
     off = which * CAP
-    chunks = (lists[COUNTS + which] + (unroll - 1)) // unroll
-
-    def chunk(i, _):
-        halves = []
-        for u in range(unroll):
-            code = lists[off + i * unroll + u]
+    count = lists[COUNTS + which]
+
+    def chunk(at, size):
+        for u in range(size):
+            code = lists[at + u]
             n, p, q, s = code & 7, (code >> 3) & 7, (code >> 6) & 7, code >> 9
             x = inter[p, n]
             h = jnp.dot(x, src[s], preferred_element_type=F32).astype(BF16)
-            halves.append((coefs[off + i * unroll + u], q, x, h))
-        for c, q, x, h in halves:
             t = lax.dot_general(h, x, (((1,), (1,)), ((), ())), preferred_element_type=F32)
-            acc[q] = acc[q] - c * t
-        return 0
-
-    lax.fori_loop(0, chunks, chunk, 0)
+            acc[q] = acc[q] - coefs[at + u] * t
+
+    if len(steps) > 1:
+        longs = (count + steps[0] - steps[1] - 1) // steps[0]
+        lax.fori_loop(0, longs, lambda i, _: chunk(off + i * steps[0], steps[0]) or 0, 0)
+        off = off + longs * steps[0]
+        count = count - longs * steps[0]
+    shorts = jnp.maximum(count + steps[-1] - 1, 0) // steps[-1]
+    lax.fori_loop(0, shorts, lambda i, _: chunk(off + i * steps[-1], steps[-1]) or 0, 0)
 
 
 def gather(src, x, ia, ib, iha, ihb):
@@ -153,31 +157,50 @@
     src[10:12] = ihb[...]
 
 
-def near_kernel_1(lists, coefs, inter, exch, energy, x, ia, ib, iha, ihb, acc, amps, recip, src):
-    slots = slots_of(0, 8)
+def start_half(half, lists, coefs, exch, energy, acc, amps, recip):
+    slots = slots_of(4 * half, 4 * half + 4)
     dens = denominators(energy, [coefs[GAP + p] for p in slots], slots)
-    gather(src, x, ia, ib, iha, ihb)
-    for q, p in enumerate(slots):
+    for j, p in enumerate(slots):
+        q = 4 * half + j
         ex = exch[p].astype(F32)
-        a0 = -lists[LIVE + p].astype(F32) * ex / dens[q]
+        a0 = -lists[LIVE + p].astype(F32) * ex / dens[j]
         amps[q] = a0
-        recip[q] = 1.0 / dens[q]
-        acc[q] = ex + dens[q] * a0
-    for half in range(2):
-        run_list(half, lists, coefs, inter, src, acc)
-
-
-def across_kernel(half, lists, coefs, inter, xh, recip, acc_in, amps_in, *outs):
-    del acc_in, amps_in
-    *out, acc, amps = outs
-    run_list(2 + half, lists, coefs, inter, xh, acc)
+        recip[q] = 1.0 / dens[j]
+        acc[q] = ex + dens[j] * a0
+
+
+def update_half(half, lists, acc, amps, recip, out):
+    each = 4 // len(out)
     for j, p in enumerate(slots_of(4 * half, 4 * half + 4)):
         q = 4 * half + j
         res = lists[LIVE + p].astype(F32) * acc[q]
         a1 = amps[q] - res * recip[q]
         amps[q] = a1
-        each = 4 // len(out)
         out[j // each][j % each] = a1.astype(BF16)
+
+
+def near_kernel_1(lists, coefs, inter_hbm, exch, energy, x, ia, ib, iha, ihb, inter_in, acc, amps, recip, src, inter, sem):
+    del inter_in
+    slabs = start_all([(inter_hbm.at[p], inter.at[p]) for p in slots_of(4, 8)], sem)
+    gather(src, x, ia, ib, iha, ihb)
+    start_half(0, lists, coefs, exch, energy, acc, amps, recip)
+    run_list(0, lists, coefs, inter, src, acc)
+    for c in slabs:
+        c.wait()
+
+
+def across_kernel(lists, coefs, inter, xh, recip, acc_in, amps_in, out, acc, amps):
+    del acc_in, amps_in
+    run_list(2, lists, coefs, inter, xh, acc, (SHORT,))
+    update_half(0, lists, acc, amps, recip, [out])
+
+
+def rest_kernel(lists, coefs, inter, exch, energy, src, xh, acc_in, amps_in, recip_in, out_a, out_b, acc, amps, recip):
+    del acc_in, amps_in, recip_in
+    start_half(1, lists, coefs, exch, energy, acc, amps, recip)
+    run_list(1, lists, coefs, inter, src, acc)
+    run_list(3, lists, coefs, inter, xh, acc, (SHORT,))
+    update_half(1, lists, acc, amps, recip, [out_a, out_b])
 
 
 def squares(res):
@@ -205,7 +228,7 @@
     copies = []
     slots = slots_of(0, 8)
     for half in range(2):
-        run_list(2 + half, lists, coefs, inter, xh, acc)
+        run_list(2 + half, lists, coefs, inter, xh, acc, (SHORT,))
         for q in range(4 * half, 4 * half + 4):
             p = slots[q]
             res = lists[LIVE + p].astype(F32) * acc[q]
@@ -231,49 +254,51 @@
     other_chip += [(j, i) for i, j in other_chip]
     big = [hbm(a) for a in (amp_exch, pno_energy, pair_gap, pair_live, fock, nbr_slot, nbr_live)]
 
-    x0 = pl.pallas_call(
-        first_kernel, out_shape=tiles4, in_specs=[AN] * 4, out_specs=VM,
-        scratch_shapes=[pltpu.VMEM((4, v, v), BF16), pltpu.VMEM((8, v), F32)] + per_pair + [dma((4,)), dma((3,))],
+    tiles2 = pltpu.VMEM((2, v, v), BF16)
+    slabs = pltpu.VMEM(intersection.shape, BF16)
+    intersection = hbm(intersection)
+    x0, inter = pl.pallas_call(
+        first_kernel, out_shape=[tiles4, slabs], in_specs=[AN] * 5, out_specs=[VM] * 2,
+        scratch_shapes=[pltpu.VMEM((4, v, v), BF16), pltpu.VMEM((8, v), F32)] + per_pair + [dma((4,)), dma((3,)), dma((1,))],
         compiler_params=params(8), cost_estimate=COST, name="first",
-    )(*big[:4])
+    )(*big[:4], intersection)
     xh = lax.ppermute(x0, "row", other_chip)
-    tiles2 = pltpu.VMEM((2, v, v), BF16)
     i0a, i0b, exch, energy, lists, coefs, inter = pl.pallas_call(
         second_kernel,
         out_shape=[tiles2, tiles2, pltpu.VMEM((8, v, v), BF16), pltpu.VMEM((8, v), F32),
-                   pltpu.SMEM((LIVE + 8,), jnp.int32), pltpu.SMEM((GAP + 8,), F32), pltpu.VMEM(intersection.shape, BF16)],
-        in_specs=[AN] * 9, out_specs=[VM] * 4 + [SM] * 2 + [VM],
+                   pltpu.SMEM((LIVE + 8,), jnp.int32), pltpu.SMEM((GAP + 8,), F32), slabs],
+        in_specs=[AN] * 9 + [VM], out_specs=[VM] * 4 + [SM] * 2 + [VM], input_output_aliases={9: 6},
         scratch_shapes=per_pair + [pltpu.SMEM((8, 8), F32)] + [pltpu.SMEM((8, 8), jnp.int32)] * 2
-        + [pltpu.SMEM((24,), jnp.int32), pltpu.SMEM((4,), jnp.int32), dma((8,)), dma((6,)), dma((8,))],
+        + [pltpu.SMEM((24,), jnp.int32), pltpu.SMEM((4,), jnp.int32), dma((8,)), dma((6,)), dma((3,))],
         compiler_params=params(8), cost_estimate=COST, name="second",
-    )(*big, hbm(intersection), x0)
+    )(*big, intersection, x0, vmem(inter))
 
     def swap(*halves):
         return [vmem(lax.ppermute(h, "row", same_chip)) for h in halves]
 
     meta = (lists, coefs)
-    exch, energy, inter = vmem(exch), vmem(energy), vmem(inter)
-    gathered = [pltpu.VMEM((12, v, v), BF16)]
-    acc, amps, recip = pl.pallas_call(
-        near_kernel_1, out_shape=[tiles8] * 3, in_specs=[SM] * 2 + [VM] * 8, out_specs=[VM] * 3, scratch_shapes=gathered,
+    exch, energy = vmem(exch), vmem(energy)
+    gathered = pltpu.VMEM((12, v, v), BF16)
+    acc, amps, recip, src, inter = pl.pallas_call(
+        near_kernel_1, out_shape=[tiles8] * 3 + [gathered, slabs], in_specs=[SM] * 2 + [AN] + [VM] * 8, out_specs=[VM] * 5,
+        scratch_shapes=[dma((4,))], input_output_aliases={10: 4},
         compiler_params=params(8), cost_estimate=COST, name="near1",
-    )(*meta, inter, exch, energy, vmem(x0), vmem(i0a), vmem(i0b), *swap(i0a, i0b))
-
-    def across(half, halo, acc, amps):
-        shapes = [tiles2, tiles2] if half else [tiles4]
-        k = len(shapes)
-        return pl.pallas_call(
-            functools.partial(across_kernel, half), out_shape=shapes + [tiles8, tiles8],
-            in_specs=[SM] * 2 + [VM] * 5, out_specs=[VM] * (k + 2), input_output_aliases={5: k, 6: k + 1},
-            compiler_params=params(8), cost_estimate=COST, name=f"across{half}",
-        )(*meta, inter, vmem(halo), vmem(recip), vmem(acc), vmem(amps))
-
-    x1, acc, amps = across(0, xh, acc, amps)
+    )(*meta, intersection, exch, energy, vmem(x0), vmem(i0a), vmem(i0b), *swap(i0a, i0b), vmem(inter))
+    inter = vmem(inter)
+    x1, acc, amps = pl.pallas_call(
+        across_kernel, out_shape=[tiles4, tiles8, tiles8],
+        in_specs=[SM] * 2 + [VM] * 5, out_specs=[VM] * 3, input_output_aliases={5: 1, 6: 2},
+        compiler_params=params(8), cost_estimate=COST, name="across",
+    )(*meta, inter, vmem(xh), vmem(recip), vmem(acc), vmem(amps))
     xh1 = lax.ppermute(x1, "row", other_chip)
-    i1a, i1b, acc, amps = across(1, xh, acc, amps)
+    i1a, i1b, acc, amps, recip = pl.pallas_call(
+        rest_kernel, out_shape=[tiles2, tiles2] + [tiles8] * 3,
+        in_specs=[SM] * 2 + [VM] * 8, out_specs=[VM] * 5, input_output_aliases={7: 2, 8: 3, 9: 4},
+        compiler_params=params(8), cost_estimate=COST, name="rest",
+    )(*meta, inter, exch, energy, vmem(src), vmem(xh), vmem(acc), vmem(amps), vmem(recip))
     acc, sq = pl.pallas_call(
         near_kernel_2, out_shape=[tiles8, pltpu.VMEM((8, 128), F32)], in_specs=[SM] * 2 + [VM] * 10, out_specs=[VM] * 2,
-        scratch_shapes=gathered, input_output_aliases={11: 0},
+        scratch_shapes=[gathered], input_output_aliases={11: 0},
         compiler_params=params(8), cost_estimate=COST, name="near2",
     )(*meta, inter, exch, energy, vmem(x1), vmem(i1a), vmem(i1b), *swap(i1a, i1b), vmem(amps), vmem(acc))
     out, sums, _ = pl.pallas_call(

time: 51.3 us -> 48.4 us (0.943)
  blocking collectives: 16.4 us -> 11.3 us
  starting transfers between devices: 10.9 us -> 13.6 us
    all_to_all x1, blocking collectives: 16.4 us -> 11.3 us  [on_device(): sums = lax.all_to_all(sums, 'row', 0, 0, tiled=True)]
    ppermute x4, starting transfers between devices: 9.56 us -> 12.2 us  [swap(): return [vmem(lax.ppermute(h, 'row', same_chip)) for h in halves]]
    pallas_call x1, Pallas kernels: 3.93 us -> 2.66 us  [on_device(): pl.pallas_call(second_kernel, out_shape=[tiles2, tiles2, pltpu.VMEM((8, v...]
    pallas_call x4, Pallas kernels: 7.93 us -> 8.47 us  [the longest x1 2.95 us: on_device(): pl.pallas_call(rest_kernel, out_shape=[tiles2, tiles2] + [tiles8] * 3, in...]
  transfers between devices with their start and end apart: 6 -> 6, of which waited for: 4 -> 4; matrix products, arithmetic and copies ran while one was open for 0% -> 0% of each run, Pallas kernels for 27% -> 28%
where the time goes in v3:
time: 48.4 us; the launch traced here: 48 us
  Pallas kernels  18.9 us (39%)
  starting transfers between devices  13.6 us (28%)
  blocking collectives  11.3 us (23%)
  waiting for transfers between devices  2.92 us (6%)
  between operations  0.72 us (1%)
  other arithmetic  0.54 us (1%)
    ppermute x4, starting transfers between devices, swap(): return [vmem(lax.ppermute(h, 'row', same_chip)) for h in halves]  12.2 us
    all_to_all x1, blocking collectives, on_device(): sums = lax.all_to_all(sums, 'row', 0, 0, tiled=True)  11.3 us
    pallas_call x1, Pallas kernels, on_device(): pl.pallas_call(near_kernel_2, out_shape=[tiles8, pltpu.VMEM((8, 128), F32...  4.73 us
    pallas_call x1, Pallas kernels, on_device(): pl.pallas_call(last_kernel, out_shape=[jax.ShapeDtypeStruct((8, v, v), F3...  3.08 us
    pallas_call x1, Pallas kernels, on_device(): pl.pallas_call(rest_kernel, out_shape=[tiles2, tiles2] + [tiles8] * 3, in...  2.95 us
    ppermute x4, waiting for transfers between devices, swap(): return [vmem(lax.ppermute(h, 'row', same_chip)) for h in halves]  2.91 us
    pallas_call x1, Pallas kernels, on_device(): pl.pallas_call(near_kernel_1, out_shape=[tiles8] * 3 + [gathered, slabs],...  2.89 us
    pallas_call x1, Pallas kernels, on_device(): pl.pallas_call(second_kernel, out_shape=[tiles2, tiles2, pltpu.VMEM((8, v...  2.66 us
  transfers between devices with their start and end apart: 6, of which 4 were waited for; matrix products, arithmetic and copies ran while one was open for 0% of the time, Pallas kernels for 28%

profile of v3, /device:TPU:0, one launch (start us, length us, event | category | flops | bytes accessed | tf_op | source)
XLA Modules:
  0.0 48.0 jit_solution(10230926101175123474)
XLA Ops:
  0.6 1.6 %first.1 = (bf16[4,256,256]{2,1,0:T(8,128)(2,1)S(1)}, bf16[8,8,256,256]{3,2,1,0:T(8,128)(2,1)S(1)}) custom-call(bf16[8,256,256]{2,1,0:T(8,128)(2,1)} %exch.3, f32[8,256]{1,0:T(8,128)} %energy.3, f32[8]{0:T(128)} %gap.3, s32[8]{0:T(128)} %live.3, bf16[8,8,256,256]{3,2,1,0:T(8,128)(2,1)} %inter_hbm.5), custom_call_target="tpu_custom_call" | custom-call | flops 1000 | bytes 1000 | tf_op jit(solution)/shard_map/first/pallas_call | solution.py:260
  2.2 0.7 %collective-permute-start.2 = (bf16[4,256,256]{2,1,0:T(8,128)(2,1)S(1)}, bf16[4,256,256]{2,1,0:T(8,128)(2,1)S(1)}, u32[]{:S(2)}, u32[]{:S(2)}) collective-permute-start(bf16[4,256,256]{2,1,0:T(8,128)(2,1)S(1)} %get-tuple-element.28.x), channel_id=1, source_target_pairs={{1,2},{3,4},{5,6},{7,8},{9,10},{11,12},{13,14},{2,1},{4,3},{6,5},{... | collective-permute-start | bytes 1572872 | tf_op jit(solution)/shard_map/ppermute | solution.py:265
  2.9 2.7 %second.1 = (bf16[2,256,256]{2,1,0:T(8,128)(2,1)S(1)}, bf16[2,256,256]{2,1,0:T(8,128)(2,1)S(1)}, bf16[8,256,256]{2,1,0:T(8,128)(2,1)S(1)}, f32[8,256]{1,0:T(8,12...) custom-call(bf16[8,256,256]{2,1,0:T(8,128)(2,1)} %exch.3, ...), custom_call_target="tpu_custom_call", output_to_operand_aliasing={{6}: (9, {})} | custom-call | flops 1000 | bytes 1000 | tf_op jit(solution)/shard_map/second/pallas_call | solution.py:266
  5.6 4.4 %collective-permute-start = (bf16[2,256,256]{2,1,0:T(8,128)(2,1)S(1)}, bf16[2,256,256]{2,1,0:T(8,128)(2,1)S(1)}, u32[]{:S(2)}, u32[]{:S(2)}) collective-permute-start(bf16[2,256,256]{2,1,0:T(8,128)(2,1)S(1)} %get-tuple-element.34.ia), channel_id=1, source_target_pairs={{0,1},{1,0},{2,3},{3,2},{4,5},{5,4},{6,7},{7,6},{8,9},{9,8},{10,11... | collective-permute-start | bytes 786440 | tf_op jit(solution)/shard_map/ppermute | solution.py:277
  10.0 0.1 collective-permute-start.1
  10.0 1.1 %collective-permute-done.iha = bf16[2,256,256]{2,1,0:T(8,128)(2,1)S(1)} collective-permute-done((bf16[2,256,256]{2,1,0:T(8,128)(2,1)S(1)}, bf16[2,256,256]{2,1,0:T(8,128)(2,1)S(1)}, u32[]{:S(2)}, u32[]{:S(2)}) %collective-permute-start) | collective-permute-done | bytes 262176 | tf_op jit(solution)/shard_map/ppermute | solution.py:277
  11.1 0.4 collective-permute-done.1.ihb
  11.5 2.9 %near1.1 = (f32[8,256,256]{2,1,0:T(8,128)S(1)}, f32[8,256,256]{2,1,0:T(8,128)S(1)}, f32[8,256,256]{2,1,0:T(8,128)S(1)}, bf16[12,256,256]{2,1,0:T(8,128)(2,1)S(1)}, bf16[8,8,256,256]{3,2,1,0:T(8,128)(2,1)S(1)}) custom-call(s32[300]{0:T(512)S(4)} %get-tuple-element.30.lists, f32[296]{0:T(512)S(4)} %get-tuple-element.31.coefs, ...), custom_call_target="tpu_custom_call", output_to_operand_aliasing={{4}: (10, {})} | custom-call | flops 1000 | bytes 1000 | tf_op jit(solution)/shard_map/near1/pallas_call | solution.py:282
  14.4 0.0 collective-permute-done.2.xh
  14.4 1.0 %across.1 = (bf16[4,256,256]{2,1,0:T(8,128)(2,1)S(1)}, f32[8,256,256]{2,1,0:T(8,128)S(1)}, f32[8,256,256]{2,1,0:T(8,128)S(1)}) custom-call(s32[300]{0:T(512)S(4)} %get-tuple-element.30.lists, f32[296]{0:T(512)S(4)} %get-tuple-element.31.coefs, bf16[8,8,256,256]{3,2,1,0:T(8,128)(2,1)S(1)} %get-tuple-element.37.inter, ...), custom_call_target="tpu_custom_call", output_to_operand_aliasing={{1}: (5, {}), {2}: (6, {})} | custom-call | flops 1000 | bytes 1000 | tf_op jit(solution)/shard_map/across/pallas_call | solution.py:288
  15.4 0.7 %collective-permute-start.3 = (bf16[4,256,256]{2,1,0:T(8,128)(2,1)S(1)}, bf16[4,256,256]{2,1,0:T(8,128)(2,1)S(1)}, u32[]{:S(2)}, u32[]{:S(2)}) collective-permute-start(bf16[4,256,256]{2,1,0:T(8,128)(2,1)S(1)} %get-tuple-element.41.x), channel_id=1, source_target_pairs={{1,2},{3,4},{5,6},{7,8},{9,10},{11,12},{13,14},{2,1},{4,3},{6,5},{... | collective-permute-start | bytes 1572872 | tf_op jit(solution)/shard_map/ppermute | solution.py:293
  16.2 2.9 %rest.1 = (bf16[2,256,256]{2,1,0:T(8,128)(2,1)S(1)}, bf16[2,256,256]{2,1,0:T(8,128)(2,1)S(1)}, f32[8,256,256]{2,1,0:T(8,128)S(1)}, f32[8,256,256]{2,1,0:T(8,128)S(1)}, f32[8,256,256]{2,1,0:T(8,128)S(1)}) custom-call(s32[300]{0:T(512)S(4)} %get-tuple-element.30.lists, ...), custom_call_target="tpu_custom_call", output_to_operand_aliasing={{2}: (7, {}), {3}: (8, {}), {4}: (9, {})} | custom-call | flops 1000 | bytes 1000 | tf_op jit(solution)/shard_map/rest/pallas_call | solution.py:294
  19.1 7.7 %collective-permute-start.4 = (bf16[2,256,256]{2,1,0:T(8,128)(2,1)S(1)}, bf16[2,256,256]{2,1,0:T(8,128)(2,1)S(1)}, u32[]{:S(2)}, u32[]{:S(2)}) collective-permute-start(bf16[2,256,256]{2,1,0:T(8,128)(2,1)S(1)} %get-tuple-element.47.ia), channel_id=1, source_target_pairs={{0,1},{1,0},{2,3},{3,2},{4,5},{5,4},{6,7},{7,6},{8,9},{9,8},{10,11... | collective-permute-start | bytes 786440 | tf_op jit(solution)/shard_map/ppermute | solution.py:277
  26.8 0.1 collective-permute-start.5
  26.9 1.1 %collective-permute-done.4.iha = bf16[2,256,256]{2,1,0:T(8,128)(2,1)S(1)} collective-permute-done((bf16[2,256,256]{2,1,0:T(8,128)(2,1)S(1)}, bf16[2,256,256]{2,1,0:T(8,128)(2,1)S(1)}, u32[]{:S(2)}, u32[]{:S(2)}) %collective-permute-start.4) | collective-permute-done | bytes 262176 | tf_op jit(solution)/shard_map/ppermute | solution.py:277
  28.0 0.4 collective-permute-done.5.ihb
  28.3 4.7 %near2.1 = (f32[8,256,256]{2,1,0:T(8,128)S(1)}, f32[8,128]{1,0:T(8,128)S(1)}) custom-call(s32[300]{0:T(512)S(4)} %get-tuple-element.30.lists, f32[296]{0:T(512)S(4)} %get-tuple-element.31.coefs, bf16[8,8,256,256]{3,2,1,0:T(8,128)(2,1)S(1)} %get-tuple-element.37.inter, ...), custom_call_target="tpu_custom_call", output_to_operand_aliasing={{0}: (11, {})} | custom-call | flops 1000 | bytes 1000 | tf_op jit(solution)/shard_map/near2/pallas_call | solution.py:299
  33.1 0.0 collective-permute-done.3.xh
  33.1 3.1 %last.1 = (f32[8,256,256]{2,1,0:T(8,128)}, f32[16,128]{1,0:T(8,128)S(1)}, f32[8,256,256]{2,1,0:T(8,128)S(1)}) custom-call(s32[300]{0:T(512)S(4)} %get-tuple-element.30.lists, f32[296]{0:T(512)S(4)} %get-tuple-element.31.coefs, bf16[8,8,256,256]{3,2,1,0:T(8,128)(2,1)S(1)} %get-tuple-element.37.inter, ...), custom_call_target="tpu_custom_call", output_to_operand_aliasing={{2}: (7, {})} | custom-call | flops 1000 | bytes 1000 | tf_op jit(solution)/shard_map/last/pallas_call | solution.py:304
  36.2 11.3 %all_to_all.12 = f32[16,1,128]{2,1,0:T(1,128)S(1)} all-to-all(f32[16,1,128]{2,1,0:T(1,128)S(1)} %bitcast.4), channel_id=1, replica_groups=mesh['grp'=2,'row'=16] {'row'}, dimensions={0} | all-to-all | bytes 16384 | tf_op jit(solution)/shard_map/all_to_all | solution.py:310
  47.5 0.5 %multiply_sqrt_fusion = f32[2]{0:T(128)} fusion(f32[2]{0:T(128)S(1)} %slice_reduce_fusion), kind=kLoop, calls=%fused_computation.1 | loop fusion | flops 2 | bytes 16 | tf_op jit(solution)/shard_map/sqrt | solution.py:311
  (1 shorter events, 0.0 us)
Async XLA Ops:
  2.2 12.2 %collective-permute-start.2 = (bf16[4,256,256]{2,1,0:T(8,128)(2,1)S(1)}, bf16[4,256,256]{2,1,0:T(8,128)(2,1)S(1)}, u32[]{:S(2)}, u32[]{:S(2)}) collective-permute-start(bf16[4,256,256]{2,1,0:T(8,128)(2,1)S(1)} %get-tuple-element.28.x), channel_id=1, source_target_pairs={{1,2},{3,4},{5,6},{7,8},{9,10},{11,12},{13,14},{2,1},{4,3},{6,5},{... | collective-permute-start | bytes 1572872 | tf_op jit(solution)/shard_map/ppermute | solution.py:265
  5.6 5.5 %collective-permute-start = (bf16[2,256,256]{2,1,0:T(8,128)(2,1)S(1)}, bf16[2,256,256]{2,1,0:T(8,128)(2,1)S(1)}, u32[]{:S(2)}, u32[]{:S(2)}) collective-permute-start(bf16[2,256,256]{2,1,0:T(8,128)(2,1)S(1)} %get-tuple-element.34.ia), channel_id=1, source_target_pairs={{0,1},{1,0},{2,3},{3,2},{4,5},{5,4},{6,7},{7,6},{8,9},{9,8},{10,11... | collective-permute-start | bytes 786440 | tf_op jit(solution)/shard_map/ppermute | solution.py:277
  10.0 1.5 %collective-permute-start.1 = (bf16[2,256,256]{2,1,0:T(8,128)(2,1)S(1)}, bf16[2,256,256]{2,1,0:T(8,128)(2,1)S(1)}, u32[]{:S(2)}, u32[]{:S(2)}) collective-permute-start(bf16[2,256,256]{2,1,0:T(8,128)(2,1)S(1)} %get-tuple-element.35.ib), channel_id=1, source_target_pairs={{0,1},{1,0},{2,3},{3,2},{4,5},{5,4},{6,7},{7,6},{8,9},{9,8},{10,11... | collective-permute-start | bytes 786440 | tf_op jit(solution)/shard_map/ppermute | solution.py:277
  15.4 17.6 %collective-permute-start.3 = (bf16[4,256,256]{2,1,0:T(8,128)(2,1)S(1)}, bf16[4,256,256]{2,1,0:T(8,128)(2,1)S(1)}, u32[]{:S(2)}, u32[]{:S(2)}) collective-permute-start(bf16[4,256,256]{2,1,0:T(8,128)(2,1)S(1)} %get-tuple-element.41.x), channel_id=1, source_target_pairs={{1,2},{3,4},{5,6},{7,8},{9,10},{11,12},{13,14},{2,1},{4,3},{6,5},{... | collective-permute-start | bytes 1572872 | tf_op jit(solution)/shard_map/ppermute | solution.py:293
  19.1 8.8 %collective-permute-start.4 = (bf16[2,256,256]{2,1,0:T(8,128)(2,1)S(1)}, bf16[2,256,256]{2,1,0:T(8,128)(2,1)S(1)}, u32[]{:S(2)}, u32[]{:S(2)}) collective-permute-start(bf16[2,256,256]{2,1,0:T(8,128)(2,1)S(1)} %get-tuple-element.47.ia), channel_id=1, source_target_pairs={{0,1},{1,0},{2,3},{3,2},{4,5},{5,4},{6,7},{7,6},{8,9},{9,8},{10,11... | collective-permute-start | bytes 786440 | tf_op jit(solution)/shard_map/ppermute | solution.py:277
  26.8 1.5 %collective-permute-start.5 = (bf16[2,256,256]{2,1,0:T(8,128)(2,1)S(1)}, bf16[2,256,256]{2,1,0:T(8,128)(2,1)S(1)}, u32[]{:S(2)}, u32[]{:S(2)}) collective-permute-start(bf16[2,256,256]{2,1,0:T(8,128)(2,1)S(1)} %get-tuple-element.48.ib), channel_id=1, source_target_pairs={{0,1},{1,0},{2,3},{3,2},{4,5},{5,4},{6,7},{7,6},{8,9},{9,8},{10,11... | collective-permute-start | bytes 786440 | tf_op jit(solution)/shard_map/ppermute | solution.py:277

commit v4 on v3

--- a/solution.py
+++ b/solution.py
@@ -57,32 +57,29 @@
     return copies
 
 
-def first_kernel(exch, energy, gap, live, inter_hbm, out, inter, buf, en, gp, lv, sem, sems, slab_sem):
+def first_kernel(exch, energy, gap, live, out, buf, en, gp, lv, sem, sems):
     slots = slots_of(0, 4)
     small = start_all([(energy, en), (gap, gp), (live, lv)], sems)
     tiles = start_all([(exch.at[p], buf.at[i]) for i, p in enumerate(slots)], sem)
-    slabs = start_all([(inter_hbm.at[p], inter.at[p]) for p in slots[:1]], slab_sem)
     for c in small:
         c.wait()
     dens = denominators(en, [gp[p] for p in slots], slots)
     for i, p in enumerate(slots):
         tiles[i].wait()
         out[i] = (-lv[p].astype(F32) * buf[i].astype(F32) / dens[i]).astype(BF16)
-    for c in slabs:
-        c.wait()
 
 
 def second_kernel(
-    exch, energy, gap, live, fock, nslot, nlive, inter_hbm, x, inter_in, out_a, out_b, ex, en, lists, coefs, inter,
+    exch, energy, gap, live, fock, nslot, nlive, inter_hbm, x, out_a, out_b, ex, en, lists, coefs, inter,
     gp, lv, fk, ns, nl, table, ends, sem, sems, slab_sem,
 ):
-    del x, inter_in
+    del x
     slots = slots_of(4, 8)
     base = base_slot()
     small = start_all([(energy, en), (gap, gp), (live, lv), (fock, fk), (nslot, ns), (nlive, nl)], sems)
     order = slots + slots_of(0, 4)
     tiles = start_all([(exch.at[p], ex.at[p]) for p in order], sem)
-    slabs = start_all([(inter_hbm.at[p], inter.at[p]) for p in order[5:]], slab_sem)
+    slabs = start_all([(inter_hbm.at[p], inter.at[p]) for p in order[4:]], slab_sem)
     for c in small:
         c.wait()
     dens = denominators(en, [gp[p] for p in slots], slots)
@@ -127,26 +124,35 @@
         c.wait()
 
 
-def run_list(which, lists, coefs, inter, src, acc, steps=(LONG, SHORT)):
-    off = which * CAP
-    count = lists[COUNTS + which]
-
-    def chunk(at, size):
-        for u in range(size):
-            code = lists[at + u]
-            n, p, q, s = code & 7, (code >> 3) & 7, (code >> 6) & 7, code >> 9
-            x = inter[p, n]
-            h = jnp.dot(x, src[s], preferred_element_type=F32).astype(BF16)
-            t = lax.dot_general(h, x, (((1,), (1,)), ((), ())), preferred_element_type=F32)
-            acc[q] = acc[q] - coefs[at + u] * t
-
-    if len(steps) > 1:
-        longs = (count + steps[0] - steps[1] - 1) // steps[0]
-        lax.fori_loop(0, longs, lambda i, _: chunk(off + i * steps[0], steps[0]) or 0, 0)
-        off = off + longs * steps[0]
-        count = count - longs * steps[0]
-    shorts = jnp.maximum(count + steps[-1] - 1, 0) // steps[-1]
-    lax.fori_loop(0, shorts, lambda i, _: chunk(off + i * steps[-1], steps[-1]) or 0, 0)
+def step(at, size, lists, coefs, inter, src, acc):
+    for u in range(size):
+        code = lists[at + u]
+        n, p, q, s = code & 7, (code >> 3) & 7, (code >> 6) & 7, code >> 9
+        x = inter[p, n]
+        h = jnp.dot(x, src[s], preferred_element_type=F32).astype(BF16)
+        t = lax.dot_general(h, x, (((1,), (1,)), ((), ())), preferred_element_type=F32)
+        acc[q] = acc[q] - coefs[at + u] * t
+
+
+def steps(at, count, size, *refs):
+    def body(i, _):
+        step(at + i * size, size, *refs)
+        return 0
+
+    lax.fori_loop(0, count, body, 0)
+
+
+def near_list(which, lists, *refs):
+    at, count = which * CAP, lists[COUNTS + which]
+    longs = (count + LONG - SHORT - 1) // LONG
+    steps(at, longs, LONG, lists, *refs)
+    left = jnp.maximum(count - longs * LONG + SHORT - 1, 0)
+    steps(at + longs * LONG, left // SHORT, SHORT, lists, *refs)
+
+
+def across_list_tail(which, lists, *refs):
+    more = jnp.maximum(lists[COUNTS + which] - 1, 0) // SHORT
+    steps(which * CAP + SHORT, more, SHORT, lists, *refs)
 
 
 def gather(src, x, ia, ib, iha, ihb):
@@ -179,27 +185,44 @@
         out[j // each][j % each] = a1.astype(BF16)
 
 
+def waits_longer():
+    return ((lax.axis_index("row") + 1) & 2) != 0
+
+
 def near_kernel_1(lists, coefs, inter_hbm, exch, energy, x, ia, ib, iha, ihb, inter_in, acc, amps, recip, src, inter, sem):
     del inter_in
     slabs = start_all([(inter_hbm.at[p], inter.at[p]) for p in slots_of(4, 8)], sem)
     gather(src, x, ia, ib, iha, ihb)
     start_half(0, lists, coefs, exch, energy, acc, amps, recip)
-    run_list(0, lists, coefs, inter, src, acc)
+    near_list(0, lists, coefs, inter, src, acc)
     for c in slabs:
         c.wait()
+
+    @pl.when(waits_longer())
+    def _():
+        start_half(1, lists, coefs, exch, energy, acc, amps, recip)
+        near_list(1, lists, coefs, inter, src, acc)
 
 
 def across_kernel(lists, coefs, inter, xh, recip, acc_in, amps_in, out, acc, amps):
     del acc_in, amps_in
-    run_list(2, lists, coefs, inter, xh, acc, (SHORT,))
+    refs = (lists, coefs, inter, xh, acc)
+    across_list_tail(2, *refs)
+    step(2 * CAP, SHORT, *refs)
     update_half(0, lists, acc, amps, recip, [out])
 
 
 def rest_kernel(lists, coefs, inter, exch, energy, src, xh, acc_in, amps_in, recip_in, out_a, out_b, acc, amps, recip):
     del acc_in, amps_in, recip_in
-    start_half(1, lists, coefs, exch, energy, acc, amps, recip)
-    run_list(1, lists, coefs, inter, src, acc)
-    run_list(3, lists, coefs, inter, xh, acc, (SHORT,))
+
+    @pl.when(jnp.logical_not(waits_longer()))
+    def _():
+        start_half(1, lists, coefs, exch, energy, acc, amps, recip)
+        near_list(1, lists, coefs, inter, src, acc)
+
+    refs = (lists, coefs, inter, xh, acc)
+    across_list_tail(3, *refs)
+    step(3 * CAP, SHORT, *refs)
     update_half(1, lists, acc, amps, recip, [out_a, out_b])
 
 
@@ -219,7 +242,7 @@
     sq[...] = total
     gather(src, x, ia, ib, iha, ihb)
     for half in range(2):
-        run_list(half, lists, coefs, inter, src, acc)
+        near_list(half, lists, coefs, inter, src, acc)
 
 
 def last_kernel(lists, coefs, inter, xh, recip, amps, sq1, acc_in, out, sums, acc, buf, sem):
@@ -227,8 +250,11 @@
     total = jnp.zeros((8, 128), F32)
     copies = []
     slots = slots_of(0, 8)
+    refs = (lists, coefs, inter, xh, acc)
     for half in range(2):
-        run_list(2 + half, lists, coefs, inter, xh, acc, (SHORT,))
+        across_list_tail(2 + half, *refs)
+    for half in range(2):
+        step((2 + half) * CAP, SHORT, *refs)
         for q in range(4 * half, 4 * half + 4):
             p = slots[q]
             res = lists[LIVE + p].astype(F32) * acc[q]
@@ -236,8 +262,9 @@
             buf[q] = amps[q] - res * recip[q]
             copies.append(pltpu.make_async_copy(buf.at[q], out.at[p], sem.at[q]))
             copies[-1].start()
-    lane = lax.broadcasted_iota(jnp.int32, sums.shape, 1)
-    sums[...] = jnp.where(lane == 0, jnp.sum(sq1[...]), jnp.where(lane == 1, jnp.sum(total), 0.0))
+    rows = (sums.shape[0], 128)
+    sums[:, :128] = jnp.broadcast_to(jnp.sum(sq1[...], axis=0, keepdims=True), rows)
+    sums[:, 128:] = jnp.broadcast_to(jnp.sum(total, axis=0, keepdims=True), rows)
     for c in copies:
         c.wait()
 
@@ -257,21 +284,21 @@
     tiles2 = pltpu.VMEM((2, v, v), BF16)
     slabs = pltpu.VMEM(intersection.shape, BF16)
     intersection = hbm(intersection)
-    x0, inter = pl.pallas_call(
-        first_kernel, out_shape=[tiles4, slabs], in_specs=[AN] * 5, out_specs=[VM] * 2,
-        scratch_shapes=[pltpu.VMEM((4, v, v), BF16), pltpu.VMEM((8, v), F32)] + per_pair + [dma((4,)), dma((3,)), dma((1,))],
+    x0 = pl.pallas_call(
+        first_kernel, out_shape=tiles4, in_specs=[AN] * 4, out_specs=VM,
+        scratch_shapes=[pltpu.VMEM((4, v, v), BF16), pltpu.VMEM((8, v), F32)] + per_pair + [dma((4,)), dma((3,))],
         compiler_params=params(8), cost_estimate=COST, name="first",
-    )(*big[:4], intersection)
+    )(*big[:4])
     xh = lax.ppermute(x0, "row", other_chip)
     i0a, i0b, exch, energy, lists, coefs, inter = pl.pallas_call(
         second_kernel,
         out_shape=[tiles2, tiles2, pltpu.VMEM((8, v, v), BF16), pltpu.VMEM((8, v), F32),
                    pltpu.SMEM((LIVE + 8,), jnp.int32), pltpu.SMEM((GAP + 8,), F32), slabs],
-        in_specs=[AN] * 9 + [VM], out_specs=[VM] * 4 + [SM] * 2 + [VM], input_output_aliases={9: 6},
+        in_specs=[AN] * 9, out_specs=[VM] * 4 + [SM] * 2 + [VM],
         scratch_shapes=per_pair + [pltpu.SMEM((8, 8), F32)] + [pltpu.SMEM((8, 8), jnp.int32)] * 2
-        + [pltpu.SMEM((24,), jnp.int32), pltpu.SMEM((4,), jnp.int32), dma((8,)), dma((6,)), dma((3,))],
+        + [pltpu.SMEM((24,), jnp.int32), pltpu.SMEM((4,), jnp.int32), dma((8,)), dma((6,)), dma((4,))],
         compiler_params=params(8), cost_estimate=COST, name="second",
-    )(*big, intersection, x0, vmem(inter))
+    )(*big, intersection, x0)
 
     def swap(*halves):
         return [vmem(lax.ppermute(h, "row", same_chip)) for h in halves]
@@ -302,13 +329,13 @@
         compiler_params=params(8), cost_estimate=COST, name="near2",
     )(*meta, inter, exch, energy, vmem(x1), vmem(i1a), vmem(i1b), *swap(i1a, i1b), vmem(amps), vmem(acc))
     out, sums, _ = pl.pallas_call(
-        last_kernel, out_shape=[jax.ShapeDtypeStruct((8, v, v), F32), pltpu.VMEM((count, 128), F32), tiles8],
+        last_kernel, out_shape=[jax.ShapeDtypeStruct((8, v, v), F32), pltpu.VMEM((count, 256), F32), tiles8],
         in_specs=[SM] * 2 + [VM] * 6, out_specs=[AN, VM, VM], input_output_aliases={7: 2},
         scratch_shapes=[pltpu.VMEM((8, v, v), F32), dma((8,))],
         compiler_params=params(8), cost_estimate=COST, name="last",
     )(*meta, inter, vmem(xh1), vmem(recip), vmem(amps), vmem(sq), vmem(acc))
     sums = lax.all_to_all(sums, "row", 0, 0, tiled=True)
-    norms = jnp.sqrt(jnp.sum(sums[:, :2], axis=0) / (amp_exch.shape[0] * count * v * v))
+    norms = jnp.sqrt(jnp.sum(sums.reshape(count, 2, 128), axis=(0, 2)) / (amp_exch.shape[0] * count * v * v))
     return out, norms
 
 

time: 48.4 us -> 48.3 us (level)
  blocking collectives: 11.3 us -> 13.6 us
  Pallas kernels: 18.9 us -> 17.6 us
  starting transfers between devices: 13.6 us -> 12.5 us
    all_to_all x1, blocking collectives: 11.3 us -> 13.6 us  [on_device(): sums = lax.all_to_all(sums, 'row', 0, 0, tiled=True)]
    ppermute x4, starting transfers between devices: 12.2 us -> 11.1 us  [swap(): return [vmem(lax.ppermute(h, 'row', same_chip)) for h in halves]]
    pallas_call x1, Pallas kernels: 4.73 us -> 3.65 us  [on_device(): pl.pallas_call(near_kernel_2, out_shape=[tiles8, pltpu.VMEM((8, 128), F32...]
  transfers between devices with their start and end apart: 6 -> 6, of which waited for: 4 -> 4; matrix products, arithmetic and copies ran while one was open for 0% -> 0% of each run, Pallas kernels for 28% -> 25%
where the time goes in v4:
time: 48.3 us; the launch traced here: 48 us
  Pallas kernels  17.6 us (36%)
  blocking collectives  13.6 us (28%)
  starting transfers between devices  12.5 us (26%)
  waiting for transfers between devices  2.92 us (6%)
  between operations  0.73 us (2%)
  other arithmetic  0.68 us (1%)
    all_to_all x1, blocking collectives, on_device(): sums = lax.all_to_all(sums, 'row', 0, 0, tiled=True)  13.6 us
    ppermute x4, starting transfers between devices, swap(): return [vmem(lax.ppermute(h, 'row', same_chip)) for h in halves]  11.1 us
    pallas_call x1, Pallas kernels, on_device(): pl.pallas_call(near_kernel_2, out_shape=[tiles8, pltpu.VMEM((8, 128), F32...  3.65 us
    pallas_call x1, Pallas kernels, on_device(): pl.pallas_call(rest_kernel, out_shape=[tiles2, tiles2] + [tiles8] * 3, in...  3.09 us
    pallas_call x1, Pallas kernels, on_device(): pl.pallas_call(last_kernel, out_shape=[jax.ShapeDtypeStruct((8, v, v), F3...  3.03 us
    ppermute x4, waiting for transfers between devices, swap(): return [vmem(lax.ppermute(h, 'row', same_chip)) for h in halves]  2.91 us
    pallas_call x1, Pallas kernels, on_device(): pl.pallas_call(second_kernel, out_shape=[tiles2, tiles2, pltpu.VMEM((8, v...  2.79 us
    pallas_call x1, Pallas kernels, on_device(): pl.pallas_call(near_kernel_1, out_shape=[tiles8] * 3 + [gathered, slabs],...  2.58 us
  transfers between devices with their start and end apart: 6, of which 4 were waited for; matrix products, arithmetic and copies ran while one was open for 0% of the time, Pallas kernels for 25%

profile of v4, /device:TPU:0, one launch (start us, length us, event | category | flops | bytes accessed | tf_op | source)
XLA Modules:
  0.0 48.0 jit_solution(6099393215534326446)
XLA Ops:
  0.6 1.4 %first.1.x = bf16[4,256,256]{2,1,0:T(8,128)(2,1)S(1)} custom-call(bf16[8,256,256]{2,1,0:T(8,128)(2,1)} %exch.3, f32[8,256]{1,0:T(8,128)} %energy.3, f32[8]{0:T(128)} %gap.3, s32[8]{0:T(128)} %live.3), custom_call_target="tpu_custom_call" | custom-call | flops 1000 | bytes 1000 | tf_op jit(solution)/shard_map/first/pallas_call | solution.py:287
  2.1 0.7 %collective-permute-start.2 = (bf16[4,256,256]{2,1,0:T(8,128)(2,1)S(1)}, bf16[4,256,256]{2,1,0:T(8,128)(2,1)S(1)}, u32[]{:S(2)}, u32[]{:S(2)}) collective-permute-start(bf16[4,256,256]{2,1,0:T(8,128)(2,1)S(1)} %first.1.x), channel_id=1, source_target_pairs={{1,2},{3,4},{5,6},{7,8},{9,10},{11,12},{13,14},{2,1},{4,3},{6,5},{... | collective-permute-start | bytes 1572872 | tf_op jit(solution)/shard_map/ppermute | solution.py:292
  2.8 2.8 %second.1 = (bf16[2,256,256]{2,1,0:T(8,128)(2,1)S(1)}, bf16[2,256,256]{2,1,0:T(8,128)(2,1)S(1)}, bf16[8,256,256]{2,1,0:T(8,128)(2,1)S(1)}, f32[8,256]{1,0:T(8,12...) custom-call(bf16[8,256,256]{2,1,0:T(8,128)(2,1)} %exch.3, f32[8,256]{1,0:T(8,128)} %energy.3, ...), custom_call_target="tpu_custom_call" | custom-call | flops 1000 | bytes 1000 | tf_op jit(solution)/shard_map/second/pallas_call | solution.py:293
  5.6 4.4 %collective-permute-start = (bf16[2,256,256]{2,1,0:T(8,128)(2,1)S(1)}, bf16[2,256,256]{2,1,0:T(8,128)(2,1)S(1)}, u32[]{:S(2)}, u32[]{:S(2)}) collective-permute-start(bf16[2,256,256]{2,1,0:T(8,128)(2,1)S(1)} %get-tuple-element.30.ia), channel_id=1, source_target_pairs={{0,1},{1,0},{2,3},{3,2},{4,5},{5,4},{6,7},{7,6},{8,9},{9,8},{10,11... | collective-permute-start | bytes 786440 | tf_op jit(solution)/shard_map/ppermute | solution.py:304
  9.9 0.1 collective-permute-start.1
  10.0 1.1 %collective-permute-done.iha = bf16[2,256,256]{2,1,0:T(8,128)(2,1)S(1)} collective-permute-done((bf16[2,256,256]{2,1,0:T(8,128)(2,1)S(1)}, bf16[2,256,256]{2,1,0:T(8,128)(2,1)S(1)}, u32[]{:S(2)}, u32[]{:S(2)}) %collective-permute-start) | collective-permute-done | bytes 262176 | tf_op jit(solution)/shard_map/ppermute | solution.py:304
  11.1 0.4 collective-permute-done.1.ihb
  11.5 2.6 %near1.1 = (f32[8,256,256]{2,1,0:T(8,128)S(1)}, f32[8,256,256]{2,1,0:T(8,128)S(1)}, f32[8,256,256]{2,1,0:T(8,128)S(1)}, bf16[12,256,256]{2,1,0:T(8,128)(2,1)S(1)}, bf16[8,8,256,256]{3,2,1,0:T(8,128)(2,1)S(1)}) custom-call(s32[300]{0:T(512)S(4)} %get-tuple-element.26.lists, f32[296]{0:T(512)S(4)} %get-tuple-element.27.coefs, ...), custom_call_target="tpu_custom_call", output_to_operand_aliasing={{4}: (10, {})} | custom-call | flops 1000 | bytes 1000 | tf_op jit(solution)/shard_map/near1/pallas_call | solution.py:309
  14.1 0.0 collective-permute-done.2.xh
  14.1 1.0 %across.1 = (bf16[4,256,256]{2,1,0:T(8,128)(2,1)S(1)}, f32[8,256,256]{2,1,0:T(8,128)S(1)}, f32[8,256,256]{2,1,0:T(8,128)S(1)}) custom-call(s32[300]{0:T(512)S(4)} %get-tuple-element.26.lists, f32[296]{0:T(512)S(4)} %get-tuple-element.27.coefs, bf16[8,8,256,256]{3,2,1,0:T(8,128)(2,1)S(1)} %get-tuple-element.33.inter, ...), custom_call_target="tpu_custom_call", output_to_operand_aliasing={{1}: (5, {}), {2}: (6, {})} | custom-call | flops 1000 | bytes 1000 | tf_op jit(solution)/shard_map/across/pallas_call | solution.py:315
  15.1 0.7 %collective-permute-start.3 = (bf16[4,256,256]{2,1,0:T(8,128)(2,1)S(1)}, bf16[4,256,256]{2,1,0:T(8,128)(2,1)S(1)}, u32[]{:S(2)}, u32[]{:S(2)}) collective-permute-start(bf16[4,256,256]{2,1,0:T(8,128)(2,1)S(1)} %get-tuple-element.37.x), channel_id=1, source_target_pairs={{1,2},{3,4},{5,6},{7,8},{9,10},{11,12},{13,14},{2,1},{4,3},{6,5},{... | collective-permute-start | bytes 1572872 | tf_op jit(solution)/shard_map/ppermute | solution.py:320
  15.8 3.1 %rest.1 = (bf16[2,256,256]{2,1,0:T(8,128)(2,1)S(1)}, bf16[2,256,256]{2,1,0:T(8,128)(2,1)S(1)}, f32[8,256,256]{2,1,0:T(8,128)S(1)}, f32[8,256,256]{2,1,0:T(8,128)S(1)}, f32[8,256,256]{2,1,0:T(8,128)S(1)}) custom-call(s32[300]{0:T(512)S(4)} %get-tuple-element.26.lists, ...), custom_call_target="tpu_custom_call", output_to_operand_aliasing={{2}: (7, {}), {3}: (8, {}), {4}: (9, {})} | custom-call | flops 1000 | bytes 1000 | tf_op jit(solution)/shard_map/rest/pallas_call | solution.py:321
  18.9 6.6 %collective-permute-start.4 = (bf16[2,256,256]{2,1,0:T(8,128)(2,1)S(1)}, bf16[2,256,256]{2,1,0:T(8,128)(2,1)S(1)}, u32[]{:S(2)}, u32[]{:S(2)}) collective-permute-start(bf16[2,256,256]{2,1,0:T(8,128)(2,1)S(1)} %get-tuple-element.43.ia), channel_id=1, source_target_pairs={{0,1},{1,0},{2,3},{3,2},{4,5},{5,4},{6,7},{7,6},{8,9},{9,8},{10,11... | collective-permute-start | bytes 786440 | tf_op jit(solution)/shard_map/ppermute | solution.py:304
  25.5 0.1 collective-permute-start.5
  25.6 1.1 %collective-permute-done.4.iha = bf16[2,256,256]{2,1,0:T(8,128)(2,1)S(1)} collective-permute-done((bf16[2,256,256]{2,1,0:T(8,128)(2,1)S(1)}, bf16[2,256,256]{2,1,0:T(8,128)(2,1)S(1)}, u32[]{:S(2)}, u32[]{:S(2)}) %collective-permute-start.4) | collective-permute-done | bytes 262176 | tf_op jit(solution)/shard_map/ppermute | solution.py:304
  26.6 0.4 collective-permute-done.5.ihb
  27.0 3.7 %near2.1 = (f32[8,256,256]{2,1,0:T(8,128)S(1)}, f32[8,128]{1,0:T(8,128)S(1)}) custom-call(s32[300]{0:T(512)S(4)} %get-tuple-element.26.lists, f32[296]{0:T(512)S(4)} %get-tuple-element.27.coefs, bf16[8,8,256,256]{3,2,1,0:T(8,128)(2,1)S(1)} %get-tuple-element.33.inter, ...), custom_call_target="tpu_custom_call", output_to_operand_aliasing={{0}: (11, {})} | custom-call | flops 1000 | bytes 1000 | tf_op jit(solution)/shard_map/near2/pallas_call | solution.py:326
  30.7 0.0 collective-permute-done.3.xh
  30.7 3.0 %last.1 = (f32[8,256,256]{2,1,0:T(8,128)}, f32[16,256]{1,0:T(8,128)S(1)}, f32[8,256,256]{2,1,0:T(8,128)S(1)}) custom-call(s32[300]{0:T(512)S(4)} %get-tuple-element.26.lists, f32[296]{0:T(512)S(4)} %get-tuple-element.27.coefs, bf16[8,8,256,256]{3,2,1,0:T(8,128)(2,1)S(1)} %get-tuple-element.33.inter, ...), custom_call_target="tpu_custom_call", output_to_operand_aliasing={{2}: (7, {})} | custom-call | flops 1000 | bytes 1000 | tf_op jit(solution)/shard_map/last/pallas_call | solution.py:331
  33.8 13.6 %all_to_all.9 = f32[16,1,256]{2,1,0:T(1,128)S(1)} all-to-all(f32[16,1,256]{2,1,0:T(1,128)S(1)} %copy.19), channel_id=1, replica_groups=mesh['grp'=2,'row'=16] {'row'}, dimensions={0} | all-to-all | bytes 32768 | tf_op jit(solution)/shard_map/all_to_all | solution.py:337
  47.3 0.1 bitcast_reduce_fusion
  47.5 0.5 %multiply_sqrt_fusion = f32[2]{0:T(128)} fusion(f32[2]{0:T(128)S(1)} %bitcast_reduce_fusion), kind=kLoop, calls=%fused_computation.1 | loop fusion | flops 2 | bytes 16 | tf_op jit(solution)/shard_map/sqrt | solution.py:338
  (2 shorter events, 0.1 us)
Async XLA Ops:
  2.1 12.0 %collective-permute-start.2 = (bf16[4,256,256]{2,1,0:T(8,128)(2,1)S(1)}, bf16[4,256,256]{2,1,0:T(8,128)(2,1)S(1)}, u32[]{:S(2)}, u32[]{:S(2)}) collective-permute-start(bf16[4,256,256]{2,1,0:T(8,128)(2,1)S(1)} %first.1.x), channel_id=1, source_target_pairs={{1,2},{3,4},{5,6},{7,8},{9,10},{11,12},{13,14},{2,1},{4,3},{6,5},{... | collective-permute-start | bytes 1572872 | tf_op jit(solution)/shard_map/ppermute | solution.py:292
  5.6 5.5 %collective-permute-start = (bf16[2,256,256]{2,1,0:T(8,128)(2,1)S(1)}, bf16[2,256,256]{2,1,0:T(8,128)(2,1)S(1)}, u32[]{:S(2)}, u32[]{:S(2)}) collective-permute-start(bf16[2,256,256]{2,1,0:T(8,128)(2,1)S(1)} %get-tuple-element.30.ia), channel_id=1, source_target_pairs={{0,1},{1,0},{2,3},{3,2},{4,5},{5,4},{6,7},{7,6},{8,9},{9,8},{10,11... | collective-permute-start | bytes 786440 | tf_op jit(solution)/shard_map/ppermute | solution.py:304
  9.9 1.5 %collective-permute-start.1 = (bf16[2,256,256]{2,1,0:T(8,128)(2,1)S(1)}, bf16[2,256,256]{2,1,0:T(8,128)(2,1)S(1)}, u32[]{:S(2)}, u32[]{:S(2)}) collective-permute-start(bf16[2,256,256]{2,1,0:T(8,128)(2,1)S(1)} %get-tuple-element.31.ib), channel_id=1, source_target_pairs={{0,1},{1,0},{2,3},{3,2},{4,5},{5,4},{6,7},{7,6},{8,9},{9,8},{10,11... | collective-permute-start | bytes 786440 | tf_op jit(solution)/shard_map/ppermute | solution.py:304
  15.1 15.6 %collective-permute-start.3 = (bf16[4,256,256]{2,1,0:T(8,128)(2,1)S(1)}, bf16[4,256,256]{2,1,0:T(8,128)(2,1)S(1)}, u32[]{:S(2)}, u32[]{:S(2)}) collective-permute-start(bf16[4,256,256]{2,1,0:T(8,128)(2,1)S(1)} %get-tuple-element.37.x), channel_id=1, source_target_pairs={{1,2},{3,4},{5,6},{7,8},{9,10},{11,12},{13,14},{2,1},{4,3},{6,5},{... | collective-permute-start | bytes 1572872 | tf_op jit(solution)/shard_map/ppermute | solution.py:320
  18.9 7.8 %collective-permute-start.4 = (bf16[2,256,256]{2,1,0:T(8,128)(2,1)S(1)}, bf16[2,256,256]{2,1,0:T(8,128)(2,1)S(1)}, u32[]{:S(2)}, u32[]{:S(2)}) collective-permute-start(bf16[2,256,256]{2,1,0:T(8,128)(2,1)S(1)} %get-tuple-element.43.ia), channel_id=1, source_target_pairs={{0,1},{1,0},{2,3},{3,2},{4,5},{5,4},{6,7},{7,6},{8,9},{9,8},{10,11... | collective-permute-start | bytes 786440 | tf_op jit(solution)/shard_map/ppermute | solution.py:304
  25.5 1.5 %collective-permute-start.5 = (bf16[2,256,256]{2,1,0:T(8,128)(2,1)S(1)}, bf16[2,256,256]{2,1,0:T(8,128)(2,1)S(1)}, u32[]{:S(2)}, u32[]{:S(2)}) collective-permute-start(bf16[2,256,256]{2,1,0:T(8,128)(2,1)S(1)} %get-tuple-element.44.ib), channel_id=1, source_target_pairs={{0,1},{1,0},{2,3},{3,2},{4,5},{5,4},{6,7},{7,6},{8,9},{9,8},{10,11... | collective-permute-start | bytes 786440 | tf_op jit(solution)/shard_map/ppermute | solution.py:304

commit v5 on v4

--- a/solution.py
+++ b/solution.py
@@ -57,34 +57,27 @@
     return copies
 
 
-def first_kernel(exch, energy, gap, live, out, buf, en, gp, lv, sem, sems):
-    slots = slots_of(0, 4)
-    small = start_all([(energy, en), (gap, gp), (live, lv)], sems)
-    tiles = start_all([(exch.at[p], buf.at[i]) for i, p in enumerate(slots)], sem)
-    for c in small:
+def goes_second():
+    return ((lax.axis_index("row") + 1) & 2) == 0
+
+
+def prepare_copies(exch, energy, gap, live, fock, nslot, nlive, inter_hbm, ex, en, inter, gp, lv, fk, ns, nl, sem, sems, slab_sem):
+    small = [(energy, en), (gap, gp), (live, lv), (fock, fk), (nslot, ns), (nlive, nl)]
+    order = slots_of(4, 8) + slots_of(0, 4)
+    pairs = [(a, b, sems.at[i]) for i, (a, b) in enumerate(small)]
+    pairs += [(exch.at[p], ex.at[p], sem.at[i]) for i, p in enumerate(order)]
+    pairs += [(inter_hbm.at[p], inter.at[p], slab_sem.at[i]) for i, p in enumerate(order[4:])]
+    return [pltpu.make_async_copy(*three) for three in pairs]
+
+
+def prepare(copies, out_a, out_b, ex, en, lists, coefs, gp, lv, fk, ns, nl, table, ends):
+    slots = slots_of(4, 8)
+    base = base_slot()
+    for c in copies[:6]:
         c.wait()
     dens = denominators(en, [gp[p] for p in slots], slots)
     for i, p in enumerate(slots):
-        tiles[i].wait()
-        out[i] = (-lv[p].astype(F32) * buf[i].astype(F32) / dens[i]).astype(BF16)
-
-
-def second_kernel(
-    exch, energy, gap, live, fock, nslot, nlive, inter_hbm, x, out_a, out_b, ex, en, lists, coefs, inter,
-    gp, lv, fk, ns, nl, table, ends, sem, sems, slab_sem,
-):
-    del x
-    slots = slots_of(4, 8)
-    base = base_slot()
-    small = start_all([(energy, en), (gap, gp), (live, lv), (fock, fk), (nslot, ns), (nlive, nl)], sems)
-    order = slots + slots_of(0, 4)
-    tiles = start_all([(exch.at[p], ex.at[p]) for p in order], sem)
-    slabs = start_all([(inter_hbm.at[p], inter.at[p]) for p in order[4:]], slab_sem)
-    for c in small:
-        c.wait()
-    dens = denominators(en, [gp[p] for p in slots], slots)
-    for i, p in enumerate(slots):
-        tiles[i].wait()
+        copies[6 + i].wait()
         tile = (-lv[p].astype(F32) * ex[p].astype(F32) / dens[i]).astype(BF16)
         if i < 2:
             out_a[i] = tile
@@ -120,8 +113,48 @@
     for p in range(8):
         lists[LIVE + p] = lv[p]
         coefs[GAP + p] = gp[p]
-    for c in tiles[4:] + slabs:
-        c.wait()
+    for c in copies[10:]:
+        c.wait()
+
+
+def first_kernel(*refs):
+    ins, (out, out_a, out_b, ex, en, lists, coefs, inter), own, rest = refs[:8], refs[8:16], refs[16:22], refs[22:]
+    exch, energy, gap, live = ins[:4]
+    buf, en4, gp4, lv4, sem4, sems4 = own
+    scalars, sems = rest[:7], rest[7:]
+    late = goes_second()
+    slots = slots_of(0, 4)
+    small = start_all([(energy, en4), (gap, gp4), (live, lv4)], sems4)
+    tiles = start_all([(exch.at[p], buf.at[i]) for i, p in enumerate(slots)], sem4)
+    copies = prepare_copies(*ins, ex, en, inter, *scalars[:5], *sems)
+
+    @pl.when(late)
+    def _():
+        for c in copies:
+            c.start()
+
+    for c in small:
+        c.wait()
+    dens = denominators(en4, [gp4[p] for p in slots], slots)
+    for i, p in enumerate(slots):
+        tiles[i].wait()
+        out[i] = (-lv4[p].astype(F32) * buf[i].astype(F32) / dens[i]).astype(BF16)
+
+    @pl.when(late)
+    def _():
+        prepare(copies, out_a, out_b, ex, en, lists, coefs, *scalars)
+
+
+def second_kernel(*refs):
+    ins, (out_a, out_b, ex, en, lists, coefs, inter), rest = refs[:8], refs[15:22], refs[22:]
+    scalars, sems = rest[:7], rest[7:]
+
+    @pl.when(jnp.logical_not(goes_second()))
+    def _():
+        copies = prepare_copies(*ins, ex, en, inter, *scalars[:5], *sems)
+        for c in copies:
+            c.start()
+        prepare(copies, out_a, out_b, ex, en, lists, coefs, *scalars)
 
 
 def step(at, size, lists, coefs, inter, src, acc):
@@ -185,10 +218,6 @@
         out[j // each][j % each] = a1.astype(BF16)
 
 
-def waits_longer():
-    return ((lax.axis_index("row") + 1) & 2) != 0
-
-
 def near_kernel_1(lists, coefs, inter_hbm, exch, energy, x, ia, ib, iha, ihb, inter_in, acc, amps, recip, src, inter, sem):
     del inter_in
     slabs = start_all([(inter_hbm.at[p], inter.at[p]) for p in slots_of(4, 8)], sem)
@@ -198,7 +227,7 @@
     for c in slabs:
         c.wait()
 
-    @pl.when(waits_longer())
+    @pl.when(goes_second())
     def _():
         start_half(1, lists, coefs, exch, energy, acc, amps, recip)
         near_list(1, lists, coefs, inter, src, acc)
@@ -215,7 +244,7 @@
 def rest_kernel(lists, coefs, inter, exch, energy, src, xh, acc_in, amps_in, recip_in, out_a, out_b, acc, amps, recip):
     del acc_in, amps_in, recip_in
 
-    @pl.when(jnp.logical_not(waits_longer()))
+    @pl.when(jnp.logical_not(goes_second()))
     def _():
         start_half(1, lists, coefs, exch, energy, acc, amps, recip)
         near_list(1, lists, coefs, inter, src, acc)
@@ -284,21 +313,23 @@
     tiles2 = pltpu.VMEM((2, v, v), BF16)
     slabs = pltpu.VMEM(intersection.shape, BF16)
     intersection = hbm(intersection)
-    x0 = pl.pallas_call(
-        first_kernel, out_shape=tiles4, in_specs=[AN] * 4, out_specs=VM,
-        scratch_shapes=[pltpu.VMEM((4, v, v), BF16), pltpu.VMEM((8, v), F32)] + per_pair + [dma((4,)), dma((3,))],
+    shapes = [tiles2, tiles2, pltpu.VMEM((8, v, v), BF16), pltpu.VMEM((8, v), F32),
+              pltpu.SMEM((LIVE + 8,), jnp.int32), pltpu.SMEM((GAP + 8,), F32), slabs]
+    places = [VM] * 4 + [SM] * 2 + [VM]
+    scratch = per_pair + [pltpu.SMEM((8, 8), F32)] + [pltpu.SMEM((8, 8), jnp.int32)] * 2
+    scratch += [pltpu.SMEM((24,), jnp.int32), pltpu.SMEM((4,), jnp.int32), dma((8,)), dma((6,)), dma((4,))]
+    x0, *made = pl.pallas_call(
+        first_kernel, out_shape=[tiles4] + shapes, in_specs=[AN] * 8, out_specs=[VM] + places,
+        scratch_shapes=[pltpu.VMEM((4, v, v), BF16), pltpu.VMEM((8, v), F32)] + per_pair + [dma((4,)), dma((3,))] + scratch,
         compiler_params=params(8), cost_estimate=COST, name="first",
-    )(*big[:4])
+    )(*big, intersection)
     xh = lax.ppermute(x0, "row", other_chip)
+    made = [m if i in (4, 5) else vmem(m) for i, m in enumerate(made)]
     i0a, i0b, exch, energy, lists, coefs, inter = pl.pallas_call(
-        second_kernel,
-        out_shape=[tiles2, tiles2, pltpu.VMEM((8, v, v), BF16), pltpu.VMEM((8, v), F32),
-                   pltpu.SMEM((LIVE + 8,), jnp.int32), pltpu.SMEM((GAP + 8,), F32), slabs],
-        in_specs=[AN] * 9, out_specs=[VM] * 4 + [SM] * 2 + [VM],
-        scratch_shapes=per_pair + [pltpu.SMEM((8, 8), F32)] + [pltpu.SMEM((8, 8), jnp.int32)] * 2
-        + [pltpu.SMEM((24,), jnp.int32), pltpu.SMEM((4,), jnp.int32), dma((8,)), dma((6,)), dma((4,))],
+        second_kernel, out_shape=shapes, in_specs=[AN] * 8 + places,
+        out_specs=places, input_output_aliases={8 + i: i for i in range(7)}, scratch_shapes=scratch,
         compiler_params=params(8), cost_estimate=COST, name="second",
-    )(*big, intersection, x0)
+    )(*big, intersection, *made)
 
     def swap(*halves):
         return [vmem(lax.ppermute(h, "row", same_chip)) for h in halves]

time: 48.3 us -> 51.1 us (1.058)
  Pallas kernels: 17.6 us -> 19.5 us
    pallas_call x1, Pallas kernels: 2.58 us -> 5.29 us  [on_device(): pl.pallas_call(near_kernel_1, out_shape=[tiles8] * 3 + [gathered, slabs],...]
    pallas_call x1, Pallas kernels: 3.09 us -> 1.2 us  [on_device(): pl.pallas_call(rest_kernel, out_shape=[tiles2, tiles2] + [tiles8] * 3, in...]
    pallas_call x1, Pallas kernels: 3.65 us -> 4.49 us  [on_device(): pl.pallas_call(near_kernel_2, out_shape=[tiles8, pltpu.VMEM((8, 128), F32...]
    all_to_all x1, blocking collectives: 13.6 us -> 14.1 us  [on_device(): sums = lax.all_to_all(sums, 'row', 0, 0, tiled=True)]
  transfers between devices with their start and end apart: 6 -> 6, of which waited for: 4 -> 4; matrix products, arithmetic and copies ran while one was open for 0% -> 0% of each run, Pallas kernels for 25% -> 22%
where the time goes in v5:
time: 51.1 us; the launch traced here: 50.8 us
  Pallas kernels  19.5 us (38%)
  blocking collectives  14.1 us (28%)
  starting transfers between devices  12.9 us (25%)
  waiting for transfers between devices  2.92 us (6%)
  between operations  0.73 us (1%)
  other arithmetic  0.68 us (1%)
    all_to_all x1, blocking collectives, on_device(): sums = lax.all_to_all(sums, 'row', 0, 0, tiled=True)  14.1 us
    ppermute x4, starting transfers between devices, swap(): return [vmem(lax.ppermute(h, 'row', same_chip)) for h in halves]  11.5 us
    pallas_call x1, Pallas kernels, on_device(): pl.pallas_call(near_kernel_1, out_shape=[tiles8] * 3 + [gathered, slabs],...  5.29 us
    pallas_call x1, Pallas kernels, on_device(): pl.pallas_call(near_kernel_2, out_shape=[tiles8, pltpu.VMEM((8, 128), F32...  4.49 us
    pallas_call x1, Pallas kernels, on_device(): pl.pallas_call(first_kernel, out_shape=[tiles4] + shapes, in_specs=[AN] *...  4.33 us
    pallas_call x1, Pallas kernels, on_device(): pl.pallas_call(last_kernel, out_shape=[jax.ShapeDtypeStruct((8, v, v), F3...  3 us
    ppermute x4, waiting for transfers between devices, swap(): return [vmem(lax.ppermute(h, 'row', same_chip)) for h in halves]  2.91 us
    pallas_call x1, Pallas kernels, on_device(): pl.pallas_call(rest_kernel, out_shape=[tiles2, tiles2] + [tiles8] * 3, in...  1.2 us
  transfers between devices with their start and end apart: 6, of which 4 were waited for; matrix products, arithmetic and copies ran while one was open for 0% of the time, Pallas kernels for 22%

profile of v5, /device:TPU:0, one launch (start us, length us, event | category | flops | bytes accessed | tf_op | source)
XLA Modules:
  0.0 50.8 jit_solution(15805931160491939636)
XLA Ops:
  0.6 4.3 %first.1 = (bf16[4,256,256]{2,1,0:T(8,128)(2,1)S(1)}, bf16[2,256,256]{2,1,0:T(8,128)(2,1)S(1)}, bf16[2,256,256]{2,1,0:T(8,128)(2,1)S(1)}, bf16[8,256,256]{2,1,0:...) custom-call(bf16[8,256,256]{2,1,0:T(8,128)(2,1)} %refs_0_.3, ...), custom_call_target="tpu_custom_call" | custom-call | flops 1000 | bytes 1000 | tf_op jit(solution)/shard_map/first/pallas_call | solution.py:321
  5.0 0.7 %collective-permute-start.2 = (bf16[4,256,256]{2,1,0:T(8,128)(2,1)S(1)}, bf16[4,256,256]{2,1,0:T(8,128)(2,1)S(1)}, u32[]{:S(2)}, u32[]{:S(2)}) collective-permute-start(bf16[4,256,256]{2,1,0:T(8,128)(2,1)S(1)} %get-tuple-element.45.x), channel_id=1, source_target_pairs={{1,2},{3,4},{5,6},{7,8},{9,10},{11,12},{13,14},{2,1},{4,3},{6,5},{... | collective-permute-start | bytes 1572872 | tf_op jit(solution)/shard_map/ppermute | solution.py:326
  5.7 0.2 second.1
  5.9 4.3 %collective-permute-start = (bf16[2,256,256]{2,1,0:T(8,128)(2,1)S(1)}, bf16[2,256,256]{2,1,0:T(8,128)(2,1)S(1)}, u32[]{:S(2)}, u32[]{:S(2)}) collective-permute-start(bf16[2,256,256]{2,1,0:T(8,128)(2,1)S(1)} %get-tuple-element.46.ia), channel_id=1, source_target_pairs={{0,1},{1,0},{2,3},{3,2},{4,5},{5,4},{6,7},{7,6},{8,9},{9,8},{10,11... | collective-permute-start | bytes 786440 | tf_op jit(solution)/shard_map/ppermute | solution.py:335
  10.1 0.1 collective-permute-start.1
  10.2 1.1 %collective-permute-done.iha = bf16[2,256,256]{2,1,0:T(8,128)(2,1)S(1)} collective-permute-done((bf16[2,256,256]{2,1,0:T(8,128)(2,1)S(1)}, bf16[2,256,256]{2,1,0:T(8,128)(2,1)S(1)}, u32[]{:S(2)}, u32[]{:S(2)}) %collective-permute-start) | collective-permute-done | bytes 262176 | tf_op jit(solution)/shard_map/ppermute | solution.py:335
  11.3 0.4 collective-permute-done.1.ihb
  11.7 5.3 %near1.1 = (f32[8,256,256]{2,1,0:T(8,128)S(1)}, f32[8,256,256]{2,1,0:T(8,128)S(1)}, f32[8,256,256]{2,1,0:T(8,128)S(1)}, bf16[12,256,256]{2,1,0:T(8,128)(2,1)S(1)}, bf16[8,8,256,256]{3,2,1,0:T(8,128)(2,1)S(1)}) custom-call(s32[300]{0:T(512)S(4)} %get-tuple-element.41.lists, f32[296]{0:T(512)S(4)} %get-tuple-element.42.coefs, ...), custom_call_target="tpu_custom_call", output_to_operand_aliasing={{4}: (10, {})} | custom-call | flops 1000 | bytes 1000 | tf_op jit(solution)/shard_map/near1/pallas_call | solution.py:340
  17.0 0.0 collective-permute-done.2.xh
  17.0 1.0 %across.1 = (bf16[4,256,256]{2,1,0:T(8,128)(2,1)S(1)}, f32[8,256,256]{2,1,0:T(8,128)S(1)}, f32[8,256,256]{2,1,0:T(8,128)S(1)}) custom-call(s32[300]{0:T(512)S(4)} %get-tuple-element.41.lists, f32[296]{0:T(512)S(4)} %get-tuple-element.42.coefs, bf16[8,8,256,256]{3,2,1,0:T(8,128)(2,1)S(1)} %get-tuple-element.49.inter, ...), custom_call_target="tpu_custom_call", output_to_operand_aliasing={{1}: (5, {}), {2}: (6, {})} | custom-call | flops 1000 | bytes 1000 | tf_op jit(solution)/shard_map/across/pallas_call | solution.py:346
  18.0 0.7 %collective-permute-start.3 = (bf16[4,256,256]{2,1,0:T(8,128)(2,1)S(1)}, bf16[4,256,256]{2,1,0:T(8,128)(2,1)S(1)}, u32[]{:S(2)}, u32[]{:S(2)}) collective-permute-start(bf16[4,256,256]{2,1,0:T(8,128)(2,1)S(1)} %get-tuple-element.53.x), channel_id=1, source_target_pairs={{1,2},{3,4},{5,6},{7,8},{9,10},{11,12},{13,14},{2,1},{4,3},{6,5},{... | collective-permute-start | bytes 1572872 | tf_op jit(solution)/shard_map/ppermute | solution.py:351
  18.7 1.2 %rest.1 = (bf16[2,256,256]{2,1,0:T(8,128)(2,1)S(1)}, bf16[2,256,256]{2,1,0:T(8,128)(2,1)S(1)}, f32[8,256,256]{2,1,0:T(8,128)S(1)}, f32[8,256,256]{2,1,0:T(8,128)S(1)}, f32[8,256,256]{2,1,0:T(8,128)S(1)}) custom-call(s32[300]{0:T(512)S(4)} %get-tuple-element.41.lists, ...), custom_call_target="tpu_custom_call", output_to_operand_aliasing={{2}: (7, {}), {3}: (8, {}), {4}: (9, {})} | custom-call | flops 1000 | bytes 1000 | tf_op jit(solution)/shard_map/rest/pallas_call | solution.py:352
  19.9 7.1 %collective-permute-start.4 = (bf16[2,256,256]{2,1,0:T(8,128)(2,1)S(1)}, bf16[2,256,256]{2,1,0:T(8,128)(2,1)S(1)}, u32[]{:S(2)}, u32[]{:S(2)}) collective-permute-start(bf16[2,256,256]{2,1,0:T(8,128)(2,1)S(1)} %get-tuple-element.59.ia), channel_id=1, source_target_pairs={{0,1},{1,0},{2,3},{3,2},{4,5},{5,4},{6,7},{7,6},{8,9},{9,8},{10,11... | collective-permute-start | bytes 786440 | tf_op jit(solution)/shard_map/ppermute | solution.py:335
  27.0 0.1 collective-permute-start.5
  27.1 1.1 %collective-permute-done.4.iha = bf16[2,256,256]{2,1,0:T(8,128)(2,1)S(1)} collective-permute-done((bf16[2,256,256]{2,1,0:T(8,128)(2,1)S(1)}, bf16[2,256,256]{2,1,0:T(8,128)(2,1)S(1)}, u32[]{:S(2)}, u32[]{:S(2)}) %collective-permute-start.4) | collective-permute-done | bytes 262176 | tf_op jit(solution)/shard_map/ppermute | solution.py:335
  28.1 0.4 collective-permute-done.5.ihb
  28.5 4.5 %near2.1 = (f32[8,256,256]{2,1,0:T(8,128)S(1)}, f32[8,128]{1,0:T(8,128)S(1)}) custom-call(s32[300]{0:T(512)S(4)} %get-tuple-element.41.lists, f32[296]{0:T(512)S(4)} %get-tuple-element.42.coefs, bf16[8,8,256,256]{3,2,1,0:T(8,128)(2,1)S(1)} %get-tuple-element.49.inter, ...), custom_call_target="tpu_custom_call", output_to_operand_aliasing={{0}: (11, {})} | custom-call | flops 1000 | bytes 1000 | tf_op jit(solution)/shard_map/near2/pallas_call | solution.py:357
  33.0 0.0 collective-permute-done.3.xh
  33.0 3.0 %last.1 = (f32[8,256,256]{2,1,0:T(8,128)}, f32[16,256]{1,0:T(8,128)S(1)}, f32[8,256,256]{2,1,0:T(8,128)S(1)}) custom-call(s32[300]{0:T(512)S(4)} %get-tuple-element.41.lists, f32[296]{0:T(512)S(4)} %get-tuple-element.42.coefs, bf16[8,8,256,256]{3,2,1,0:T(8,128)(2,1)S(1)} %get-tuple-element.49.inter, ...), custom_call_target="tpu_custom_call", output_to_operand_aliasing={{2}: (7, {})} | custom-call | flops 1000 | bytes 1000 | tf_op jit(solution)/shard_map/last/pallas_call | solution.py:362
  36.0 14.1 %all_to_all.9 = f32[16,1,256]{2,1,0:T(1,128)S(1)} all-to-all(f32[16,1,256]{2,1,0:T(1,128)S(1)} %copy.26), channel_id=1, replica_groups=mesh['grp'=2,'row'=16] {'row'}, dimensions={0} | all-to-all | bytes 32768 | tf_op jit(solution)/shard_map/all_to_all | solution.py:368
  50.2 0.1 bitcast_reduce_fusion
  50.3 0.5 %multiply_sqrt_fusion = f32[2]{0:T(128)} fusion(f32[2]{0:T(128)S(1)} %bitcast_reduce_fusion), kind=kLoop, calls=%fused_computation.1 | loop fusion | flops 2 | bytes 16 | tf_op jit(solution)/shard_map/sqrt | solution.py:369
  (2 shorter events, 0.1 us)
Async XLA Ops:
  5.0 12.0 %collective-permute-start.2 = (bf16[4,256,256]{2,1,0:T(8,128)(2,1)S(1)}, bf16[4,256,256]{2,1,0:T(8,128)(2,1)S(1)}, u32[]{:S(2)}, u32[]{:S(2)}) collective-permute-start(bf16[4,256,256]{2,1,0:T(8,128)(2,1)S(1)} %get-tuple-element.45.x), channel_id=1, source_target_pairs={{1,2},{3,4},{5,6},{7,8},{9,10},{11,12},{13,14},{2,1},{4,3},{6,5},{... | collective-permute-start | bytes 1572872 | tf_op jit(solution)/shard_map/ppermute | solution.py:326
  5.9 5.5 %collective-permute-start = (bf16[2,256,256]{2,1,0:T(8,128)(2,1)S(1)}, bf16[2,256,256]{2,1,0:T(8,128)(2,1)S(1)}, u32[]{:S(2)}, u32[]{:S(2)}) collective-permute-start(bf16[2,256,256]{2,1,0:T(8,128)(2,1)S(1)} %get-tuple-element.46.ia), channel_id=1, source_target_pairs={{0,1},{1,0},{2,3},{3,2},{4,5},{5,4},{6,7},{7,6},{8,9},{9,8},{10,11... | collective-permute-start | bytes 786440 | tf_op jit(solution)/shard_map/ppermute | solution.py:335
  10.1 1.5 %collective-permute-start.1 = (bf16[2,256,256]{2,1,0:T(8,128)(2,1)S(1)}, bf16[2,256,256]{2,1,0:T(8,128)(2,1)S(1)}, u32[]{:S(2)}, u32[]{:S(2)}) collective-permute-start(bf16[2,256,256]{2,1,0:T(8,128)(2,1)S(1)} %get-tuple-element.47.ib), channel_id=1, source_target_pairs={{0,1},{1,0},{2,3},{3,2},{4,5},{5,4},{6,7},{7,6},{8,9},{9,8},{10,11... | collective-permute-start | bytes 786440 | tf_op jit(solution)/shard_map/ppermute | solution.py:335
  18.0 15.0 %collective-permute-start.3 = (bf16[4,256,256]{2,1,0:T(8,128)(2,1)S(1)}, bf16[4,256,256]{2,1,0:T(8,128)(2,1)S(1)}, u32[]{:S(2)}, u32[]{:S(2)}) collective-permute-start(bf16[4,256,256]{2,1,0:T(8,128)(2,1)S(1)} %get-tuple-element.53.x), channel_id=1, source_target_pairs={{1,2},{3,4},{5,6},{7,8},{9,10},{11,12},{13,14},{2,1},{4,3},{6,5},{... | collective-permute-start | bytes 1572872 | tf_op jit(solution)/shard_map/ppermute | solution.py:351
  19.9 8.2 %collective-permute-start.4 = (bf16[2,256,256]{2,1,0:T(8,128)(2,1)S(1)}, bf16[2,256,256]{2,1,0:T(8,128)(2,1)S(1)}, u32[]{:S(2)}, u32[]{:S(2)}) collective-permute-start(bf16[2,256,256]{2,1,0:T(8,128)(2,1)S(1)} %get-tuple-element.59.ia), channel_id=1, source_target_pairs={{0,1},{1,0},{2,3},{3,2},{4,5},{5,4},{6,7},{7,6},{8,9},{9,8},{10,11... | collective-permute-start | bytes 786440 | tf_op jit(solution)/shard_map/ppermute | solution.py:335
  27.0 1.5 %collective-permute-start.5 = (bf16[2,256,256]{2,1,0:T(8,128)(2,1)S(1)}, bf16[2,256,256]{2,1,0:T(8,128)(2,1)S(1)}, u32[]{:S(2)}, u32[]{:S(2)}) collective-permute-start(bf16[2,256,256]{2,1,0:T(8,128)(2,1)S(1)} %get-tuple-element.60.ib), channel_id=1, source_target_pairs={{0,1},{1,0},{2,3},{3,2},{4,5},{5,4},{6,7},{7,6},{8,9},{9,8},{10,11... | collective-permute-start | bytes 786440 | tf_op jit(solution)/shard_map/ppermute | solution.py:335

commit v6 on v4

--- a/solution.py
+++ b/solution.py
@@ -12,10 +12,12 @@
 VM = pl.BlockSpec(memory_space=pltpu.VMEM)
 SM = pl.BlockSpec(memory_space=pltpu.SMEM)
 AN = pl.BlockSpec(memory_space=pl.ANY)
-CAP = 72
+CAP = 80
 LONG, SHORT = 16, 8
-COUNTS, LIVE = 4 * CAP, 4 * CAP + 4
-GAP = 4 * CAP
+LISTS = 7
+COUNTS, LIVE = LISTS * CAP, LISTS * CAP + LISTS
+GAP = LISTS * CAP
+EARLY = 3
 MIB = 1 << 20
 
 
@@ -96,7 +98,7 @@
         table[16 + s] = jnp.where(base == 0, ((8 + s) << 9) | 1, (s << 9) | 3)
     for s in range(8):
         table[8 + s] = (((s + base) & 7) << 9) | lv[s]
-    for k in range(4):
+    for k in range(LISTS):
         ends[k] = k * CAP
 
     def entry(i, _):
@@ -107,11 +109,19 @@
         pos = ends[which]
         lists[pos] = ((what >> 9) << 9) | (q << 6) | (p << 3) | n
         coefs[pos] = fk[p, n]
-        ends[which] = pos + (nl[p, n] & lv[p] & what & 1)
+        one = nl[p, n] & lv[p] & what & 1
+        ends[which] = pos + one
+        s = what >> 9
+        late = s >= EARLY
+        which = jnp.where((what & 2) != 0, jnp.where(late, 5, 4), 6)
+        pos = ends[which]
+        lists[pos] = (jnp.where(late, s - EARLY, s) << 9) | (q << 6) | (p << 3) | n
+        coefs[pos] = fk[p, n]
+        ends[which] = pos + one
         return 0
 
     lax.fori_loop(0, 64, entry, 0, unroll=4)
-    for k in range(4):
+    for k in range(LISTS - 1):
         e = ends[k]
         lists[COUNTS + k] = e - k * CAP
         for u in range(LONG):
@@ -142,7 +152,7 @@
     lax.fori_loop(0, count, body, 0)
 
 
-def near_list(which, lists, *refs):
+def long_list(which, lists, *refs):
     at, count = which * CAP, lists[COUNTS + which]
     longs = (count + LONG - SHORT - 1) // LONG
     steps(at, longs, LONG, lists, *refs)
@@ -155,8 +165,11 @@
     steps(which * CAP + SHORT, more, SHORT, lists, *refs)
 
 
-def gather(src, x, ia, ib, iha, ihb):
-    src[0:4] = x[...]
+def gather(src, xs, ia, ib, iha, ihb):
+    at = 0
+    for x in xs:
+        src[at : at + x.shape[0]] = x[...]
+        at += x.shape[0]
     src[4:6] = ia[...]
     src[6:8] = ib[...]
     src[8:10] = iha[...]
@@ -176,13 +189,13 @@
 
 
 def update_half(half, lists, acc, amps, recip, out):
-    each = 4 // len(out)
+    places = [o.at[k] for o in out for k in range(o.shape[0])]
     for j, p in enumerate(slots_of(4 * half, 4 * half + 4)):
         q = 4 * half + j
         res = lists[LIVE + p].astype(F32) * acc[q]
         a1 = amps[q] - res * recip[q]
         amps[q] = a1
-        out[j // each][j % each] = a1.astype(BF16)
+        places[j][...] = a1.astype(BF16)
 
 
 def waits_longer():
@@ -192,24 +205,24 @@
 def near_kernel_1(lists, coefs, inter_hbm, exch, energy, x, ia, ib, iha, ihb, inter_in, acc, amps, recip, src, inter, sem):
     del inter_in
     slabs = start_all([(inter_hbm.at[p], inter.at[p]) for p in slots_of(4, 8)], sem)
-    gather(src, x, ia, ib, iha, ihb)
+    gather(src, [x], ia, ib, iha, ihb)
     start_half(0, lists, coefs, exch, energy, acc, amps, recip)
-    near_list(0, lists, coefs, inter, src, acc)
+    long_list(0, lists, coefs, inter, src, acc)
     for c in slabs:
         c.wait()
 
     @pl.when(waits_longer())
     def _():
         start_half(1, lists, coefs, exch, energy, acc, amps, recip)
-        near_list(1, lists, coefs, inter, src, acc)
-
-
-def across_kernel(lists, coefs, inter, xh, recip, acc_in, amps_in, out, acc, amps):
+        long_list(1, lists, coefs, inter, src, acc)
+
+
+def across_kernel(lists, coefs, inter, xh, recip, acc_in, amps_in, out_a, out_b, acc, amps):
     del acc_in, amps_in
     refs = (lists, coefs, inter, xh, acc)
     across_list_tail(2, *refs)
     step(2 * CAP, SHORT, *refs)
-    update_half(0, lists, acc, amps, recip, [out])
+    update_half(0, lists, acc, amps, recip, [out_a, out_b])
 
 
 def rest_kernel(lists, coefs, inter, exch, energy, src, xh, acc_in, amps_in, recip_in, out_a, out_b, acc, amps, recip):
@@ -218,7 +231,7 @@
     @pl.when(jnp.logical_not(waits_longer()))
     def _():
         start_half(1, lists, coefs, exch, energy, acc, amps, recip)
-        near_list(1, lists, coefs, inter, src, acc)
+        long_list(1, lists, coefs, inter, src, acc)
 
     refs = (lists, coefs, inter, xh, acc)
     across_list_tail(3, *refs)
@@ -231,7 +244,7 @@
     return s[:, :128] + s[:, 128:]
 
 
-def near_kernel_2(lists, coefs, inter, exch, energy, x, ia, ib, iha, ihb, amps, acc_in, acc, sq, src):
+def near_kernel_2(lists, coefs, inter, exch, energy, xa, xb, ia, ib, iha, ihb, amps, acc_in, acc, sq, src):
     del acc_in
     slots = slots_of(0, 8)
     dens = denominators(energy, [coefs[GAP + p] for p in slots], slots)
@@ -240,28 +253,29 @@
         total = total + squares(lists[LIVE + p].astype(F32) * acc[q])
         acc[q] = exch[p].astype(F32) + dens[q] * amps[q]
     sq[...] = total
-    gather(src, x, ia, ib, iha, ihb)
+    gather(src, [xa, xb], ia, ib, iha, ihb)
     for half in range(2):
-        near_list(half, lists, coefs, inter, src, acc)
+        long_list(half, lists, coefs, inter, src, acc)
+
+
+def early_kernel(lists, coefs, inter, xh, acc_in, acc):
+    del acc_in
+    long_list(4, lists, coefs, inter, xh, acc)
 
 
 def last_kernel(lists, coefs, inter, xh, recip, amps, sq1, acc_in, out, sums, acc, buf, sem):
     del acc_in
     total = jnp.zeros((8, 128), F32)
     copies = []
-    slots = slots_of(0, 8)
     refs = (lists, coefs, inter, xh, acc)
-    for half in range(2):
-        across_list_tail(2 + half, *refs)
-    for half in range(2):
-        step((2 + half) * CAP, SHORT, *refs)
-        for q in range(4 * half, 4 * half + 4):
-            p = slots[q]
-            res = lists[LIVE + p].astype(F32) * acc[q]
-            total = total + squares(res)
-            buf[q] = amps[q] - res * recip[q]
-            copies.append(pltpu.make_async_copy(buf.at[q], out.at[p], sem.at[q]))
-            copies[-1].start()
+    across_list_tail(5, *refs)
+    step(5 * CAP, SHORT, *refs)
+    for q, p in enumerate(slots_of(0, 8)):
+        res = lists[LIVE + p].astype(F32) * acc[q]
+        total = total + squares(res)
+        buf[q] = amps[q] - res * recip[q]
+        copies.append(pltpu.make_async_copy(buf.at[q], out.at[p], sem.at[q]))
+        copies[-1].start()
     rows = (sums.shape[0], 128)
     sums[:, :128] = jnp.broadcast_to(jnp.sum(sq1[...], axis=0, keepdims=True), rows)
     sums[:, 128:] = jnp.broadcast_to(jnp.sum(total, axis=0, keepdims=True), rows)
@@ -296,7 +310,7 @@
                    pltpu.SMEM((LIVE + 8,), jnp.int32), pltpu.SMEM((GAP + 8,), F32), slabs],
         in_specs=[AN] * 9, out_specs=[VM] * 4 + [SM] * 2 + [VM],
         scratch_shapes=per_pair + [pltpu.SMEM((8, 8), F32)] + [pltpu.SMEM((8, 8), jnp.int32)] * 2
-        + [pltpu.SMEM((24,), jnp.int32), pltpu.SMEM((4,), jnp.int32), dma((8,)), dma((6,)), dma((4,))],
+        + [pltpu.SMEM((24,), jnp.int32), pltpu.SMEM((LISTS,), jnp.int32), dma((8,)), dma((6,)), dma((4,))],
         compiler_params=params(8), cost_estimate=COST, name="second",
     )(*big, intersection, x0)
 
@@ -312,28 +326,34 @@
         compiler_params=params(8), cost_estimate=COST, name="near1",
     )(*meta, intersection, exch, energy, vmem(x0), vmem(i0a), vmem(i0b), *swap(i0a, i0b), vmem(inter))
     inter = vmem(inter)
-    x1, acc, amps = pl.pallas_call(
-        across_kernel, out_shape=[tiles4, tiles8, tiles8],
-        in_specs=[SM] * 2 + [VM] * 5, out_specs=[VM] * 3, input_output_aliases={5: 1, 6: 2},
+    early, late = pltpu.VMEM((EARLY, v, v), BF16), pltpu.VMEM((4 - EARLY, v, v), BF16)
+    x1a, x1b, acc, amps = pl.pallas_call(
+        across_kernel, out_shape=[early, late, tiles8, tiles8],
+        in_specs=[SM] * 2 + [VM] * 5, out_specs=[VM] * 4, input_output_aliases={5: 2, 6: 3},
         compiler_params=params(8), cost_estimate=COST, name="across",
     )(*meta, inter, vmem(xh), vmem(recip), vmem(acc), vmem(amps))
-    xh1 = lax.ppermute(x1, "row", other_chip)
+    xh1a = lax.ppermute(x1a, "row", other_chip)
+    xh1b = lax.ppermute(x1b, "row", other_chip)
     i1a, i1b, acc, amps, recip = pl.pallas_call(
         rest_kernel, out_shape=[tiles2, tiles2] + [tiles8] * 3,
         in_specs=[SM] * 2 + [VM] * 8, out_specs=[VM] * 5, input_output_aliases={7: 2, 8: 3, 9: 4},
         compiler_params=params(8), cost_estimate=COST, name="rest",
     )(*meta, inter, exch, energy, vmem(src), vmem(xh), vmem(acc), vmem(amps), vmem(recip))
     acc, sq = pl.pallas_call(
-        near_kernel_2, out_shape=[tiles8, pltpu.VMEM((8, 128), F32)], in_specs=[SM] * 2 + [VM] * 10, out_specs=[VM] * 2,
-        scratch_shapes=[gathered], input_output_aliases={11: 0},
+        near_kernel_2, out_shape=[tiles8, pltpu.VMEM((8, 128), F32)], in_specs=[SM] * 2 + [VM] * 11, out_specs=[VM] * 2,
+        scratch_shapes=[gathered], input_output_aliases={12: 0},
         compiler_params=params(8), cost_estimate=COST, name="near2",
-    )(*meta, inter, exch, energy, vmem(x1), vmem(i1a), vmem(i1b), *swap(i1a, i1b), vmem(amps), vmem(acc))
+    )(*meta, inter, exch, energy, vmem(x1a), vmem(x1b), vmem(i1a), vmem(i1b), *swap(i1a, i1b), vmem(amps), vmem(acc))
+    acc = pl.pallas_call(
+        early_kernel, out_shape=tiles8, in_specs=[SM] * 2 + [VM] * 3, out_specs=VM, input_output_aliases={4: 0},
+        compiler_params=params(8), cost_estimate=COST, name="early",
+    )(*meta, inter, vmem(xh1a), vmem(acc))
     out, sums, _ = pl.pallas_call(
         last_kernel, out_shape=[jax.ShapeDtypeStruct((8, v, v), F32), pltpu.VMEM((count, 256), F32), tiles8],
         in_specs=[SM] * 2 + [VM] * 6, out_specs=[AN, VM, VM], input_output_aliases={7: 2},
         scratch_shapes=[pltpu.VMEM((8, v, v), F32), dma((8,))],
         compiler_params=params(8), cost_estimate=COST, name="last",
-    )(*meta, inter, vmem(xh1), vmem(recip), vmem(amps), vmem(sq), vmem(acc))
+    )(*meta, inter, vmem(xh1b), vmem(recip), vmem(amps), vmem(sq), vmem(acc))
     sums = lax.all_to_all(sums, "row", 0, 0, tiled=True)
     norms = jnp.sqrt(jnp.sum(sums.reshape(count, 2, 128), axis=(0, 2)) / (amp_exch.shape[0] * count * v * v))
     return out, norms

time: 48.3 us -> 48.8 us (1.010)
  Pallas kernels: 17.6 us -> 16.6 us
  starting transfers between devices: 12.5 us -> 13.4 us
  blocking collectives: 13.6 us -> 14.3 us
  waiting for transfers between devices: 2.92 us -> 2.26 us
    pallas_call x1, Pallas kernels: 3.65 us -> 2.54 us  [on_device(): pl.pallas_call(near_kernel_2, out_shape=[tiles8, pltpu.VMEM((8, 128), F32...]
    pallas_call x1 -> x2, Pallas kernels: 1.02 us -> 1.88 us  [the longest x1 1.03 us: on_device(): pl.pallas_call(across_kernel, out_shape=[early, late, tiles8, tiles8], in...]
    all_to_all x1, blocking collectives: 13.6 us -> 14.3 us  [on_device(): sums = lax.all_to_all(sums, 'row', 0, 0, tiled=True)]
    ppermute x4, waiting for transfers between devices: 2.91 us -> 2.25 us  [swap(): return [vmem(lax.ppermute(h, 'row', same_chip)) for h in halves]]
    ppermute x1 -> x2, starting transfers between devices: 0.69 us -> 1.34 us  [the longest x1 0.69 us: on_device(): xh1a = lax.ppermute(x1a, 'row', other_chip)]
    pallas_call x1, Pallas kernels: 3.09 us -> 2.53 us  [on_device(): pl.pallas_call(rest_kernel, out_shape=[tiles2, tiles2] + [tiles8] * 3, in...]
  transfers between devices with their start and end apart: 6 -> 7, of which waited for: 4 -> 4; matrix products, arithmetic and copies ran while one was open for 0% -> 0% of each run, Pallas kernels for 25% -> 24%
where the time goes in v6:
time: 48.8 us; the launch traced here: 48 us
  Pallas kernels  16.6 us (34%)
  blocking collectives  14.3 us (29%)
  starting transfers between devices  13.4 us (27%)
  waiting for transfers between devices  2.26 us (5%)
  between operations  0.75 us (2%)
  other arithmetic  0.68 us (1%)
    all_to_all x1, blocking collectives, on_device(): sums = lax.all_to_all(sums, 'row', 0, 0, tiled=True)  14.3 us
    ppermute x4, starting transfers between devices, swap(): return [vmem(lax.ppermute(h, 'row', same_chip)) for h in halves]  11.4 us
    pallas_call x1, Pallas kernels, on_device(): pl.pallas_call(second_kernel, out_shape=[tiles2, tiles2, pltpu.VMEM((8, v...  3.09 us
    pallas_call x1, Pallas kernels, on_device(): pl.pallas_call(near_kernel_1, out_shape=[tiles8] * 3 + [gathered, slabs],...  2.58 us
    pallas_call x1, Pallas kernels, on_device(): pl.pallas_call(last_kernel, out_shape=[jax.ShapeDtypeStruct((8, v, v), F3...  2.56 us
    pallas_call x1, Pallas kernels, on_device(): pl.pallas_call(near_kernel_2, out_shape=[tiles8, pltpu.VMEM((8, 128), F32...  2.54 us
    pallas_call x1, Pallas kernels, on_device(): pl.pallas_call(rest_kernel, out_shape=[tiles2, tiles2] + [tiles8] * 3, in...  2.53 us
    ppermute x4, waiting for transfers between devices, swap(): return [vmem(lax.ppermute(h, 'row', same_chip)) for h in halves]  2.25 us
  transfers between devices with their start and end apart: 7, of which 4 were waited for; matrix products, arithmetic and copies ran while one was open for 0% of the time, Pallas kernels for 24%

profile of v6, /device:TPU:0, one launch (start us, length us, event | category | flops | bytes accessed | tf_op | source)
XLA Modules:
  0.0 48.0 jit_solution(3086430872883412476)
XLA Ops:
  0.6 1.4 %first.1.x = bf16[4,256,256]{2,1,0:T(8,128)(2,1)S(1)} custom-call(bf16[8,256,256]{2,1,0:T(8,128)(2,1)} %exch.3, f32[8,256]{1,0:T(8,128)} %energy.3, f32[8]{0:T(128)} %gap.3, s32[8]{0:T(128)} %live.3), custom_call_target="tpu_custom_call" | custom-call | flops 1000 | bytes 1000 | tf_op jit(solution)/shard_map/first/pallas_call | solution.py:301
  2.1 0.7 %collective-permute-start.2 = (bf16[4,256,256]{2,1,0:T(8,128)(2,1)S(1)}, bf16[4,256,256]{2,1,0:T(8,128)(2,1)S(1)}, u32[]{:S(2)}, u32[]{:S(2)}) collective-permute-start(bf16[4,256,256]{2,1,0:T(8,128)(2,1)S(1)} %first.1.x), channel_id=1, source_target_pairs={{1,2},{3,4},{5,6},{7,8},{9,10},{11,12},{13,14},{2,1},{4,3},{6,5},{... | collective-permute-start | bytes 1572872 | tf_op jit(solution)/shard_map/ppermute | solution.py:306
  2.8 3.1 %second.1 = (bf16[2,256,256]{2,1,0:T(8,128)(2,1)S(1)}, bf16[2,256,256]{2,1,0:T(8,128)(2,1)S(1)}, bf16[8,256,256]{2,1,0:T(8,128)(2,1)S(1)}, f32[8,256]{1,0:T(8,12...) custom-call(bf16[8,256,256]{2,1,0:T(8,128)(2,1)} %exch.3, f32[8,256]{1,0:T(8,128)} %energy.3, ...), custom_call_target="tpu_custom_call" | custom-call | flops 1000 | bytes 1000 | tf_op jit(solution)/shard_map/second/pallas_call | solution.py:307
  5.9 4.4 %collective-permute-start = (bf16[2,256,256]{2,1,0:T(8,128)(2,1)S(1)}, bf16[2,256,256]{2,1,0:T(8,128)(2,1)S(1)}, u32[]{:S(2)}, u32[]{:S(2)}) collective-permute-start(bf16[2,256,256]{2,1,0:T(8,128)(2,1)S(1)} %get-tuple-element.31.ia), channel_id=1, source_target_pairs={{0,1},{1,0},{2,3},{3,2},{4,5},{5,4},{6,7},{7,6},{8,9},{9,8},{10,11... | collective-permute-start | bytes 786440 | tf_op jit(solution)/shard_map/ppermute | solution.py:318
  10.2 0.1 collective-permute-start.1
  10.3 1.1 %collective-permute-done.iha = bf16[2,256,256]{2,1,0:T(8,128)(2,1)S(1)} collective-permute-done((bf16[2,256,256]{2,1,0:T(8,128)(2,1)S(1)}, bf16[2,256,256]{2,1,0:T(8,128)(2,1)S(1)}, u32[]{:S(2)}, u32[]{:S(2)}) %collective-permute-start) | collective-permute-done | bytes 262176 | tf_op jit(solution)/shard_map/ppermute | solution.py:318
  11.4 0.4 collective-permute-done.1.ihb
  11.8 2.6 %near1.1 = (f32[8,256,256]{2,1,0:T(8,128)S(1)}, f32[8,256,256]{2,1,0:T(8,128)S(1)}, f32[8,256,256]{2,1,0:T(8,128)S(1)}, bf16[12,256,256]{2,1,0:T(8,128)(2,1)S(1)}, bf16[8,8,256,256]{3,2,1,0:T(8,128)(2,1)S(1)}) custom-call(s32[575]{0:T(1024)S(4)} %get-tuple-element.27.lists, f32[568]{0:T(1024)S(4)} %get-tuple-element.28.coefs, ...), custom_call_target="tpu_custom_call", output_to_operand_aliasing={{4}: (10, {})} | custom-call | flops 1000 | bytes 1000 | tf_op jit(solution)/shard_map/near1/pallas_call | solution.py:323
  14.4 0.0 collective-permute-done.2.xh
  14.4 1.0 %across.1 = (bf16[3,256,256]{2,1,0:T(8,128)(2,1)S(1)}, bf16[1,256,256]{2,1,0:T(8,128)(2,1)S(1)}, f32[8,256,256]{2,1,0:T(8,128)S(1)}, f32[8,256,256]{2,1,0:T(8,128)S(1)}) custom-call(s32[575]{0:T(1024)S(4)} %get-tuple-element.27.lists, f32[568]{0:T(1024)S(4)} %get-tuple-element.28.coefs, ...), custom_call_target="tpu_custom_call", output_to_operand_aliasing={{2}: (5, {}), {3}: (6, {})} | custom-call | flops 1000 | bytes 1000 | tf_op jit(solution)/shard_map/across/pallas_call | solution.py:330
  15.4 0.7 %collective-permute-start.6 = (bf16[3,256,256]{2,1,0:T(8,128)(2,1)S(1)}, bf16[3,256,256]{2,1,0:T(8,128)(2,1)S(1)}, u32[]{:S(2)}, u32[]{:S(2)}) collective-permute-start(bf16[3,256,256]{2,1,0:T(8,128)(2,1)S(1)} %get-tuple-element.44.xa), channel_id=1, source_target_pairs={{1,2},{3,4},{5,6},{7,8},{9,10},{11,12},{13,14},{2,1},{4,3},{6,5},{... | collective-permute-start | bytes 1179656 | tf_op jit(solution)/shard_map/ppermute | solution.py:335
  16.1 2.5 %rest.1 = (bf16[2,256,256]{2,1,0:T(8,128)(2,1)S(1)}, bf16[2,256,256]{2,1,0:T(8,128)(2,1)S(1)}, f32[8,256,256]{2,1,0:T(8,128)S(1)}, f32[8,256,256]{2,1,0:T(8,128)S(1)}, f32[8,256,256]{2,1,0:T(8,128)S(1)}) custom-call(s32[575]{0:T(1024)S(4)} %get-tuple-element.27.lists, ...), custom_call_target="tpu_custom_call", output_to_operand_aliasing={{2}: (7, {}), {3}: (8, {}), {4}: (9, {})} | custom-call | flops 1000 | bytes 1000 | tf_op jit(solution)/shard_map/rest/pallas_call | solution.py:337
  18.6 6.9 %collective-permute-start.4 = (bf16[2,256,256]{2,1,0:T(8,128)(2,1)S(1)}, bf16[2,256,256]{2,1,0:T(8,128)(2,1)S(1)}, u32[]{:S(2)}, u32[]{:S(2)}) collective-permute-start(bf16[2,256,256]{2,1,0:T(8,128)(2,1)S(1)} %get-tuple-element.45.ia), channel_id=1, source_target_pairs={{0,1},{1,0},{2,3},{3,2},{4,5},{5,4},{6,7},{7,6},{8,9},{9,8},{10,11... | collective-permute-start | bytes 786440 | tf_op jit(solution)/shard_map/ppermute | solution.py:318
  25.5 0.1 collective-permute-start.5
  25.6 0.7 %collective-permute-start.3 = (bf16[1,256,256]{2,1,0:T(8,128)(2,1)S(1)}, bf16[1,256,256]{2,1,0:T(8,128)(2,1)S(1)}, u32[]{:S(2)}, u32[]{:S(2)}) collective-permute-start(bf16[1,256,256]{2,1,0:T(8,128)(2,1)S(1)} %get-tuple-element.38.xb), channel_id=1, source_target_pairs={{1,2},{3,4},{5,6},{7,8},{9,10},{11,12},{13,14},{2,1},{4,3},{6,5},{... | collective-permute-start | bytes 393224 | tf_op jit(solution)/shard_map/ppermute | solution.py:336
  26.2 0.4 collective-permute-done.4.iha
  26.7 0.4 collective-permute-done.5.ihb
  27.0 2.5 %near2.1 = (f32[8,256,256]{2,1,0:T(8,128)S(1)}, f32[8,128]{1,0:T(8,128)S(1)}) custom-call(s32[575]{0:T(1024)S(4)} %get-tuple-element.27.lists, f32[568]{0:T(1024)S(4)} %get-tuple-element.28.coefs, bf16[8,8,256,256]{3,2,1,0:T(8,128)(2,1)S(1)} %get-tuple-element.34.inter, ...), custom_call_target="tpu_custom_call", output_to_operand_aliasing={{0}: (12, {})} | custom-call | flops 1000 | bytes 1000 | tf_op jit(solution)/shard_map/near2/pallas_call | solution.py:342
  29.6 0.0 collective-permute-done.6.xh
  29.6 0.9 %early.1.acc_in = f32[8,256,256]{2,1,0:T(8,128)S(1)} custom-call(s32[575]{0:T(1024)S(4)} %get-tuple-element.27.lists, f32[568]{0:T(1024)S(4)} %get-tuple-element.28.coefs, bf16[8,8,256,256]{3,2,1,0:T(8,128)(2,1)S(1)} %get-tuple-element.34.inter, bf16[3,256,256]{2,1,0:T(8,128)(2,1)S(1)} %collective-permute-done.6.xh, ...), custom_call_target="tpu_custom_call", output_to_operand_aliasing={{}: (4, {})} | custom-call | flops 1000 | bytes 1000 | tf_op jit(solution)/shard_map/early/pallas_call | solution.py:347
  30.4 0.0 collective-permute-done.3.xh
  30.5 2.6 %last.1 = (f32[8,256,256]{2,1,0:T(8,128)}, f32[16,256]{1,0:T(8,128)S(1)}, f32[8,256,256]{2,1,0:T(8,128)S(1)}) custom-call(s32[575]{0:T(1024)S(4)} %get-tuple-element.27.lists, f32[568]{0:T(1024)S(4)} %get-tuple-element.28.coefs, bf16[8,8,256,256]{3,2,1,0:T(8,128)(2,1)S(1)} %get-tuple-element.34.inter, ...), custom_call_target="tpu_custom_call", output_to_operand_aliasing={{2}: (7, {})} | custom-call | flops 1000 | bytes 1000 | tf_op jit(solution)/shard_map/last/pallas_call | solution.py:351
  33.0 14.3 %all_to_all.9 = f32[16,1,256]{2,1,0:T(1,128)S(1)} all-to-all(f32[16,1,256]{2,1,0:T(1,128)S(1)} %copy.20), channel_id=1, replica_groups=mesh['grp'=2,'row'=16] {'row'}, dimensions={0} | all-to-all | bytes 32768 | tf_op jit(solution)/shard_map/all_to_all | solution.py:357
  47.4 0.1 bitcast_reduce_fusion
  47.5 0.5 %multiply_sqrt_fusion = f32[2]{0:T(128)} fusion(f32[2]{0:T(128)S(1)} %bitcast_reduce_fusion), kind=kLoop, calls=%fused_computation.1 | loop fusion | flops 2 | bytes 16 | tf_op jit(solution)/shard_map/sqrt | solution.py:358
  (2 shorter events, 0.1 us)
Async XLA Ops:
  2.1 12.3 %collective-permute-start.2 = (bf16[4,256,256]{2,1,0:T(8,128)(2,1)S(1)}, bf16[4,256,256]{2,1,0:T(8,128)(2,1)S(1)}, u32[]{:S(2)}, u32[]{:S(2)}) collective-permute-start(bf16[4,256,256]{2,1,0:T(8,128)(2,1)S(1)} %first.1.x), channel_id=1, source_target_pairs={{1,2},{3,4},{5,6},{7,8},{9,10},{11,12},{13,14},{2,1},{4,3},{6,5},{... | collective-permute-start | bytes 1572872 | tf_op jit(solution)/shard_map/ppermute | solution.py:306
  5.9 5.5 %collective-permute-start = (bf16[2,256,256]{2,1,0:T(8,128)(2,1)S(1)}, bf16[2,256,256]{2,1,0:T(8,128)(2,1)S(1)}, u32[]{:S(2)}, u32[]{:S(2)}) collective-permute-start(bf16[2,256,256]{2,1,0:T(8,128)(2,1)S(1)} %get-tuple-element.31.ia), channel_id=1, source_target_pairs={{0,1},{1,0},{2,3},{3,2},{4,5},{5,4},{6,7},{7,6},{8,9},{9,8},{10,11... | collective-permute-start | bytes 786440 | tf_op jit(solution)/shard_map/ppermute | solution.py:318
  10.2 1.5 %collective-permute-start.1 = (bf16[2,256,256]{2,1,0:T(8,128)(2,1)S(1)}, bf16[2,256,256]{2,1,0:T(8,128)(2,1)S(1)}, u32[]{:S(2)}, u32[]{:S(2)}) collective-permute-start(bf16[2,256,256]{2,1,0:T(8,128)(2,1)S(1)} %get-tuple-element.32.ib), channel_id=1, source_target_pairs={{0,1},{1,0},{2,3},{3,2},{4,5},{5,4},{6,7},{7,6},{8,9},{9,8},{10,11... | collective-permute-start | bytes 786440 | tf_op jit(solution)/shard_map/ppermute | solution.py:318
  15.4 14.2 %collective-permute-start.6 = (bf16[3,256,256]{2,1,0:T(8,128)(2,1)S(1)}, bf16[3,256,256]{2,1,0:T(8,128)(2,1)S(1)}, u32[]{:S(2)}, u32[]{:S(2)}) collective-permute-start(bf16[3,256,256]{2,1,0:T(8,128)(2,1)S(1)} %get-tuple-element.44.xa), channel_id=1, source_target_pairs={{1,2},{3,4},{5,6},{7,8},{9,10},{11,12},{13,14},{2,1},{4,3},{6,5},{... | collective-permute-start | bytes 1179656 | tf_op jit(solution)/shard_map/ppermute | solution.py:335
  18.6 8.0 %collective-permute-start.4 = (bf16[2,256,256]{2,1,0:T(8,128)(2,1)S(1)}, bf16[2,256,256]{2,1,0:T(8,128)(2,1)S(1)}, u32[]{:S(2)}, u32[]{:S(2)}) collective-permute-start(bf16[2,256,256]{2,1,0:T(8,128)(2,1)S(1)} %get-tuple-element.45.ia), channel_id=1, source_target_pairs={{0,1},{1,0},{2,3},{3,2},{4,5},{5,4},{6,7},{7,6},{8,9},{9,8},{10,11... | collective-permute-start | bytes 786440 | tf_op jit(solution)/shard_map/ppermute | solution.py:318
  25.5 1.5 %collective-permute-start.5 = (bf16[2,256,256]{2,1,0:T(8,128)(2,1)S(1)}, bf16[2,256,256]{2,1,0:T(8,128)(2,1)S(1)}, u32[]{:S(2)}, u32[]{:S(2)}) collective-permute-start(bf16[2,256,256]{2,1,0:T(8,128)(2,1)S(1)} %get-tuple-element.46.ib), channel_id=1, source_target_pairs={{0,1},{1,0},{2,3},{3,2},{4,5},{5,4},{6,7},{7,6},{8,9},{9,8},{10,11... | collective-permute-start | bytes 786440 | tf_op jit(solution)/shard_map/ppermute | solution.py:318
  25.6 4.9 %collective-permute-start.3 = (bf16[1,256,256]{2,1,0:T(8,128)(2,1)S(1)}, bf16[1,256,256]{2,1,0:T(8,128)(2,1)S(1)}, u32[]{:S(2)}, u32[]{:S(2)}) collective-permute-start(bf16[1,256,256]{2,1,0:T(8,128)(2,1)S(1)} %get-tuple-element.38.xb), channel_id=1, source_target_pairs={{1,2},{3,4},{5,6},{7,8},{9,10},{11,12},{13,14},{2,1},{4,3},{6,5},{... | collective-permute-start | bytes 393224 | tf_op jit(solution)/shard_map/ppermute | solution.py:336

commit v7 on v6

--- a/solution.py
+++ b/solution.py
@@ -13,8 +13,8 @@
 SM = pl.BlockSpec(memory_space=pltpu.SMEM)
 AN = pl.BlockSpec(memory_space=pl.ANY)
 CAP = 80
-LONG, SHORT = 16, 8
-LISTS = 7
+LONG, SHORT, FEW = 16, 8, 4
+LOCAL, NEAR, ACROSS, FIRST_PART, SECOND_PART, LISTS = 0, 2, 4, 6, 7, 10
 COUNTS, LIVE = LISTS * CAP, LISTS * CAP + LISTS
 GAP = LISTS * CAP
 EARLY = 3
@@ -94,8 +94,8 @@
             out_b[i - 2] = tile
 
     for s in range(4):
-        table[4 + s] = jnp.where(base == 0, (s << 9) | 3, ((8 + s) << 9) | 1)
-        table[16 + s] = jnp.where(base == 0, ((8 + s) << 9) | 1, (s << 9) | 3)
+        table[4 + s] = (s << 9) | 1 | jnp.where(base == 0, ACROSS, NEAR) << 1
+        table[16 + s] = (s << 9) | 1 | jnp.where(base == 0, NEAR, ACROSS) << 1
     for s in range(8):
         table[8 + s] = (((s + base) & 7) << 9) | lv[s]
     for k in range(LISTS):
@@ -105,19 +105,16 @@
         q, n = i >> 3, i & 7
         p = (q + base) & 7
         what = table[ns[p, n]]
-        which = (what & 2) + (q >> 2)
-        pos = ends[which]
-        lists[pos] = ((what >> 9) << 9) | (q << 6) | (p << 3) | n
-        coefs[pos] = fk[p, n]
+        kind, half, s = (what >> 1) & 7, q >> 2, what >> 9
+        late = s >= EARLY
+        again = jnp.where(kind == ACROSS, jnp.where(late, SECOND_PART + half, FIRST_PART), LISTS - 1)
+        low = (q << 6) | (p << 3) | n
         one = nl[p, n] & lv[p] & what & 1
-        ends[which] = pos + one
-        s = what >> 9
-        late = s >= EARLY
-        which = jnp.where((what & 2) != 0, jnp.where(late, 5, 4), 6)
-        pos = ends[which]
-        lists[pos] = (jnp.where(late, s - EARLY, s) << 9) | (q << 6) | (p << 3) | n
-        coefs[pos] = fk[p, n]
-        ends[which] = pos + one
+        for which, place in ((kind + half, s), (again, jnp.where(late, s - EARLY, s))):
+            pos = ends[which]
+            lists[pos] = (place << 9) | low
+            coefs[pos] = fk[p, n]
+            ends[which] = pos + one
         return 0
 
     lax.fori_loop(0, 64, entry, 0, unroll=4)
@@ -160,20 +157,16 @@
     steps(at + longs * LONG, left // SHORT, SHORT, lists, *refs)
 
 
-def across_list_tail(which, lists, *refs):
-    more = jnp.maximum(lists[COUNTS + which] - 1, 0) // SHORT
-    steps(which * CAP + SHORT, more, SHORT, lists, *refs)
-
-
-def gather(src, xs, ia, ib, iha, ihb):
+def list_tail(which, size, lists, *refs):
+    more = jnp.maximum(lists[COUNTS + which] - 1, 0) // size
+    steps(which * CAP + size, more, size, lists, *refs)
+
+
+def gather(src, *parts):
     at = 0
-    for x in xs:
+    for x in parts:
         src[at : at + x.shape[0]] = x[...]
         at += x.shape[0]
-    src[4:6] = ia[...]
-    src[6:8] = ib[...]
-    src[8:10] = iha[...]
-    src[10:12] = ihb[...]
 
 
 def start_half(half, lists, coefs, exch, energy, acc, amps, recip):
@@ -202,40 +195,51 @@
     return ((lax.axis_index("row") + 1) & 2) != 0
 
 
-def near_kernel_1(lists, coefs, inter_hbm, exch, energy, x, ia, ib, iha, ihb, inter_in, acc, amps, recip, src, inter, sem):
+def local_kernel_1(lists, coefs, inter_hbm, exch, energy, x, ia, ib, inter_in, acc, amps, recip, src, inter, sem):
     del inter_in
     slabs = start_all([(inter_hbm.at[p], inter.at[p]) for p in slots_of(4, 8)], sem)
-    gather(src, [x], ia, ib, iha, ihb)
+    gather(src, x, ia, ib)
     start_half(0, lists, coefs, exch, energy, acc, amps, recip)
-    long_list(0, lists, coefs, inter, src, acc)
+    long_list(LOCAL, lists, coefs, inter, src, acc)
     for c in slabs:
         c.wait()
 
     @pl.when(waits_longer())
     def _():
         start_half(1, lists, coefs, exch, energy, acc, amps, recip)
-        long_list(1, lists, coefs, inter, src, acc)
+        long_list(LOCAL + 1, lists, coefs, inter, src, acc)
+
+
+def near_kernel_1(lists, coefs, inter, iha, ihb, acc_in, acc, ih):
+    del acc_in
+    gather(ih, iha, ihb)
+    long_list(NEAR, lists, coefs, inter, ih, acc)
+
+    @pl.when(waits_longer())
+    def _():
+        long_list(NEAR + 1, lists, coefs, inter, ih, acc)
 
 
 def across_kernel(lists, coefs, inter, xh, recip, acc_in, amps_in, out_a, out_b, acc, amps):
     del acc_in, amps_in
     refs = (lists, coefs, inter, xh, acc)
-    across_list_tail(2, *refs)
-    step(2 * CAP, SHORT, *refs)
+    list_tail(ACROSS, SHORT, *refs)
+    step(ACROSS * CAP, SHORT, *refs)
     update_half(0, lists, acc, amps, recip, [out_a, out_b])
 
 
-def rest_kernel(lists, coefs, inter, exch, energy, src, xh, acc_in, amps_in, recip_in, out_a, out_b, acc, amps, recip):
+def rest_kernel(lists, coefs, inter, exch, energy, src, ih, xh, acc_in, amps_in, recip_in, out_a, out_b, acc, amps, recip):
     del acc_in, amps_in, recip_in
 
     @pl.when(jnp.logical_not(waits_longer()))
     def _():
         start_half(1, lists, coefs, exch, energy, acc, amps, recip)
-        long_list(1, lists, coefs, inter, src, acc)
+        long_list(LOCAL + 1, lists, coefs, inter, src, acc)
+        long_list(NEAR + 1, lists, coefs, inter, ih, acc)
 
     refs = (lists, coefs, inter, xh, acc)
-    across_list_tail(3, *refs)
-    step(3 * CAP, SHORT, *refs)
+    list_tail(ACROSS + 1, SHORT, *refs)
+    step((ACROSS + 1) * CAP, SHORT, *refs)
     update_half(1, lists, acc, amps, recip, [out_a, out_b])
 
 
@@ -244,7 +248,7 @@
     return s[:, :128] + s[:, 128:]
 
 
-def near_kernel_2(lists, coefs, inter, exch, energy, xa, xb, ia, ib, iha, ihb, amps, acc_in, acc, sq, src):
+def local_kernel_2(lists, coefs, inter, exch, energy, xa, xb, ia, ib, amps, acc_in, acc, sq, src):
     del acc_in
     slots = slots_of(0, 8)
     dens = denominators(energy, [coefs[GAP + p] for p in slots], slots)
@@ -253,14 +257,21 @@
         total = total + squares(lists[LIVE + p].astype(F32) * acc[q])
         acc[q] = exch[p].astype(F32) + dens[q] * amps[q]
     sq[...] = total
-    gather(src, [xa, xb], ia, ib, iha, ihb)
+    gather(src, xa, xb, ia, ib)
     for half in range(2):
-        long_list(half, lists, coefs, inter, src, acc)
+        long_list(LOCAL + half, lists, coefs, inter, src, acc)
+
+
+def near_kernel_2(lists, coefs, inter, iha, ihb, acc_in, acc, ih):
+    del acc_in
+    gather(ih, iha, ihb)
+    for half in range(2):
+        long_list(NEAR + half, lists, coefs, inter, ih, acc)
 
 
 def early_kernel(lists, coefs, inter, xh, acc_in, acc):
     del acc_in
-    long_list(4, lists, coefs, inter, xh, acc)
+    long_list(FIRST_PART, lists, coefs, inter, xh, acc)
 
 
 def last_kernel(lists, coefs, inter, xh, recip, amps, sq1, acc_in, out, sums, acc, buf, sem):
@@ -268,14 +279,18 @@
     total = jnp.zeros((8, 128), F32)
     copies = []
     refs = (lists, coefs, inter, xh, acc)
-    across_list_tail(5, *refs)
-    step(5 * CAP, SHORT, *refs)
-    for q, p in enumerate(slots_of(0, 8)):
-        res = lists[LIVE + p].astype(F32) * acc[q]
-        total = total + squares(res)
-        buf[q] = amps[q] - res * recip[q]
-        copies.append(pltpu.make_async_copy(buf.at[q], out.at[p], sem.at[q]))
-        copies[-1].start()
+    slots = slots_of(0, 8)
+    for half in range(2):
+        list_tail(SECOND_PART + half, FEW, *refs)
+    for half in range(2):
+        step((SECOND_PART + half) * CAP, FEW, *refs)
+        for q in range(4 * half, 4 * half + 4):
+            p = slots[q]
+            res = lists[LIVE + p].astype(F32) * acc[q]
+            total = total + squares(res)
+            buf[q] = amps[q] - res * recip[q]
+            copies.append(pltpu.make_async_copy(buf.at[q], out.at[p], sem.at[q]))
+            copies[-1].start()
     rows = (sums.shape[0], 128)
     sums[:, :128] = jnp.broadcast_to(jnp.sum(sq1[...], axis=0, keepdims=True), rows)
     sums[:, 128:] = jnp.broadcast_to(jnp.sum(total, axis=0, keepdims=True), rows)
@@ -319,13 +334,17 @@
 
     meta = (lists, coefs)
     exch, energy = vmem(exch), vmem(energy)
-    gathered = pltpu.VMEM((12, v, v), BF16)
+    own = pltpu.VMEM((8, v, v), BF16)
     acc, amps, recip, src, inter = pl.pallas_call(
-        near_kernel_1, out_shape=[tiles8] * 3 + [gathered, slabs], in_specs=[SM] * 2 + [AN] + [VM] * 8, out_specs=[VM] * 5,
-        scratch_shapes=[dma((4,))], input_output_aliases={10: 4},
+        local_kernel_1, out_shape=[tiles8] * 3 + [own, slabs], in_specs=[SM] * 2 + [AN] + [VM] * 6, out_specs=[VM] * 5,
+        scratch_shapes=[dma((4,))], input_output_aliases={8: 4},
+        compiler_params=params(8), cost_estimate=COST, name="local1",
+    )(*meta, intersection, exch, energy, vmem(x0), vmem(i0a), vmem(i0b), vmem(inter))
+    inter = vmem(inter)
+    acc, ih = pl.pallas_call(
+        near_kernel_1, out_shape=[tiles8, tiles4], in_specs=[SM] * 2 + [VM] * 4, out_specs=[VM] * 2, input_output_aliases={5: 0},
         compiler_params=params(8), cost_estimate=COST, name="near1",
-    )(*meta, intersection, exch, energy, vmem(x0), vmem(i0a), vmem(i0b), *swap(i0a, i0b), vmem(inter))
-    inter = vmem(inter)
+    )(*meta, inter, *swap(i0a, i0b), vmem(acc))
     early, late = pltpu.VMEM((EARLY, v, v), BF16), pltpu.VMEM((4 - EARLY, v, v), BF16)
     x1a, x1b, acc, amps = pl.pallas_call(
         across_kernel, out_shape=[early, late, tiles8, tiles8],
@@ -336,14 +355,18 @@
     xh1b = lax.ppermute(x1b, "row", other_chip)
     i1a, i1b, acc, amps, recip = pl.pallas_call(
         rest_kernel, out_shape=[tiles2, tiles2] + [tiles8] * 3,
-        in_specs=[SM] * 2 + [VM] * 8, out_specs=[VM] * 5, input_output_aliases={7: 2, 8: 3, 9: 4},
+        in_specs=[SM] * 2 + [VM] * 9, out_specs=[VM] * 5, input_output_aliases={8: 2, 9: 3, 10: 4},
         compiler_params=params(8), cost_estimate=COST, name="rest",
-    )(*meta, inter, exch, energy, vmem(src), vmem(xh), vmem(acc), vmem(amps), vmem(recip))
+    )(*meta, inter, exch, energy, vmem(src), vmem(ih), vmem(xh), vmem(acc), vmem(amps), vmem(recip))
     acc, sq = pl.pallas_call(
-        near_kernel_2, out_shape=[tiles8, pltpu.VMEM((8, 128), F32)], in_specs=[SM] * 2 + [VM] * 11, out_specs=[VM] * 2,
-        scratch_shapes=[gathered], input_output_aliases={12: 0},
-        compiler_params=params(8), cost_estimate=COST, name="near2",
-    )(*meta, inter, exch, energy, vmem(x1a), vmem(x1b), vmem(i1a), vmem(i1b), *swap(i1a, i1b), vmem(amps), vmem(acc))
+        local_kernel_2, out_shape=[tiles8, pltpu.VMEM((8, 128), F32)], in_specs=[SM] * 2 + [VM] * 9, out_specs=[VM] * 2,
+        scratch_shapes=[own], input_output_aliases={10: 0},
+        compiler_params=params(8), cost_estimate=COST, name="local2",
+    )(*meta, inter, exch, energy, vmem(x1a), vmem(x1b), vmem(i1a), vmem(i1b), vmem(amps), vmem(acc))
+    acc = pl.pallas_call(
+        near_kernel_2, out_shape=tiles8, in_specs=[SM] * 2 + [VM] * 4, out_specs=VM, input_output_aliases={5: 0},
+        scratch_shapes=[tiles4], compiler_params=params(8), cost_estimate=COST, name="near2",
+    )(*meta, inter, *swap(i1a, i1b), vmem(acc))
     acc = pl.pallas_call(
         early_kernel, out_shape=tiles8, in_specs=[SM] * 2 + [VM] * 3, out_specs=VM, input_output_aliases={4: 0},
         compiler_params=params(8), cost_estimate=COST, name="early",

time: 48.8 us -> 49.2 us (level); the launches traced: 48 us -> 49.2 us
  Pallas kernels: 16.6 us -> 22.4 us
  waiting for transfers between devices: 2.26 us -> 0.02 us
  blocking collectives: 14.3 us -> 13 us
  starting transfers between devices: 13.4 us -> 12.4 us
    pallas_call x2 -> x4, Pallas kernels: 5.12 us -> 9.07 us  [the longest x1 3.86 us: on_device(): pl.pallas_call(local_kernel_2, out_shape=[tiles8, pltpu.VMEM((8, 128), F3...]
    ppermute x4, waiting for transfers between devices: 2.25 us -> 0.01 us  [swap(): return [vmem(lax.ppermute(h, 'row', same_chip)) for h in halves]]
    all_to_all x1, blocking collectives: 14.3 us -> 13 us  [on_device(): sums = lax.all_to_all(sums, 'row', 0, 0, tiled=True)]
    pallas_call x1, Pallas kernels: 2.53 us -> 3.76 us  [on_device(): pl.pallas_call(rest_kernel, out_shape=[tiles2, tiles2] + [tiles8] * 3, in...]
    ppermute x4, starting transfers between devices: 11.4 us -> 10.3 us  [swap(): return [vmem(lax.ppermute(h, 'row', same_chip)) for h in halves]]
    pallas_call x1, Pallas kernels: 0.85 us -> 1.41 us  [on_device(): pl.pallas_call(early_kernel, out_shape=tiles8, in_specs=[SM] * 2 + [VM] *...]
  transfers between devices with their start and end apart: 7 -> 7, of which waited for: 4 -> 0; matrix products, arithmetic and copies ran while one was open for 0% -> 0% of each run, Pallas kernels for 24% -> 35%
where the time goes in v7:
time: 49.2 us
  Pallas kernels  22.4 us (46%)
  blocking collectives  13 us (26%)
  starting transfers between devices  12.4 us (25%)
  between operations  0.8 us (2%)
  other arithmetic  0.68 us (1%)
    all_to_all x1, blocking collectives, on_device(): sums = lax.all_to_all(sums, 'row', 0, 0, tiled=True)  13 us
    ppermute x4, starting transfers between devices, swap(): return [vmem(lax.ppermute(h, 'row', same_chip)) for h in halves]  10.3 us
    pallas_call x1, Pallas kernels, on_device(): pl.pallas_call(local_kernel_2, out_shape=[tiles8, pltpu.VMEM((8, 128), F3...  3.86 us
    pallas_call x1, Pallas kernels, on_device(): pl.pallas_call(rest_kernel, out_shape=[tiles2, tiles2] + [tiles8] * 3, in...  3.76 us
    pallas_call x1, Pallas kernels, on_device(): pl.pallas_call(second_kernel, out_shape=[tiles2, tiles2, pltpu.VMEM((8, v...  3.09 us
    pallas_call x1, Pallas kernels, on_device(): pl.pallas_call(local_kernel_1, out_shape=[tiles8] * 3 + [own, slabs], in_...  2.58 us
    pallas_call x1, Pallas kernels, on_device(): pl.pallas_call(last_kernel, out_shape=[jax.ShapeDtypeStruct((8, v, v), F3...  2.38 us
    pallas_call x1, Pallas kernels, on_device(): pl.pallas_call(near_kernel_2, out_shape=tiles8, in_specs=[SM] * 2 + [VM]...  1.73 us
  transfers between devices with their start and end apart: 7, of which 0 were waited for; matrix products, arithmetic and copies ran while one was open for 0% of the time, Pallas kernels for 35%

profile of v7, /device:TPU:0, one launch (start us, length us, event | category | flops | bytes accessed | tf_op | source)
XLA Modules:
  0.0 49.2 jit_solution(2811054188795377304)
XLA Ops:
  0.6 1.4 %first.1.x = bf16[4,256,256]{2,1,0:T(8,128)(2,1)S(1)} custom-call(bf16[8,256,256]{2,1,0:T(8,128)(2,1)} %exch.3, f32[8,256]{1,0:T(8,128)} %energy.3, f32[8]{0:T(128)} %gap.3, s32[8]{0:T(128)} %live.3), custom_call_target="tpu_custom_call" | custom-call | flops 1000 | bytes 1000 | tf_op jit(solution)/shard_map/first/pallas_call | solution.py:316
  2.1 0.7 %collective-permute-start = (bf16[4,256,256]{2,1,0:T(8,128)(2,1)S(1)}, bf16[4,256,256]{2,1,0:T(8,128)(2,1)S(1)}, u32[]{:S(2)}, u32[]{:S(2)}) collective-permute-start(bf16[4,256,256]{2,1,0:T(8,128)(2,1)S(1)} %first.1.x), channel_id=1, source_target_pairs={{1,2},{3,4},{5,6},{7,8},{9,10},{11,12},{13,14},{2,1},{4,3},{6,5},{... | collective-permute-start | bytes 1572872 | tf_op jit(solution)/shard_map/ppermute | solution.py:321
  2.8 3.1 %second.1 = (bf16[2,256,256]{2,1,0:T(8,128)(2,1)S(1)}, bf16[2,256,256]{2,1,0:T(8,128)(2,1)S(1)}, bf16[8,256,256]{2,1,0:T(8,128)(2,1)S(1)}, f32[8,256]{1,0:T(8,12...) custom-call(bf16[8,256,256]{2,1,0:T(8,128)(2,1)} %exch.3, f32[8,256]{1,0:T(8,128)} %energy.3, ...), custom_call_target="tpu_custom_call" | custom-call | flops 1000 | bytes 1000 | tf_op jit(solution)/shard_map/second/pallas_call | solution.py:322
  5.9 4.4 %collective-permute-start.1 = (bf16[2,256,256]{2,1,0:T(8,128)(2,1)S(1)}, bf16[2,256,256]{2,1,0:T(8,128)(2,1)S(1)}, u32[]{:S(2)}, u32[]{:S(2)}) collective-permute-start(bf16[2,256,256]{2,1,0:T(8,128)(2,1)S(1)} %get-tuple-element.33.ia), channel_id=1, source_target_pairs={{0,1},{1,0},{2,3},{3,2},{4,5},{5,4},{6,7},{7,6},{8,9},{9,8},{10,11... | collective-permute-start | bytes 786440 | tf_op jit(solution)/shard_map/ppermute | solution.py:333
  10.2 0.1 collective-permute-start.2
  10.3 2.6 %local1.1 = (f32[8,256,256]{2,1,0:T(8,128)S(1)}, f32[8,256,256]{2,1,0:T(8,128)S(1)}, f32[8,256,256]{2,1,0:T(8,128)S(1)}, bf16[8,256,256]{2,1,0:T(8,128)(2,1)S(1)}, bf16[8,8,256,256]{3,2,1,0:T(8,128)(2,1)S(1)}) custom-call(s32[818]{0:T(1024)S(4)} %get-tuple-element.29.lists, f32[808]{0:T(1024)S(4)} %get-tuple-element.30.coefs, ...), custom_call_target="tpu_custom_call", output_to_operand_aliasing={{4}: (8, {})} | custom-call | flops 1000 | bytes 1000 | tf_op jit(solution)/shard_map/local1/pallas_call | solution.py:338
  12.9 0.0 collective-permute-done.1.iha
  12.9 0.0 collective-permute-done.2.ihb
  12.9 0.9 %near1.1 = (f32[8,256,256]{2,1,0:T(8,128)S(1)}, bf16[4,256,256]{2,1,0:T(8,128)(2,1)S(1)}) custom-call(s32[818]{0:T(1024)S(4)} %get-tuple-element.29.lists, f32[808]{0:T(1024)S(4)} %get-tuple-element.30.coefs, bf16[8,8,256,256]{3,2,1,0:T(8,128)(2,1)S(1)} %get-tuple-element.36.inter, ...), custom_call_target="tpu_custom_call", output_to_operand_aliasing={{0}: (5, {})} | custom-call | flops 1000 | bytes 1000 | tf_op jit(solution)/shard_map/near1/pallas_call | solution.py:344
  13.8 0.0 collective-permute-done.xh
  13.8 1.2 %across.1 = (bf16[3,256,256]{2,1,0:T(8,128)(2,1)S(1)}, bf16[1,256,256]{2,1,0:T(8,128)(2,1)S(1)}, f32[8,256,256]{2,1,0:T(8,128)S(1)}, f32[8,256,256]{2,1,0:T(8,128)S(1)}) custom-call(s32[818]{0:T(1024)S(4)} %get-tuple-element.29.lists, f32[808]{0:T(1024)S(4)} %get-tuple-element.30.coefs, ...), custom_call_target="tpu_custom_call", output_to_operand_aliasing={{2}: (5, {}), {3}: (6, {})} | custom-call | flops 1000 | bytes 1000 | tf_op jit(solution)/shard_map/across/pallas_call | solution.py:349
  15.0 0.7 %collective-permute-start.4 = (bf16[3,256,256]{2,1,0:T(8,128)(2,1)S(1)}, bf16[3,256,256]{2,1,0:T(8,128)(2,1)S(1)}, u32[]{:S(2)}, u32[]{:S(2)}) collective-permute-start(bf16[3,256,256]{2,1,0:T(8,128)(2,1)S(1)} %get-tuple-element.48.xa), channel_id=1, source_target_pairs={{1,2},{3,4},{5,6},{7,8},{9,10},{11,12},{13,14},{2,1},{4,3},{6,5},{... | collective-permute-start | bytes 1179656 | tf_op jit(solution)/shard_map/ppermute | solution.py:354
  15.7 3.8 %rest.1 = (bf16[2,256,256]{2,1,0:T(8,128)(2,1)S(1)}, bf16[2,256,256]{2,1,0:T(8,128)(2,1)S(1)}, f32[8,256,256]{2,1,0:T(8,128)S(1)}, f32[8,256,256]{2,1,0:T(8,128)S(1)}, f32[8,256,256]{2,1,0:T(8,128)S(1)}) custom-call(s32[818]{0:T(1024)S(4)} %get-tuple-element.29.lists, ...), custom_call_target="tpu_custom_call", output_to_operand_aliasing={{2}: (8, {}), {3}: (9, {}), {4}: (10, {})} | custom-call | flops 1000 | bytes 1000 | tf_op jit(solution)/shard_map/rest/pallas_call | solution.py:356
  19.5 5.8 %collective-permute-start.5 = (bf16[2,256,256]{2,1,0:T(8,128)(2,1)S(1)}, bf16[2,256,256]{2,1,0:T(8,128)(2,1)S(1)}, u32[]{:S(2)}, u32[]{:S(2)}) collective-permute-start(bf16[2,256,256]{2,1,0:T(8,128)(2,1)S(1)} %get-tuple-element.49.ia), channel_id=1, source_target_pairs={{0,1},{1,0},{2,3},{3,2},{4,5},{5,4},{6,7},{7,6},{8,9},{9,8},{10,11... | collective-permute-start | bytes 786440 | tf_op jit(solution)/shard_map/ppermute | solution.py:333
  25.3 0.1 collective-permute-start.6
  25.4 0.7 %collective-permute-start.3 = (bf16[1,256,256]{2,1,0:T(8,128)(2,1)S(1)}, bf16[1,256,256]{2,1,0:T(8,128)(2,1)S(1)}, u32[]{:S(2)}, u32[]{:S(2)}) collective-permute-start(bf16[1,256,256]{2,1,0:T(8,128)(2,1)S(1)} %get-tuple-element.41.xb), channel_id=1, source_target_pairs={{1,2},{3,4},{5,6},{7,8},{9,10},{11,12},{13,14},{2,1},{4,3},{6,5},{... | collective-permute-start | bytes 393224 | tf_op jit(solution)/shard_map/ppermute | solution.py:355
  26.1 3.9 %local2.1 = (f32[8,256,256]{2,1,0:T(8,128)S(1)}, f32[8,128]{1,0:T(8,128)S(1)}) custom-call(s32[818]{0:T(1024)S(4)} %get-tuple-element.29.lists, f32[808]{0:T(1024)S(4)} %get-tuple-element.30.coefs, bf16[8,8,256,256]{3,2,1,0:T(8,128)(2,1)S(1)} %get-tuple-element.36.inter, ...), custom_call_target="tpu_custom_call", output_to_operand_aliasing={{0}: (10, {})} | custom-call | flops 1000 | bytes 1000 | tf_op jit(solution)/shard_map/local2/pallas_call | solution.py:361
  29.9 0.0 collective-permute-done.5.iha
  29.9 0.0 collective-permute-done.6.ihb
  29.9 1.7 %near2.1.acc_in = f32[8,256,256]{2,1,0:T(8,128)S(1)} custom-call(s32[818]{0:T(1024)S(4)} %get-tuple-element.29.lists, f32[808]{0:T(1024)S(4)} %get-tuple-element.30.coefs, bf16[8,8,256,256]{3,2,1,0:T(8,128)(2,1)S(1)} %get-tuple-element.36.inter, bf16[2,256,256]{2,1,0:T(8,128)(2,1)S(1)} %collective-permute-done.5.iha, ...), custom_call_target="tpu_custom_call", output_to_operand_aliasing={{}: (5, {})} | custom-call | flops 1000 | bytes 1000 | tf_op jit(solution)/shard_map/near2/pallas_call | solution.py:366
  31.7 0.0 collective-permute-done.4.xh
  31.7 1.4 %early.1.acc_in = f32[8,256,256]{2,1,0:T(8,128)S(1)} custom-call(s32[818]{0:T(1024)S(4)} %get-tuple-element.29.lists, f32[808]{0:T(1024)S(4)} %get-tuple-element.30.coefs, bf16[8,8,256,256]{3,2,1,0:T(8,128)(2,1)S(1)} %get-tuple-element.36.inter, bf16[3,256,256]{2,1,0:T(8,128)(2,1)S(1)} %collective-permute-done.4.xh, ...), custom_call_target="tpu_custom_call", output_to_operand_aliasing={{}: (4, {})} | custom-call | flops 1000 | bytes 1000 | tf_op jit(solution)/shard_map/early/pallas_call | solution.py:370
  33.1 0.0 collective-permute-done.3.xh
  33.1 2.4 %last.1 = (f32[8,256,256]{2,1,0:T(8,128)}, f32[16,256]{1,0:T(8,128)S(1)}, f32[8,256,256]{2,1,0:T(8,128)S(1)}) custom-call(s32[818]{0:T(1024)S(4)} %get-tuple-element.29.lists, f32[808]{0:T(1024)S(4)} %get-tuple-element.30.coefs, bf16[8,8,256,256]{3,2,1,0:T(8,128)(2,1)S(1)} %get-tuple-element.36.inter, ...), custom_call_target="tpu_custom_call", output_to_operand_aliasing={{2}: (7, {})} | custom-call | flops 1000 | bytes 1000 | tf_op jit(solution)/shard_map/last/pallas_call | solution.py:374
  35.5 13.0 %all_to_all.9 = f32[16,1,256]{2,1,0:T(1,128)S(1)} all-to-all(f32[16,1,256]{2,1,0:T(1,128)S(1)} %copy.22), channel_id=1, replica_groups=mesh['grp'=2,'row'=16] {'row'}, dimensions={0} | all-to-all | bytes 32768 | tf_op jit(solution)/shard_map/all_to_all | solution.py:380
  48.6 0.1 bitcast_reduce_fusion
  48.7 0.5 %multiply_sqrt_fusion = f32[2]{0:T(128)} fusion(f32[2]{0:T(128)S(1)} %bitcast_reduce_fusion), kind=kLoop, calls=%fused_computation.1 | loop fusion | flops 2 | bytes 16 | tf_op jit(solution)/shard_map/sqrt | solution.py:381
  (2 shorter events, 0.1 us)
Async XLA Ops:
  2.1 11.8 %collective-permute-start = (bf16[4,256,256]{2,1,0:T(8,128)(2,1)S(1)}, bf16[4,256,256]{2,1,0:T(8,128)(2,1)S(1)}, u32[]{:S(2)}, u32[]{:S(2)}) collective-permute-start(bf16[4,256,256]{2,1,0:T(8,128)(2,1)S(1)} %first.1.x), channel_id=1, source_target_pairs={{1,2},{3,4},{5,6},{7,8},{9,10},{11,12},{13,14},{2,1},{4,3},{6,5},{... | collective-permute-start | bytes 1572872 | tf_op jit(solution)/shard_map/ppermute | solution.py:321
  5.9 7.0 %collective-permute-start.1 = (bf16[2,256,256]{2,1,0:T(8,128)(2,1)S(1)}, bf16[2,256,256]{2,1,0:T(8,128)(2,1)S(1)}, u32[]{:S(2)}, u32[]{:S(2)}) collective-permute-start(bf16[2,256,256]{2,1,0:T(8,128)(2,1)S(1)} %get-tuple-element.33.ia), channel_id=1, source_target_pairs={{0,1},{1,0},{2,3},{3,2},{4,5},{5,4},{6,7},{7,6},{8,9},{9,8},{10,11... | collective-permute-start | bytes 786440 | tf_op jit(solution)/shard_map/ppermute | solution.py:333
  10.2 2.7 %collective-permute-start.2 = (bf16[2,256,256]{2,1,0:T(8,128)(2,1)S(1)}, bf16[2,256,256]{2,1,0:T(8,128)(2,1)S(1)}, u32[]{:S(2)}, u32[]{:S(2)}) collective-permute-start(bf16[2,256,256]{2,1,0:T(8,128)(2,1)S(1)} %get-tuple-element.34.ib), channel_id=1, source_target_pairs={{0,1},{1,0},{2,3},{3,2},{4,5},{5,4},{6,7},{7,6},{8,9},{9,8},{10,11... | collective-permute-start | bytes 786440 | tf_op jit(solution)/shard_map/ppermute | solution.py:333
  15.0 16.6 %collective-permute-start.4 = (bf16[3,256,256]{2,1,0:T(8,128)(2,1)S(1)}, bf16[3,256,256]{2,1,0:T(8,128)(2,1)S(1)}, u32[]{:S(2)}, u32[]{:S(2)}) collective-permute-start(bf16[3,256,256]{2,1,0:T(8,128)(2,1)S(1)} %get-tuple-element.48.xa), channel_id=1, source_target_pairs={{1,2},{3,4},{5,6},{7,8},{9,10},{11,12},{13,14},{2,1},{4,3},{6,5},{... | collective-permute-start | bytes 1179656 | tf_op jit(solution)/shard_map/ppermute | solution.py:354
  19.5 10.4 %collective-permute-start.5 = (bf16[2,256,256]{2,1,0:T(8,128)(2,1)S(1)}, bf16[2,256,256]{2,1,0:T(8,128)(2,1)S(1)}, u32[]{:S(2)}, u32[]{:S(2)}) collective-permute-start(bf16[2,256,256]{2,1,0:T(8,128)(2,1)S(1)} %get-tuple-element.49.ia), channel_id=1, source_target_pairs={{0,1},{1,0},{2,3},{3,2},{4,5},{5,4},{6,7},{7,6},{8,9},{9,8},{10,11... | collective-permute-start | bytes 786440 | tf_op jit(solution)/shard_map/ppermute | solution.py:333
  25.3 4.6 %collective-permute-start.6 = (bf16[2,256,256]{2,1,0:T(8,128)(2,1)S(1)}, bf16[2,256,256]{2,1,0:T(8,128)(2,1)S(1)}, u32[]{:S(2)}, u32[]{:S(2)}) collective-permute-start(bf16[2,256,256]{2,1,0:T(8,128)(2,1)S(1)} %get-tuple-element.50.ib), channel_id=1, source_target_pairs={{0,1},{1,0},{2,3},{3,2},{4,5},{5,4},{6,7},{7,6},{8,9},{9,8},{10,11... | collective-permute-start | bytes 786440 | tf_op jit(solution)/shard_map/ppermute | solution.py:333
  25.4 7.7 %collective-permute-start.3 = (bf16[1,256,256]{2,1,0:T(8,128)(2,1)S(1)}, bf16[1,256,256]{2,1,0:T(8,128)(2,1)S(1)}, u32[]{:S(2)}, u32[]{:S(2)}) collective-permute-start(bf16[1,256,256]{2,1,0:T(8,128)(2,1)S(1)} %get-tuple-element.41.xb), channel_id=1, source_target_pairs={{1,2},{3,4},{5,6},{7,8},{9,10},{11,12},{13,14},{2,1},{4,3},{6,5},{... | collective-permute-start | bytes 393224 | tf_op jit(solution)/shard_map/ppermute | solution.py:355

commit v8 on v4

--- a/solution.py
+++ b/solution.py
@@ -64,9 +64,10 @@
     for c in small:
         c.wait()
     dens = denominators(en, [gp[p] for p in slots], slots)
-    for i, p in enumerate(slots):
+    factors = [-lv[p].astype(F32) / dens[i] for i, p in enumerate(slots)]
+    for i in range(4):
         tiles[i].wait()
-        out[i] = (-lv[p].astype(F32) * buf[i].astype(F32) / dens[i]).astype(BF16)
+        out[i] = (buf[i].astype(F32) * factors[i]).astype(BF16)
 
 
 def second_kernel(
@@ -245,10 +246,9 @@
         near_list(half, lists, coefs, inter, src, acc)
 
 
-def last_kernel(lists, coefs, inter, xh, recip, amps, sq1, acc_in, out, sums, acc, buf, sem):
+def last_kernel(lists, coefs, inter, xh, sq1, acc_in, sums, acc):
     del acc_in
     total = jnp.zeros((8, 128), F32)
-    copies = []
     slots = slots_of(0, 8)
     refs = (lists, coefs, inter, xh, acc)
     for half in range(2):
@@ -256,15 +256,18 @@
     for half in range(2):
         step((2 + half) * CAP, SHORT, *refs)
         for q in range(4 * half, 4 * half + 4):
-            p = slots[q]
-            res = lists[LIVE + p].astype(F32) * acc[q]
-            total = total + squares(res)
-            buf[q] = amps[q] - res * recip[q]
-            copies.append(pltpu.make_async_copy(buf.at[q], out.at[p], sem.at[q]))
-            copies[-1].start()
-    rows = (sums.shape[0], 128)
-    sums[:, :128] = jnp.broadcast_to(jnp.sum(sq1[...], axis=0, keepdims=True), rows)
-    sums[:, 128:] = jnp.broadcast_to(jnp.sum(total, axis=0, keepdims=True), rows)
+            total = total + squares(lists[LIVE + slots[q]].astype(F32) * acc[q])
+    row = lax.broadcasted_iota(jnp.int32, sums.shape, 0) & 1
+    first = jnp.sum(sq1[...], axis=0, keepdims=True)
+    sums[...] = jnp.where(row == 0, first, jnp.sum(total, axis=0, keepdims=True))
+
+
+def output_kernel(lists, recip, amps, acc, out, buf, sem):
+    copies = []
+    for q, p in enumerate(slots_of(0, 8)):
+        buf[q] = amps[q] - lists[LIVE + p].astype(F32) * acc[q] * recip[q]
+        copies.append(pltpu.make_async_copy(buf.at[q], out.at[p], sem.at[q]))
+        copies[-1].start()
     for c in copies:
         c.wait()
 
@@ -328,12 +331,17 @@
         scratch_shapes=[gathered], input_output_aliases={11: 0},
         compiler_params=params(8), cost_estimate=COST, name="near2",
     )(*meta, inter, exch, energy, vmem(x1), vmem(i1a), vmem(i1b), *swap(i1a, i1b), vmem(amps), vmem(acc))
-    out, sums, _ = pl.pallas_call(
-        last_kernel, out_shape=[jax.ShapeDtypeStruct((8, v, v), F32), pltpu.VMEM((count, 256), F32), tiles8],
-        in_specs=[SM] * 2 + [VM] * 6, out_specs=[AN, VM, VM], input_output_aliases={7: 2},
+    sums, acc = pl.pallas_call(
+        last_kernel, out_shape=[pltpu.VMEM((2 * count, 128), F32), tiles8],
+        in_specs=[SM] * 2 + [VM] * 4, out_specs=[VM, VM], input_output_aliases={5: 1},
+        compiler_params=params(8), cost_estimate=COST, name="last",
+    )(*meta, inter, vmem(xh1), vmem(sq), vmem(acc))
+    out = pl.pallas_call(
+        output_kernel, out_shape=jax.ShapeDtypeStruct((8, v, v), F32), in_specs=[SM] + [VM] * 3, out_specs=AN,
         scratch_shapes=[pltpu.VMEM((8, v, v), F32), dma((8,))],
-        compiler_params=params(8), cost_estimate=COST, name="last",
-    )(*meta, inter, vmem(xh1), vmem(recip), vmem(amps), vmem(sq), vmem(acc))
+        compiler_params=params(16), name="output",
+        cost_estimate=pl.CostEstimate(flops=10**7, bytes_accessed=10**7, transcendentals=0),
+    )(lists, vmem(recip), vmem(amps), vmem(acc))
     sums = lax.all_to_all(sums, "row", 0, 0, tiled=True)
     norms = jnp.sqrt(jnp.sum(sums.reshape(count, 2, 128), axis=(0, 2)) / (amp_exch.shape[0] * count * v * v))
     return out, norms

time: 48.3 us -> 47.8 us (0.990)
  blocking collectives: 13.6 us -> 0 us
  starting transfers between devices: 12.5 us -> 17.8 us
  local copies, waits for them, and re-layouts: 0.02 us -> 3.19 us
  Pallas kernels: 17.6 us -> 20.2 us
  waiting for transfers between devices: 2.92 us -> 4.81 us
    all_to_all x1 -> x0, blocking collectives: 13.6 us -> none  [on_device(): sums = lax.all_to_all(sums, 'row', 0, 0, tiled=True)]
    all_to_all x0 -> x1, starting transfers between devices: none -> 6.22 us  [on_device(): sums = lax.all_to_all(sums, 'row', 0, 0, tiled=True)]
    unnamed x0 -> x8, local copies, waits for them, and re-layouts: none -> 3.19 us
    all_to_all x0 -> x1, waiting for transfers between devices: none -> 1.89 us  [on_device(): sums = lax.all_to_all(sums, 'row', 0, 0, tiled=True)]
    pallas_call x1, Pallas kernels: 3.09 us -> 4.03 us  [on_device(): pl.pallas_call(rest_kernel, out_shape=[tiles2, tiles2] + [tiles8] * 3, in...]
    pallas_call x1, Pallas kernels: 3.65 us -> 4.59 us  [on_device(): pl.pallas_call(near_kernel_2, out_shape=[tiles8, pltpu.VMEM((8, 128), F32...]
    ppermute x4, starting transfers between devices: 11.1 us -> 10.2 us  [swap(): return [vmem(lax.ppermute(h, 'row', same_chip)) for h in halves]]
    pallas_call x1 -> x2, Pallas kernels: 3.03 us -> 3.8 us  [the longest x1 2.38 us: on_device(): pl.pallas_call(last_kernel, out_shape=[pltpu.VMEM((2 * count, 128), F32),...]
  transfers between devices with their start and end apart: 6 -> 7, of which waited for: 4 -> 5; matrix products, arithmetic and copies ran while one was open for 0% -> 0% of each run, Pallas kernels for 25% -> 32%
where the time goes in v8:
time: 47.8 us; the launch traced here: 47.5 us
  Pallas kernels  20.2 us (42%)
  starting transfers between devices  17.8 us (37%)
  waiting for transfers between devices  4.81 us (10%)
  local copies, waits for them, and re-layouts  3.19 us (7%)
  between operations  0.77 us (2%)
  other arithmetic  0.66 us (1%)
    ppermute x4, starting transfers between devices, swap(): return [vmem(lax.ppermute(h, 'row', same_chip)) for h in halves]  10.2 us
    all_to_all x1, starting transfers between devices, on_device(): sums = lax.all_to_all(sums, 'row', 0, 0, tiled=True)  6.22 us
    pallas_call x1, Pallas kernels, on_device(): pl.pallas_call(near_kernel_2, out_shape=[tiles8, pltpu.VMEM((8, 128), F32...  4.59 us
    pallas_call x1, Pallas kernels, on_device(): pl.pallas_call(rest_kernel, out_shape=[tiles2, tiles2] + [tiles8] * 3, in...  4.03 us
    unnamed x8, local copies, waits for them, and re-layouts  3.19 us
    ppermute x4, waiting for transfers between devices, swap(): return [vmem(lax.ppermute(h, 'row', same_chip)) for h in halves]  2.91 us
    pallas_call x1, Pallas kernels, on_device(): pl.pallas_call(second_kernel, out_shape=[tiles2, tiles2, pltpu.VMEM((8, v...  2.79 us
    pallas_call x1, Pallas kernels, on_device(): pl.pallas_call(near_kernel_1, out_shape=[tiles8] * 3 + [gathered, slabs],...  2.58 us
  transfers between devices with their start and end apart: 7, of which 5 were waited for; matrix products, arithmetic and copies ran while one was open for 0% of the time, Pallas kernels for 32%

profile of v8, /device:TPU:0, one launch (start us, length us, event | category | flops | bytes accessed | tf_op | source)
XLA Modules:
  0.0 47.5 jit_solution(9626656827494570191)
XLA Ops:
  0.6 1.4 %first.1.x = bf16[4,256,256]{2,1,0:T(8,128)(2,1)S(1)} custom-call(bf16[8,256,256]{2,1,0:T(8,128)(2,1)} %exch.3, f32[8,256]{1,0:T(8,128)} %energy.3, f32[8]{0:T(128)} %gap.3, s32[8]{0:T(128)} %live.3), custom_call_target="tpu_custom_call" | custom-call | flops 1000 | bytes 1000 | tf_op jit(solution)/shard_map/first/pallas_call | solution.py:290
  2.0 0.7 %collective-permute-start.2 = (bf16[4,256,256]{2,1,0:T(8,128)(2,1)S(1)}, bf16[4,256,256]{2,1,0:T(8,128)(2,1)S(1)}, u32[]{:S(2)}, u32[]{:S(2)}) collective-permute-start(bf16[4,256,256]{2,1,0:T(8,128)(2,1)S(1)} %first.1.x), channel_id=1, source_target_pairs={{1,2},{3,4},{5,6},{7,8},{9,10},{11,12},{13,14},{2,1},{4,3},{6,5},{... | collective-permute-start | bytes 1572872 | tf_op jit(solution)/shard_map/ppermute | solution.py:295
  2.7 2.8 %second.1 = (bf16[2,256,256]{2,1,0:T(8,128)(2,1)S(1)}, bf16[2,256,256]{2,1,0:T(8,128)(2,1)S(1)}, bf16[8,256,256]{2,1,0:T(8,128)(2,1)S(1)}, f32[8,256]{1,0:T(8,12...) custom-call(bf16[8,256,256]{2,1,0:T(8,128)(2,1)} %exch.3, f32[8,256]{1,0:T(8,128)} %energy.3, ...), custom_call_target="tpu_custom_call" | custom-call | flops 1000 | bytes 1000 | tf_op jit(solution)/shard_map/second/pallas_call | solution.py:296
  5.5 4.4 %collective-permute-start = (bf16[2,256,256]{2,1,0:T(8,128)(2,1)S(1)}, bf16[2,256,256]{2,1,0:T(8,128)(2,1)S(1)}, u32[]{:S(2)}, u32[]{:S(2)}) collective-permute-start(bf16[2,256,256]{2,1,0:T(8,128)(2,1)S(1)} %get-tuple-element.30.ia), channel_id=1, source_target_pairs={{0,1},{1,0},{2,3},{3,2},{4,5},{5,4},{6,7},{7,6},{8,9},{9,8},{10,11... | collective-permute-start | bytes 786440 | tf_op jit(solution)/shard_map/ppermute | solution.py:307
  9.9 0.1 collective-permute-start.1
  9.9 1.1 %collective-permute-done.iha = bf16[2,256,256]{2,1,0:T(8,128)(2,1)S(1)} collective-permute-done((bf16[2,256,256]{2,1,0:T(8,128)(2,1)S(1)}, bf16[2,256,256]{2,1,0:T(8,128)(2,1)S(1)}, u32[]{:S(2)}, u32[]{:S(2)}) %collective-permute-start) | collective-permute-done | bytes 262176 | tf_op jit(solution)/shard_map/ppermute | solution.py:307
  11.0 0.4 collective-permute-done.1.ihb
  11.4 2.6 %near1.1 = (f32[8,256,256]{2,1,0:T(8,128)S(1)}, f32[8,256,256]{2,1,0:T(8,128)S(1)}, f32[8,256,256]{2,1,0:T(8,128)S(1)}, bf16[12,256,256]{2,1,0:T(8,128)(2,1)S(1)}, bf16[8,8,256,256]{3,2,1,0:T(8,128)(2,1)S(1)}) custom-call(s32[300]{0:T(512)S(4)} %get-tuple-element.26.lists, f32[296]{0:T(512)S(4)} %get-tuple-element.27.coefs, ...), custom_call_target="tpu_custom_call", output_to_operand_aliasing={{4}: (10, {})} | custom-call | flops 1000 | bytes 1000 | tf_op jit(solution)/shard_map/near1/pallas_call | solution.py:312
  14.0 0.0 collective-permute-done.2.xh
  14.0 1.1 %across.1 = (bf16[4,256,256]{2,1,0:T(8,128)(2,1)S(1)}, f32[8,256,256]{2,1,0:T(8,128)S(1)}, f32[8,256,256]{2,1,0:T(8,128)S(1)}) custom-call(s32[300]{0:T(512)S(4)} %get-tuple-element.26.lists, f32[296]{0:T(512)S(4)} %get-tuple-element.27.coefs, bf16[8,8,256,256]{3,2,1,0:T(8,128)(2,1)S(1)} %get-tuple-element.33.inter, ...), custom_call_target="tpu_custom_call", output_to_operand_aliasing={{1}: (5, {}), {2}: (6, {})} | custom-call | flops 1000 | bytes 1000 | tf_op jit(solution)/shard_map/across/pallas_call | solution.py:318
  15.1 0.7 %collective-permute-start.3 = (bf16[4,256,256]{2,1,0:T(8,128)(2,1)S(1)}, bf16[4,256,256]{2,1,0:T(8,128)(2,1)S(1)}, u32[]{:S(2)}, u32[]{:S(2)}) collective-permute-start(bf16[4,256,256]{2,1,0:T(8,128)(2,1)S(1)} %get-tuple-element.42.x), channel_id=1, source_target_pairs={{1,2},{3,4},{5,6},{7,8},{9,10},{11,12},{13,14},{2,1},{4,3},{6,5},{... | collective-permute-start | bytes 1572872 | tf_op jit(solution)/shard_map/ppermute | solution.py:323
  15.8 4.0 %rest.1 = (bf16[2,256,256]{2,1,0:T(8,128)(2,1)S(1)}, bf16[2,256,256]{2,1,0:T(8,128)(2,1)S(1)}, f32[8,256,256]{2,1,0:T(8,128)S(1)}, f32[8,256,256]{2,1,0:T(8,128)S(1)}, f32[8,256,256]{2,1,0:T(8,128)S(1)}) custom-call(s32[300]{0:T(512)S(4)} %get-tuple-element.26.lists, ...), custom_call_target="tpu_custom_call", output_to_operand_aliasing={{2}: (7, {}), {3}: (8, {}), {4}: (9, {})} | custom-call | flops 1000 | bytes 1000 | tf_op jit(solution)/shard_map/rest/pallas_call | solution.py:324
  19.8 0.0 copy-start
  19.8 0.0 copy-start.2
  19.8 5.7 %collective-permute-start.4 = (bf16[2,256,256]{2,1,0:T(8,128)(2,1)S(1)}, bf16[2,256,256]{2,1,0:T(8,128)(2,1)S(1)}, u32[]{:S(2)}, u32[]{:S(2)}) collective-permute-start(bf16[2,256,256]{2,1,0:T(8,128)(2,1)S(1)} %get-tuple-element.43.ia), channel_id=1, source_target_pairs={{0,1},{1,0},{2,3},{3,2},{4,5},{5,4},{6,7},{7,6},{8,9},{9,8},{10,11... | collective-permute-start | bytes 786440 | tf_op jit(solution)/shard_map/ppermute | solution.py:307
  25.5 0.1 collective-permute-start.5
  25.6 1.1 %collective-permute-done.4.iha = bf16[2,256,256]{2,1,0:T(8,128)(2,1)S(1)} collective-permute-done((bf16[2,256,256]{2,1,0:T(8,128)(2,1)S(1)}, bf16[2,256,256]{2,1,0:T(8,128)(2,1)S(1)}, u32[]{:S(2)}, u32[]{:S(2)}) %collective-permute-start.4) | collective-permute-done | bytes 262176 | tf_op jit(solution)/shard_map/ppermute | solution.py:307
  26.7 0.4 collective-permute-done.5.ihb
  27.1 4.6 %near2.1 = (f32[8,256,256]{2,1,0:T(8,128)S(1)}, f32[8,128]{1,0:T(8,128)S(1)}) custom-call(s32[300]{0:T(512)S(4)} %get-tuple-element.26.lists, f32[296]{0:T(512)S(4)} %get-tuple-element.27.coefs, bf16[8,8,256,256]{3,2,1,0:T(8,128)(2,1)S(1)} %get-tuple-element.33.inter, ...), custom_call_target="tpu_custom_call", output_to_operand_aliasing={{0}: (11, {})} | custom-call | flops 1000 | bytes 1000 | tf_op jit(solution)/shard_map/near2/pallas_call | solution.py:329
  31.7 0.0 copy-done
  31.7 0.0 copy-done.2
  31.7 0.0 collective-permute-done.3.xh
  31.7 2.4 %last.1 = (f32[32,128]{1,0:T(8,128)}, f32[8,256,256]{2,1,0:T(8,128)S(1)}) custom-call(s32[300]{0:T(512)S(4)} %get-tuple-element.26.lists, f32[296]{0:T(512)S(4)} %get-tuple-element.27.coefs, bf16[8,8,256,256]{3,2,1,0:T(8,128)(2,1)S(1)} %get-tuple-element.33.inter, ...), custom_call_target="tpu_custom_call", output_to_operand_aliasing={{1}: (5, {})} | custom-call | flops 1000 | bytes 1000 | tf_op jit(solution)/shard_map/last/pallas_call | solution.py:334
  34.1 6.2 %all-to-all-start = ((f32[16,2,128]{2,1,0:T(2,128)}), f32[16,2,128]{2,1,0:T(2,128)S(1)}, u32[]{:S(2)}, u32[]{:S(2)}) async-start(f32[16,2,128]{2,1,0:T(2,128)} %bitcast), calls=%async_computation | async-start | bytes 32768 | tf_op jit(solution)/shard_map/all_to_all | solution.py:345
  40.3 0.0 copy-start.1
  40.3 1.6 %copy-done.1 = f32[8,256,256]{2,1,0:T(8,128)S(1)} copy-done((f32[8,256,256]{2,1,0:T(8,128)S(1)}, f32[8,256,256]{2,1,0:T(8,128)}, u32[]{:S(2)}) %copy-start.1) | copy-done | bytes 2097176
  41.9 0.0 copy-start.3
  41.9 1.6 %copy-done.3 = f32[8,256,256]{2,1,0:T(8,128)S(1)} copy-done((f32[8,256,256]{2,1,0:T(8,128)S(1)}, f32[8,256,256]{2,1,0:T(8,128)}, u32[]{:S(2)}) %copy-start.3) | copy-done | bytes 2097176
  43.5 1.4 %output.1 = f32[8,256,256]{2,1,0:T(8,128)} custom-call(s32[300]{0:T(512)S(4)} %get-tuple-element.26.lists, f32[8,256,256]{2,1,0:T(8,128)S(1)} %copy-done.3, f32[8,256,256]{2,1,0:T(8,128)S(1)} %copy-done.1, f32[8,256,256]{2,1,0:T(8,128)S(1)} %get-tuple-element.48.acc), custom_call_target="tpu_custom_call" | custom-call | flops 10000000 | bytes 10000000 | tf_op jit(solution)/shard_map/output/pallas_call | solution.py:339
  44.9 1.9 %all-to-all-done = f32[16,2,128]{2,1,0:T(2,128)S(1)} async-done(((f32[16,2,128]{2,1,0:T(2,128)}), f32[16,2,128]{2,1,0:T(2,128)S(1)}, u32[]{:S(2)}, u32[]{:S(2)}) %all-to-all-start) | async-done | bytes 16416 | tf_op jit(solution)/shard_map/all_to_all | solution.py:345
  46.8 0.1 reduce_sum.9
  47.0 0.5 %multiply_sqrt_fusion = f32[2]{0:T(128)} fusion(f32[2]{0:T(128)S(1)} %reduce_sum.9), kind=kLoop, calls=%fused_computation | loop fusion | flops 2 | bytes 16 | tf_op jit(solution)/shard_map/sqrt | solution.py:346
Async XLA Ops:
  2.0 12.0 %collective-permute-start.2 = (bf16[4,256,256]{2,1,0:T(8,128)(2,1)S(1)}, bf16[4,256,256]{2,1,0:T(8,128)(2,1)S(1)}, u32[]{:S(2)}, u32[]{:S(2)}) collective-permute-start(bf16[4,256,256]{2,1,0:T(8,128)(2,1)S(1)} %first.1.x), channel_id=1, source_target_pairs={{1,2},{3,4},{5,6},{7,8},{9,10},{11,12},{13,14},{2,1},{4,3},{6,5},{... | collective-permute-start | bytes 1572872 | tf_op jit(solution)/shard_map/ppermute | solution.py:295
  5.5 5.5 %collective-permute-start = (bf16[2,256,256]{2,1,0:T(8,128)(2,1)S(1)}, bf16[2,256,256]{2,1,0:T(8,128)(2,1)S(1)}, u32[]{:S(2)}, u32[]{:S(2)}) collective-permute-start(bf16[2,256,256]{2,1,0:T(8,128)(2,1)S(1)} %get-tuple-element.30.ia), channel_id=1, source_target_pairs={{0,1},{1,0},{2,3},{3,2},{4,5},{5,4},{6,7},{7,6},{8,9},{9,8},{10,11... | collective-permute-start | bytes 786440 | tf_op jit(solution)/shard_map/ppermute | solution.py:307
  9.9 1.5 %collective-permute-start.1 = (bf16[2,256,256]{2,1,0:T(8,128)(2,1)S(1)}, bf16[2,256,256]{2,1,0:T(8,128)(2,1)S(1)}, u32[]{:S(2)}, u32[]{:S(2)}) collective-permute-start(bf16[2,256,256]{2,1,0:T(8,128)(2,1)S(1)} %get-tuple-element.31.ib), channel_id=1, source_target_pairs={{0,1},{1,0},{2,3},{3,2},{4,5},{5,4},{6,7},{7,6},{8,9},{9,8},{10,11... | collective-permute-start | bytes 786440 | tf_op jit(solution)/shard_map/ppermute | solution.py:307
  15.1 16.6 %collective-permute-start.3 = (bf16[4,256,256]{2,1,0:T(8,128)(2,1)S(1)}, bf16[4,256,256]{2,1,0:T(8,128)(2,1)S(1)}, u32[]{:S(2)}, u32[]{:S(2)}) collective-permute-start(bf16[4,256,256]{2,1,0:T(8,128)(2,1)S(1)} %get-tuple-element.42.x), channel_id=1, source_target_pairs={{1,2},{3,4},{5,6},{7,8},{9,10},{11,12},{13,14},{2,1},{4,3},{6,5},{... | collective-permute-start | bytes 1572872 | tf_op jit(solution)/shard_map/ppermute | solution.py:323
  19.8 11.9 %copy-start = (f32[8,256,256]{2,1,0:T(8,128)}, f32[8,256,256]{2,1,0:T(8,128)S(1)}, u32[]{:S(2)}) copy-start(f32[8,256,256]{2,1,0:T(8,128)S(1)} %get-tuple-element.41.amps) | copy-start | bytes 6291460
  19.8 11.9 %copy-start.2 = (f32[8,256,256]{2,1,0:T(8,128)}, f32[8,256,256]{2,1,0:T(8,128)S(1)}, u32[]{:S(2)}) copy-start(f32[8,256,256]{2,1,0:T(8,128)S(1)} %get-tuple-element.40.recip) | copy-start | bytes 6291460
  19.8 6.9 %collective-permute-start.4 = (bf16[2,256,256]{2,1,0:T(8,128)(2,1)S(1)}, bf16[2,256,256]{2,1,0:T(8,128)(2,1)S(1)}, u32[]{:S(2)}, u32[]{:S(2)}) collective-permute-start(bf16[2,256,256]{2,1,0:T(8,128)(2,1)S(1)} %get-tuple-element.43.ia), channel_id=1, source_target_pairs={{0,1},{1,0},{2,3},{3,2},{4,5},{5,4},{6,7},{7,6},{8,9},{9,8},{10,11... | collective-permute-start | bytes 786440 | tf_op jit(solution)/shard_map/ppermute | solution.py:307
  25.5 1.5 %collective-permute-start.5 = (bf16[2,256,256]{2,1,0:T(8,128)(2,1)S(1)}, bf16[2,256,256]{2,1,0:T(8,128)(2,1)S(1)}, u32[]{:S(2)}, u32[]{:S(2)}) collective-permute-start(bf16[2,256,256]{2,1,0:T(8,128)(2,1)S(1)} %get-tuple-element.44.ib), channel_id=1, source_target_pairs={{0,1},{1,0},{2,3},{3,2},{4,5},{5,4},{6,7},{7,6},{8,9},{9,8},{10,11... | collective-permute-start | bytes 786440 | tf_op jit(solution)/shard_map/ppermute | solution.py:307
  34.1 12.7 %all-to-all-start = ((f32[16,2,128]{2,1,0:T(2,128)}), f32[16,2,128]{2,1,0:T(2,128)S(1)}, u32[]{:S(2)}, u32[]{:S(2)}) async-start(f32[16,2,128]{2,1,0:T(2,128)} %bitcast), calls=%async_computation | async-start | bytes 32768 | tf_op jit(solution)/shard_map/all_to_all | solution.py:345
  40.3 1.6 %copy-start.1 = (f32[8,256,256]{2,1,0:T(8,128)S(1)}, f32[8,256,256]{2,1,0:T(8,128)}, u32[]{:S(2)}) copy-start(f32[8,256,256]{2,1,0:T(8,128)} %copy-done) | copy-start | bytes 6291460
  41.9 1.6 %copy-start.3 = (f32[8,256,256]{2,1,0:T(8,128)S(1)}, f32[8,256,256]{2,1,0:T(8,128)}, u32[]{:S(2)}) copy-start(f32[8,256,256]{2,1,0:T(8,128)} %copy-done.2) | copy-start | bytes 6291460

commit v9 on v8

--- a/solution.py
+++ b/solution.py
@@ -246,7 +246,7 @@
         near_list(half, lists, coefs, inter, src, acc)
 
 
-def last_kernel(lists, coefs, inter, xh, sq1, acc_in, sums, acc):
+def last_kernel(lists, coefs, inter, xh, recip, amps, sq1, acc_in, sums, acc):
     del acc_in
     total = jnp.zeros((8, 128), F32)
     slots = slots_of(0, 8)
@@ -256,19 +256,16 @@
     for half in range(2):
         step((2 + half) * CAP, SHORT, *refs)
         for q in range(4 * half, 4 * half + 4):
-            total = total + squares(lists[LIVE + slots[q]].astype(F32) * acc[q])
+            res = lists[LIVE + slots[q]].astype(F32) * acc[q]
+            total = total + squares(res)
+            acc[q] = amps[q] - res * recip[q]
     row = lax.broadcasted_iota(jnp.int32, sums.shape, 0) & 1
     first = jnp.sum(sq1[...], axis=0, keepdims=True)
     sums[...] = jnp.where(row == 0, first, jnp.sum(total, axis=0, keepdims=True))
 
 
-def output_kernel(lists, recip, amps, acc, out, buf, sem):
-    copies = []
-    for q, p in enumerate(slots_of(0, 8)):
-        buf[q] = amps[q] - lists[LIVE + p].astype(F32) * acc[q] * recip[q]
-        copies.append(pltpu.make_async_copy(buf.at[q], out.at[p], sem.at[q]))
-        copies[-1].start()
-    for c in copies:
+def output_kernel(tiles, out, sem):
+    for c in start_all([(tiles.at[q], out.at[p]) for q, p in enumerate(slots_of(0, 8))], sem):
         c.wait()
 
 
@@ -333,15 +330,14 @@
     )(*meta, inter, exch, energy, vmem(x1), vmem(i1a), vmem(i1b), *swap(i1a, i1b), vmem(amps), vmem(acc))
     sums, acc = pl.pallas_call(
         last_kernel, out_shape=[pltpu.VMEM((2 * count, 128), F32), tiles8],
-        in_specs=[SM] * 2 + [VM] * 4, out_specs=[VM, VM], input_output_aliases={5: 1},
+        in_specs=[SM] * 2 + [VM] * 6, out_specs=[VM, VM], input_output_aliases={7: 1},
         compiler_params=params(8), cost_estimate=COST, name="last",
-    )(*meta, inter, vmem(xh1), vmem(sq), vmem(acc))
+    )(*meta, inter, vmem(xh1), vmem(recip), vmem(amps), vmem(sq), vmem(acc))
     out = pl.pallas_call(
-        output_kernel, out_shape=jax.ShapeDtypeStruct((8, v, v), F32), in_specs=[SM] + [VM] * 3, out_specs=AN,
-        scratch_shapes=[pltpu.VMEM((8, v, v), F32), dma((8,))],
-        compiler_params=params(16), name="output",
-        cost_estimate=pl.CostEstimate(flops=10**7, bytes_accessed=10**7, transcendentals=0),
-    )(lists, vmem(recip), vmem(amps), vmem(acc))
+        output_kernel, out_shape=jax.ShapeDtypeStruct((8, v, v), F32), in_specs=[VM], out_specs=AN,
+        scratch_shapes=[dma((8,))], compiler_params=params(4), name="output",
+        cost_estimate=pl.CostEstimate(flops=10**6, bytes_accessed=10**7, transcendentals=0),
+    )(vmem(acc))
     sums = lax.all_to_all(sums, "row", 0, 0, tiled=True)
     norms = jnp.sqrt(jnp.sum(sums.reshape(count, 2, 128), axis=(0, 2)) / (amp_exch.shape[0] * count * v * v))
     return out, norms

time: 47.8 us -> 48.1 us (level)
  starting transfers between devices: 17.8 us -> 21.3 us
  waiting for transfers between devices: 4.81 us -> 8.02 us
  local copies, waits for them, and re-layouts: 3.19 us -> 0 us
  Pallas kernels: 20.2 us -> 17.1 us
    all_to_all x1, waiting for transfers between devices: 1.89 us -> 5.1 us  [on_device(): sums = lax.all_to_all(sums, 'row', 0, 0, tiled=True)]
    unnamed x8 -> x0, local copies, waits for them, and re-layouts: 3.19 us -> none
    all_to_all x1, starting transfers between devices: 6.22 us -> 8.29 us  [on_device(): sums = lax.all_to_all(sums, 'row', 0, 0, tiled=True)]
    pallas_call x1, Pallas kernels: 4.59 us -> 2.56 us  [on_device(): pl.pallas_call(near_kernel_2, out_shape=[tiles8, pltpu.VMEM((8, 128), F32...]
    pallas_call x1, Pallas kernels: 4.03 us -> 2.59 us  [on_device(): pl.pallas_call(rest_kernel, out_shape=[tiles2, tiles2] + [tiles8] * 3, in...]
    ppermute x4, starting transfers between devices: 10.2 us -> 11.7 us  [swap(): return [vmem(lax.ppermute(h, 'row', same_chip)) for h in halves]]
  transfers between devices with their start and end apart: 7 -> 7, of which waited for: 5 -> 5; matrix products, arithmetic and copies ran while one was open for 0% -> 0% of each run, Pallas kernels for 32% -> 25%
where the time goes in v9:
time: 48.1 us; the launch traced here: 47.8 us
  starting transfers between devices  21.3 us (44%)
  Pallas kernels  17.1 us (36%)
  waiting for transfers between devices  8.02 us (17%)
  between operations  0.73 us (2%)
  other arithmetic  0.66 us (1%)
    ppermute x4, starting transfers between devices, swap(): return [vmem(lax.ppermute(h, 'row', same_chip)) for h in halves]  11.7 us
    all_to_all x1, starting transfers between devices, on_device(): sums = lax.all_to_all(sums, 'row', 0, 0, tiled=True)  8.29 us
    all_to_all x1, waiting for transfers between devices, on_device(): sums = lax.all_to_all(sums, 'row', 0, 0, tiled=True)  5.1 us
    ppermute x4, waiting for transfers between devices, swap(): return [vmem(lax.ppermute(h, 'row', same_chip)) for h in halves]  2.91 us
    pallas_call x1, Pallas kernels, on_device(): pl.pallas_call(second_kernel, out_shape=[tiles2, tiles2, pltpu.VMEM((8, v...  2.79 us
    pallas_call x1, Pallas kernels, on_device(): pl.pallas_call(last_kernel, out_shape=[pltpu.VMEM((2 * count, 128), F32),...  2.73 us
    pallas_call x1, Pallas kernels, on_device(): pl.pallas_call(rest_kernel, out_shape=[tiles2, tiles2] + [tiles8] * 3, in...  2.59 us
    pallas_call x1, Pallas kernels, on_device(): pl.pallas_call(near_kernel_1, out_shape=[tiles8] * 3 + [gathered, slabs],...  2.58 us
  transfers between devices with their start and end apart: 7, of which 5 were waited for; matrix products, arithmetic and copies ran while one was open for 0% of the time, Pallas kernels for 25%

profile of v9, /device:TPU:0, one launch (start us, length us, event | category | flops | bytes accessed | tf_op | source)
XLA Modules:
  0.0 47.8 jit_solution(16109913349909273384)
XLA Ops:
  0.6 1.4 %first.1.x = bf16[4,256,256]{2,1,0:T(8,128)(2,1)S(1)} custom-call(bf16[8,256,256]{2,1,0:T(8,128)(2,1)} %exch.3, f32[8,256]{1,0:T(8,128)} %energy.3, f32[8]{0:T(128)} %gap.3, s32[8]{0:T(128)} %live.3), custom_call_target="tpu_custom_call" | custom-call | flops 1000 | bytes 1000 | tf_op jit(solution)/shard_map/first/pallas_call | solution.py:287
  2.0 0.7 %collective-permute-start.2 = (bf16[4,256,256]{2,1,0:T(8,128)(2,1)S(1)}, bf16[4,256,256]{2,1,0:T(8,128)(2,1)S(1)}, u32[]{:S(2)}, u32[]{:S(2)}) collective-permute-start(bf16[4,256,256]{2,1,0:T(8,128)(2,1)S(1)} %first.1.x), channel_id=1, source_target_pairs={{1,2},{3,4},{5,6},{7,8},{9,10},{11,12},{13,14},{2,1},{4,3},{6,5},{... | collective-permute-start | bytes 1572872 | tf_op jit(solution)/shard_map/ppermute | solution.py:292
  2.7 2.8 %second.1 = (bf16[2,256,256]{2,1,0:T(8,128)(2,1)S(1)}, bf16[2,256,256]{2,1,0:T(8,128)(2,1)S(1)}, bf16[8,256,256]{2,1,0:T(8,128)(2,1)S(1)}, f32[8,256]{1,0:T(8,12...) custom-call(bf16[8,256,256]{2,1,0:T(8,128)(2,1)} %exch.3, f32[8,256]{1,0:T(8,128)} %energy.3, ...), custom_call_target="tpu_custom_call" | custom-call | flops 1000 | bytes 1000 | tf_op jit(solution)/shard_map/second/pallas_call | solution.py:293
  5.5 4.4 %collective-permute-start = (bf16[2,256,256]{2,1,0:T(8,128)(2,1)S(1)}, bf16[2,256,256]{2,1,0:T(8,128)(2,1)S(1)}, u32[]{:S(2)}, u32[]{:S(2)}) collective-permute-start(bf16[2,256,256]{2,1,0:T(8,128)(2,1)S(1)} %get-tuple-element.30.ia), channel_id=1, source_target_pairs={{0,1},{1,0},{2,3},{3,2},{4,5},{5,4},{6,7},{7,6},{8,9},{9,8},{10,11... | collective-permute-start | bytes 786440 | tf_op jit(solution)/shard_map/ppermute | solution.py:304
  9.9 0.1 collective-permute-start.1
  9.9 1.1 %collective-permute-done.iha = bf16[2,256,256]{2,1,0:T(8,128)(2,1)S(1)} collective-permute-done((bf16[2,256,256]{2,1,0:T(8,128)(2,1)S(1)}, bf16[2,256,256]{2,1,0:T(8,128)(2,1)S(1)}, u32[]{:S(2)}, u32[]{:S(2)}) %collective-permute-start) | collective-permute-done | bytes 262176 | tf_op jit(solution)/shard_map/ppermute | solution.py:304
  11.0 0.4 collective-permute-done.1.ihb
  11.4 2.6 %near1.1 = (f32[8,256,256]{2,1,0:T(8,128)S(1)}, f32[8,256,256]{2,1,0:T(8,128)S(1)}, f32[8,256,256]{2,1,0:T(8,128)S(1)}, bf16[12,256,256]{2,1,0:T(8,128)(2,1)S(1)}, bf16[8,8,256,256]{3,2,1,0:T(8,128)(2,1)S(1)}) custom-call(s32[300]{0:T(512)S(4)} %get-tuple-element.26.lists, f32[296]{0:T(512)S(4)} %get-tuple-element.27.coefs, ...), custom_call_target="tpu_custom_call", output_to_operand_aliasing={{4}: (10, {})} | custom-call | flops 1000 | bytes 1000 | tf_op jit(solution)/shard_map/near1/pallas_call | solution.py:309
  14.0 0.0 collective-permute-done.2.xh
  14.0 1.1 %across.1 = (bf16[4,256,256]{2,1,0:T(8,128)(2,1)S(1)}, f32[8,256,256]{2,1,0:T(8,128)S(1)}, f32[8,256,256]{2,1,0:T(8,128)S(1)}) custom-call(s32[300]{0:T(512)S(4)} %get-tuple-element.26.lists, f32[296]{0:T(512)S(4)} %get-tuple-element.27.coefs, bf16[8,8,256,256]{3,2,1,0:T(8,128)(2,1)S(1)} %get-tuple-element.33.inter, ...), custom_call_target="tpu_custom_call", output_to_operand_aliasing={{1}: (5, {}), {2}: (6, {})} | custom-call | flops 1000 | bytes 1000 | tf_op jit(solution)/shard_map/across/pallas_call | solution.py:315
  15.1 0.7 %collective-permute-start.3 = (bf16[4,256,256]{2,1,0:T(8,128)(2,1)S(1)}, bf16[4,256,256]{2,1,0:T(8,128)(2,1)S(1)}, u32[]{:S(2)}, u32[]{:S(2)}) collective-permute-start(bf16[4,256,256]{2,1,0:T(8,128)(2,1)S(1)} %get-tuple-element.37.x), channel_id=1, source_target_pairs={{1,2},{3,4},{5,6},{7,8},{9,10},{11,12},{13,14},{2,1},{4,3},{6,5},{... | collective-permute-start | bytes 1572872 | tf_op jit(solution)/shard_map/ppermute | solution.py:320
  15.8 2.6 %rest.1 = (bf16[2,256,256]{2,1,0:T(8,128)(2,1)S(1)}, bf16[2,256,256]{2,1,0:T(8,128)(2,1)S(1)}, f32[8,256,256]{2,1,0:T(8,128)S(1)}, f32[8,256,256]{2,1,0:T(8,128)S(1)}, f32[8,256,256]{2,1,0:T(8,128)S(1)}) custom-call(s32[300]{0:T(512)S(4)} %get-tuple-element.26.lists, ...), custom_call_target="tpu_custom_call", output_to_operand_aliasing={{2}: (7, {}), {3}: (8, {}), {4}: (9, {})} | custom-call | flops 1000 | bytes 1000 | tf_op jit(solution)/shard_map/rest/pallas_call | solution.py:321
  18.4 7.1 %collective-permute-start.4 = (bf16[2,256,256]{2,1,0:T(8,128)(2,1)S(1)}, bf16[2,256,256]{2,1,0:T(8,128)(2,1)S(1)}, u32[]{:S(2)}, u32[]{:S(2)}) collective-permute-start(bf16[2,256,256]{2,1,0:T(8,128)(2,1)S(1)} %get-tuple-element.43.ia), channel_id=1, source_target_pairs={{0,1},{1,0},{2,3},{3,2},{4,5},{5,4},{6,7},{7,6},{8,9},{9,8},{10,11... | collective-permute-start | bytes 786440 | tf_op jit(solution)/shard_map/ppermute | solution.py:304
  25.5 0.1 collective-permute-start.5
  25.6 1.1 %collective-permute-done.4.iha = bf16[2,256,256]{2,1,0:T(8,128)(2,1)S(1)} collective-permute-done((bf16[2,256,256]{2,1,0:T(8,128)(2,1)S(1)}, bf16[2,256,256]{2,1,0:T(8,128)(2,1)S(1)}, u32[]{:S(2)}, u32[]{:S(2)}) %collective-permute-start.4) | collective-permute-done | bytes 262176 | tf_op jit(solution)/shard_map/ppermute | solution.py:304
  26.7 0.4 collective-permute-done.5.ihb
  27.1 2.6 %near2.1 = (f32[8,256,256]{2,1,0:T(8,128)S(1)}, f32[8,128]{1,0:T(8,128)S(1)}) custom-call(s32[300]{0:T(512)S(4)} %get-tuple-element.26.lists, f32[296]{0:T(512)S(4)} %get-tuple-element.27.coefs, bf16[8,8,256,256]{3,2,1,0:T(8,128)(2,1)S(1)} %get-tuple-element.33.inter, ...), custom_call_target="tpu_custom_call", output_to_operand_aliasing={{0}: (11, {})} | custom-call | flops 1000 | bytes 1000 | tf_op jit(solution)/shard_map/near2/pallas_call | solution.py:326
  29.6 0.0 collective-permute-done.3.xh
  29.6 2.7 %last.1 = (f32[32,128]{1,0:T(8,128)}, f32[8,256,256]{2,1,0:T(8,128)S(1)}) custom-call(s32[300]{0:T(512)S(4)} %get-tuple-element.26.lists, f32[296]{0:T(512)S(4)} %get-tuple-element.27.coefs, bf16[8,8,256,256]{3,2,1,0:T(8,128)(2,1)S(1)} %get-tuple-element.33.inter, ...), custom_call_target="tpu_custom_call", output_to_operand_aliasing={{1}: (7, {})} | custom-call | flops 1000 | bytes 1000 | tf_op jit(solution)/shard_map/last/pallas_call | solution.py:331
  32.4 8.3 %all-to-all-start = ((f32[16,2,128]{2,1,0:T(2,128)}), f32[16,2,128]{2,1,0:T(2,128)S(1)}, u32[]{:S(2)}, u32[]{:S(2)}) async-start(f32[16,2,128]{2,1,0:T(2,128)} %bitcast), calls=%async_computation | async-start | bytes 32768 | tf_op jit(solution)/shard_map/all_to_all | solution.py:341
  40.7 1.4 %output.1 = f32[8,256,256]{2,1,0:T(8,128)} custom-call(f32[8,256,256]{2,1,0:T(8,128)S(1)} %get-tuple-element.48.tiles), custom_call_target="tpu_custom_call" | custom-call | flops 1000000 | bytes 10000000 | tf_op jit(solution)/shard_map/output/pallas_call | solution.py:336
  42.1 5.1 %all-to-all-done = f32[16,2,128]{2,1,0:T(2,128)S(1)} async-done(((f32[16,2,128]{2,1,0:T(2,128)}), f32[16,2,128]{2,1,0:T(2,128)S(1)}, u32[]{:S(2)}, u32[]{:S(2)}) %all-to-all-start) | async-done | bytes 16416 | tf_op jit(solution)/shard_map/all_to_all | solution.py:341
  47.2 0.1 reduce_sum.9
  47.3 0.5 %multiply_sqrt_fusion = f32[2]{0:T(128)} fusion(f32[2]{0:T(128)S(1)} %reduce_sum.9), kind=kLoop, calls=%fused_computation | loop fusion | flops 2 | bytes 16 | tf_op jit(solution)/shard_map/sqrt | solution.py:342
Async XLA Ops:
  2.0 12.0 %collective-permute-start.2 = (bf16[4,256,256]{2,1,0:T(8,128)(2,1)S(1)}, bf16[4,256,256]{2,1,0:T(8,128)(2,1)S(1)}, u32[]{:S(2)}, u32[]{:S(2)}) collective-permute-start(bf16[4,256,256]{2,1,0:T(8,128)(2,1)S(1)} %first.1.x), channel_id=1, source_target_pairs={{1,2},{3,4},{5,6},{7,8},{9,10},{11,12},{13,14},{2,1},{4,3},{6,5},{... | collective-permute-start | bytes 1572872 | tf_op jit(solution)/shard_map/ppermute | solution.py:292
  5.5 5.5 %collective-permute-start = (bf16[2,256,256]{2,1,0:T(8,128)(2,1)S(1)}, bf16[2,256,256]{2,1,0:T(8,128)(2,1)S(1)}, u32[]{:S(2)}, u32[]{:S(2)}) collective-permute-start(bf16[2,256,256]{2,1,0:T(8,128)(2,1)S(1)} %get-tuple-element.30.ia), channel_id=1, source_target_pairs={{0,1},{1,0},{2,3},{3,2},{4,5},{5,4},{6,7},{7,6},{8,9},{9,8},{10,11... | collective-permute-start | bytes 786440 | tf_op jit(solution)/shard_map/ppermute | solution.py:304
  9.9 1.5 %collective-permute-start.1 = (bf16[2,256,256]{2,1,0:T(8,128)(2,1)S(1)}, bf16[2,256,256]{2,1,0:T(8,128)(2,1)S(1)}, u32[]{:S(2)}, u32[]{:S(2)}) collective-permute-start(bf16[2,256,256]{2,1,0:T(8,128)(2,1)S(1)} %get-tuple-element.31.ib), channel_id=1, source_target_pairs={{0,1},{1,0},{2,3},{3,2},{4,5},{5,4},{6,7},{7,6},{8,9},{9,8},{10,11... | collective-permute-start | bytes 786440 | tf_op jit(solution)/shard_map/ppermute | solution.py:304
  15.1 14.6 %collective-permute-start.3 = (bf16[4,256,256]{2,1,0:T(8,128)(2,1)S(1)}, bf16[4,256,256]{2,1,0:T(8,128)(2,1)S(1)}, u32[]{:S(2)}, u32[]{:S(2)}) collective-permute-start(bf16[4,256,256]{2,1,0:T(8,128)(2,1)S(1)} %get-tuple-element.37.x), channel_id=1, source_target_pairs={{1,2},{3,4},{5,6},{7,8},{9,10},{11,12},{13,14},{2,1},{4,3},{6,5},{... | collective-permute-start | bytes 1572872 | tf_op jit(solution)/shard_map/ppermute | solution.py:320
  18.4 8.3 %collective-permute-start.4 = (bf16[2,256,256]{2,1,0:T(8,128)(2,1)S(1)}, bf16[2,256,256]{2,1,0:T(8,128)(2,1)S(1)}, u32[]{:S(2)}, u32[]{:S(2)}) collective-permute-start(bf16[2,256,256]{2,1,0:T(8,128)(2,1)S(1)} %get-tuple-element.43.ia), channel_id=1, source_target_pairs={{0,1},{1,0},{2,3},{3,2},{4,5},{5,4},{6,7},{7,6},{8,9},{9,8},{10,11... | collective-permute-start | bytes 786440 | tf_op jit(solution)/shard_map/ppermute | solution.py:304
  25.5 1.5 %collective-permute-start.5 = (bf16[2,256,256]{2,1,0:T(8,128)(2,1)S(1)}, bf16[2,256,256]{2,1,0:T(8,128)(2,1)S(1)}, u32[]{:S(2)}, u32[]{:S(2)}) collective-permute-start(bf16[2,256,256]{2,1,0:T(8,128)(2,1)S(1)} %get-tuple-element.44.ib), channel_id=1, source_target_pairs={{0,1},{1,0},{2,3},{3,2},{4,5},{5,4},{6,7},{7,6},{8,9},{9,8},{10,11... | collective-permute-start | bytes 786440 | tf_op jit(solution)/shard_map/ppermute | solution.py:304
  32.4 14.8 %all-to-all-start = ((f32[16,2,128]{2,1,0:T(2,128)}), f32[16,2,128]{2,1,0:T(2,128)S(1)}, u32[]{:S(2)}, u32[]{:S(2)}) async-start(f32[16,2,128]{2,1,0:T(2,128)} %bitcast), calls=%async_computation | async-start | bytes 32768 | tf_op jit(solution)/shard_map/all_to_all | solution.py:341

commit v10 on v8

--- a/solution.py
+++ b/solution.py
@@ -251,8 +251,12 @@
     total = jnp.zeros((8, 128), F32)
     slots = slots_of(0, 8)
     refs = (lists, coefs, inter, xh, acc)
-    for half in range(2):
-        across_list_tail(2 + half, *refs)
+
+    @pl.when(jnp.maximum(lists[COUNTS + 2], lists[COUNTS + 3]) > SHORT)
+    def _():
+        for half in range(2):
+            across_list_tail(2 + half, *refs)
+
     for half in range(2):
         step((2 + half) * CAP, SHORT, *refs)
         for q in range(4 * half, 4 * half + 4):
@@ -343,7 +347,8 @@
         cost_estimate=pl.CostEstimate(flops=10**7, bytes_accessed=10**7, transcendentals=0),
     )(lists, vmem(recip), vmem(amps), vmem(acc))
     sums = lax.all_to_all(sums, "row", 0, 0, tiled=True)
-    norms = jnp.sqrt(jnp.sum(sums.reshape(count, 2, 128), axis=(0, 2)) / (amp_exch.shape[0] * count * v * v))
+    sums = sum(sums[2 * i : 2 * i + 2] for i in range(count))
+    norms = jnp.sqrt(jnp.sum(sums, axis=1) / (amp_exch.shape[0] * count * v * v))
     return out, norms
 
 

time: 47.8 us -> 47.8 us (level)
  Pallas kernels: 20.2 us -> 16.7 us
  starting transfers between devices: 17.8 us -> 21.3 us
    all_to_all x1, starting transfers between devices: 6.22 us -> 8.26 us  [on_device(): sums = lax.all_to_all(sums, 'row', 0, 0, tiled=True)]
    pallas_call x1, Pallas kernels: 4.59 us -> 2.56 us  [on_device(): pl.pallas_call(near_kernel_2, out_shape=[tiles8, pltpu.VMEM((8, 128), F32...]
    pallas_call x1, Pallas kernels: 4.03 us -> 2.59 us  [on_device(): pl.pallas_call(rest_kernel, out_shape=[tiles2, tiles2] + [tiles8] * 3, in...]
    ppermute x4, starting transfers between devices: 10.2 us -> 11.7 us  [swap(): return [vmem(lax.ppermute(h, 'row', same_chip)) for h in halves]]
  transfers between devices with their start and end apart: 7 -> 7, of which waited for: 5 -> 5; matrix products, arithmetic and copies ran while one was open for 0% -> 0% of each run, Pallas kernels for 32% -> 25%
where the time goes in v10:
time: 47.8 us; the launch traced here: 47.5 us
  starting transfers between devices  21.3 us (45%)
  Pallas kernels  16.7 us (35%)
  waiting for transfers between devices  4.81 us (10%)
  local copies, waits for them, and re-layouts  3.19 us (7%)
  between operations  0.77 us (2%)
  other arithmetic  0.65 us (1%)
    ppermute x4, starting transfers between devices, swap(): return [vmem(lax.ppermute(h, 'row', same_chip)) for h in halves]  11.7 us
    all_to_all x1, starting transfers between devices, on_device(): sums = lax.all_to_all(sums, 'row', 0, 0, tiled=True)  8.26 us
    unnamed x8, local copies, waits for them, and re-layouts  3.19 us
    ppermute x4, waiting for transfers between devices, swap(): return [vmem(lax.ppermute(h, 'row', same_chip)) for h in halves]  2.91 us
    pallas_call x1, Pallas kernels, on_device(): pl.pallas_call(second_kernel, out_shape=[tiles2, tiles2, pltpu.VMEM((8, v...  2.79 us
    pallas_call x1, Pallas kernels, on_device(): pl.pallas_call(rest_kernel, out_shape=[tiles2, tiles2] + [tiles8] * 3, in...  2.59 us
    pallas_call x1, Pallas kernels, on_device(): pl.pallas_call(near_kernel_1, out_shape=[tiles8] * 3 + [gathered, slabs],...  2.58 us
    pallas_call x1, Pallas kernels, on_device(): pl.pallas_call(near_kernel_2, out_shape=[tiles8, pltpu.VMEM((8, 128), F32...  2.56 us
  transfers between devices with their start and end apart: 7, of which 5 were waited for; matrix products, arithmetic and copies ran while one was open for 0% of the time, Pallas kernels for 25%

profile of v10, /device:TPU:0, one launch (start us, length us, event | category | flops | bytes accessed | tf_op | source)
XLA Modules:
  0.0 47.5 jit_solution(1766868897505710973)
XLA Ops:
  0.6 1.4 %first.1.x = bf16[4,256,256]{2,1,0:T(8,128)(2,1)S(1)} custom-call(bf16[8,256,256]{2,1,0:T(8,128)(2,1)} %exch.3, f32[8,256]{1,0:T(8,128)} %energy.3, f32[8]{0:T(128)} %gap.3, s32[8]{0:T(128)} %live.3), custom_call_target="tpu_custom_call" | custom-call | flops 1000 | bytes 1000 | tf_op jit(solution)/shard_map/first/pallas_call | solution.py:294
  2.0 0.7 %collective-permute-start.2 = (bf16[4,256,256]{2,1,0:T(8,128)(2,1)S(1)}, bf16[4,256,256]{2,1,0:T(8,128)(2,1)S(1)}, u32[]{:S(2)}, u32[]{:S(2)}) collective-permute-start(bf16[4,256,256]{2,1,0:T(8,128)(2,1)S(1)} %first.1.x), channel_id=1, source_target_pairs={{1,2},{3,4},{5,6},{7,8},{9,10},{11,12},{13,14},{2,1},{4,3},{6,5},{... | collective-permute-start | bytes 1572872 | tf_op jit(solution)/shard_map/ppermute | solution.py:299
  2.7 2.8 %second.1 = (bf16[2,256,256]{2,1,0:T(8,128)(2,1)S(1)}, bf16[2,256,256]{2,1,0:T(8,128)(2,1)S(1)}, bf16[8,256,256]{2,1,0:T(8,128)(2,1)S(1)}, f32[8,256]{1,0:T(8,12...) custom-call(bf16[8,256,256]{2,1,0:T(8,128)(2,1)} %exch.3, f32[8,256]{1,0:T(8,128)} %energy.3, ...), custom_call_target="tpu_custom_call" | custom-call | flops 1000 | bytes 1000 | tf_op jit(solution)/shard_map/second/pallas_call | solution.py:300
  5.5 4.4 %collective-permute-start = (bf16[2,256,256]{2,1,0:T(8,128)(2,1)S(1)}, bf16[2,256,256]{2,1,0:T(8,128)(2,1)S(1)}, u32[]{:S(2)}, u32[]{:S(2)}) collective-permute-start(bf16[2,256,256]{2,1,0:T(8,128)(2,1)S(1)} %get-tuple-element.30.ia), channel_id=1, source_target_pairs={{0,1},{1,0},{2,3},{3,2},{4,5},{5,4},{6,7},{7,6},{8,9},{9,8},{10,11... | collective-permute-start | bytes 786440 | tf_op jit(solution)/shard_map/ppermute | solution.py:311
  9.9 0.1 collective-permute-start.1
  9.9 1.1 %collective-permute-done.iha = bf16[2,256,256]{2,1,0:T(8,128)(2,1)S(1)} collective-permute-done((bf16[2,256,256]{2,1,0:T(8,128)(2,1)S(1)}, bf16[2,256,256]{2,1,0:T(8,128)(2,1)S(1)}, u32[]{:S(2)}, u32[]{:S(2)}) %collective-permute-start) | collective-permute-done | bytes 262176 | tf_op jit(solution)/shard_map/ppermute | solution.py:311
  11.0 0.4 collective-permute-done.1.ihb
  11.4 2.6 %near1.1 = (f32[8,256,256]{2,1,0:T(8,128)S(1)}, f32[8,256,256]{2,1,0:T(8,128)S(1)}, f32[8,256,256]{2,1,0:T(8,128)S(1)}, bf16[12,256,256]{2,1,0:T(8,128)(2,1)S(1)}, bf16[8,8,256,256]{3,2,1,0:T(8,128)(2,1)S(1)}) custom-call(s32[300]{0:T(512)S(4)} %get-tuple-element.26.lists, f32[296]{0:T(512)S(4)} %get-tuple-element.27.coefs, ...), custom_call_target="tpu_custom_call", output_to_operand_aliasing={{4}: (10, {})} | custom-call | flops 1000 | bytes 1000 | tf_op jit(solution)/shard_map/near1/pallas_call | solution.py:316
  14.0 0.0 collective-permute-done.2.xh
  14.0 1.1 %across.1 = (bf16[4,256,256]{2,1,0:T(8,128)(2,1)S(1)}, f32[8,256,256]{2,1,0:T(8,128)S(1)}, f32[8,256,256]{2,1,0:T(8,128)S(1)}) custom-call(s32[300]{0:T(512)S(4)} %get-tuple-element.26.lists, f32[296]{0:T(512)S(4)} %get-tuple-element.27.coefs, bf16[8,8,256,256]{3,2,1,0:T(8,128)(2,1)S(1)} %get-tuple-element.33.inter, ...), custom_call_target="tpu_custom_call", output_to_operand_aliasing={{1}: (5, {}), {2}: (6, {})} | custom-call | flops 1000 | bytes 1000 | tf_op jit(solution)/shard_map/across/pallas_call | solution.py:322
  15.1 0.7 %collective-permute-start.3 = (bf16[4,256,256]{2,1,0:T(8,128)(2,1)S(1)}, bf16[4,256,256]{2,1,0:T(8,128)(2,1)S(1)}, u32[]{:S(2)}, u32[]{:S(2)}) collective-permute-start(bf16[4,256,256]{2,1,0:T(8,128)(2,1)S(1)} %get-tuple-element.42.x), channel_id=1, source_target_pairs={{1,2},{3,4},{5,6},{7,8},{9,10},{11,12},{13,14},{2,1},{4,3},{6,5},{... | collective-permute-start | bytes 1572872 | tf_op jit(solution)/shard_map/ppermute | solution.py:327
  15.8 2.6 %rest.1 = (bf16[2,256,256]{2,1,0:T(8,128)(2,1)S(1)}, bf16[2,256,256]{2,1,0:T(8,128)(2,1)S(1)}, f32[8,256,256]{2,1,0:T(8,128)S(1)}, f32[8,256,256]{2,1,0:T(8,128)S(1)}, f32[8,256,256]{2,1,0:T(8,128)S(1)}) custom-call(s32[300]{0:T(512)S(4)} %get-tuple-element.26.lists, ...), custom_call_target="tpu_custom_call", output_to_operand_aliasing={{2}: (7, {}), {3}: (8, {}), {4}: (9, {})} | custom-call | flops 1000 | bytes 1000 | tf_op jit(solution)/shard_map/rest/pallas_call | solution.py:328
  18.4 0.0 copy-start
  18.4 0.0 copy-start.2
  18.4 7.1 %collective-permute-start.4 = (bf16[2,256,256]{2,1,0:T(8,128)(2,1)S(1)}, bf16[2,256,256]{2,1,0:T(8,128)(2,1)S(1)}, u32[]{:S(2)}, u32[]{:S(2)}) collective-permute-start(bf16[2,256,256]{2,1,0:T(8,128)(2,1)S(1)} %get-tuple-element.43.ia), channel_id=1, source_target_pairs={{0,1},{1,0},{2,3},{3,2},{4,5},{5,4},{6,7},{7,6},{8,9},{9,8},{10,11... | collective-permute-start | bytes 786440 | tf_op jit(solution)/shard_map/ppermute | solution.py:311
  25.5 0.1 collective-permute-start.5
  25.6 1.1 %collective-permute-done.4.iha = bf16[2,256,256]{2,1,0:T(8,128)(2,1)S(1)} collective-permute-done((bf16[2,256,256]{2,1,0:T(8,128)(2,1)S(1)}, bf16[2,256,256]{2,1,0:T(8,128)(2,1)S(1)}, u32[]{:S(2)}, u32[]{:S(2)}) %collective-permute-start.4) | collective-permute-done | bytes 262176 | tf_op jit(solution)/shard_map/ppermute | solution.py:311
  26.7 0.4 collective-permute-done.5.ihb
  27.1 2.6 %near2.1 = (f32[8,256,256]{2,1,0:T(8,128)S(1)}, f32[8,128]{1,0:T(8,128)S(1)}) custom-call(s32[300]{0:T(512)S(4)} %get-tuple-element.26.lists, f32[296]{0:T(512)S(4)} %get-tuple-element.27.coefs, bf16[8,8,256,256]{3,2,1,0:T(8,128)(2,1)S(1)} %get-tuple-element.33.inter, ...), custom_call_target="tpu_custom_call", output_to_operand_aliasing={{0}: (11, {})} | custom-call | flops 1000 | bytes 1000 | tf_op jit(solution)/shard_map/near2/pallas_call | solution.py:333
  29.7 0.0 copy-done
  29.7 0.0 copy-done.2
  29.7 0.0 collective-permute-done.3.xh
  29.7 2.4 %last.1 = (f32[32,128]{1,0:T(8,128)}, f32[8,256,256]{2,1,0:T(8,128)S(1)}) custom-call(s32[300]{0:T(512)S(4)} %get-tuple-element.26.lists, f32[296]{0:T(512)S(4)} %get-tuple-element.27.coefs, bf16[8,8,256,256]{3,2,1,0:T(8,128)(2,1)S(1)} %get-tuple-element.33.inter, ...), custom_call_target="tpu_custom_call", output_to_operand_aliasing={{1}: (5, {})} | custom-call | flops 1000 | bytes 1000 | tf_op jit(solution)/shard_map/last/pallas_call | solution.py:338
  32.1 8.3 %all-to-all-start = ((f32[16,2,128]{2,1,0:T(2,128)}), f32[16,2,128]{2,1,0:T(2,128)S(1)}, u32[]{:S(2)}, u32[]{:S(2)}) async-start(f32[16,2,128]{2,1,0:T(2,128)} %bitcast), calls=%async_computation | async-start | bytes 32768 | tf_op jit(solution)/shard_map/all_to_all | solution.py:349
  40.3 0.0 copy-start.1
  40.3 1.6 %copy-done.1 = f32[8,256,256]{2,1,0:T(8,128)S(1)} copy-done((f32[8,256,256]{2,1,0:T(8,128)S(1)}, f32[8,256,256]{2,1,0:T(8,128)}, u32[]{:S(2)}) %copy-start.1) | copy-done | bytes 2097176
  41.9 0.0 copy-start.3
  41.9 1.6 %copy-done.3 = f32[8,256,256]{2,1,0:T(8,128)S(1)} copy-done((f32[8,256,256]{2,1,0:T(8,128)S(1)}, f32[8,256,256]{2,1,0:T(8,128)}, u32[]{:S(2)}) %copy-start.3) | copy-done | bytes 2097176
  43.5 1.4 %output.1 = f32[8,256,256]{2,1,0:T(8,128)} custom-call(s32[300]{0:T(512)S(4)} %get-tuple-element.26.lists, f32[8,256,256]{2,1,0:T(8,128)S(1)} %copy-done.3, f32[8,256,256]{2,1,0:T(8,128)S(1)} %copy-done.1, f32[8,256,256]{2,1,0:T(8,128)S(1)} %get-tuple-element.48.acc), custom_call_target="tpu_custom_call" | custom-call | flops 10000000 | bytes 10000000 | tf_op jit(solution)/shard_map/output/pallas_call | solution.py:343
  44.9 1.9 %all-to-all-done = f32[16,2,128]{2,1,0:T(2,128)S(1)} async-done(((f32[16,2,128]{2,1,0:T(2,128)}), f32[16,2,128]{2,1,0:T(2,128)S(1)}, u32[]{:S(2)}, u32[]{:S(2)}) %all-to-all-start) | async-done | bytes 16416 | tf_op jit(solution)/shard_map/all_to_all | solution.py:349
  46.8 0.1 fusion
  46.9 0.5 %multiply_sqrt_fusion = f32[2]{0:T(128)} fusion(f32[2]{0:T(128)S(1)} %fusion), kind=kLoop, calls=%fused_computation.16 | loop fusion | flops 2 | bytes 16 | tf_op jit(solution)/shard_map/sqrt | solution.py:351
Async XLA Ops:
  2.0 12.0 %collective-permute-start.2 = (bf16[4,256,256]{2,1,0:T(8,128)(2,1)S(1)}, bf16[4,256,256]{2,1,0:T(8,128)(2,1)S(1)}, u32[]{:S(2)}, u32[]{:S(2)}) collective-permute-start(bf16[4,256,256]{2,1,0:T(8,128)(2,1)S(1)} %first.1.x), channel_id=1, source_target_pairs={{1,2},{3,4},{5,6},{7,8},{9,10},{11,12},{13,14},{2,1},{4,3},{6,5},{... | collective-permute-start | bytes 1572872 | tf_op jit(solution)/shard_map/ppermute | solution.py:299
  5.5 5.5 %collective-permute-start = (bf16[2,256,256]{2,1,0:T(8,128)(2,1)S(1)}, bf16[2,256,256]{2,1,0:T(8,128)(2,1)S(1)}, u32[]{:S(2)}, u32[]{:S(2)}) collective-permute-start(bf16[2,256,256]{2,1,0:T(8,128)(2,1)S(1)} %get-tuple-element.30.ia), channel_id=1, source_target_pairs={{0,1},{1,0},{2,3},{3,2},{4,5},{5,4},{6,7},{7,6},{8,9},{9,8},{10,11... | collective-permute-start | bytes 786440 | tf_op jit(solution)/shard_map/ppermute | solution.py:311
  9.9 1.5 %collective-permute-start.1 = (bf16[2,256,256]{2,1,0:T(8,128)(2,1)S(1)}, bf16[2,256,256]{2,1,0:T(8,128)(2,1)S(1)}, u32[]{:S(2)}, u32[]{:S(2)}) collective-permute-start(bf16[2,256,256]{2,1,0:T(8,128)(2,1)S(1)} %get-tuple-element.31.ib), channel_id=1, source_target_pairs={{0,1},{1,0},{2,3},{3,2},{4,5},{5,4},{6,7},{7,6},{8,9},{9,8},{10,11... | collective-permute-start | bytes 786440 | tf_op jit(solution)/shard_map/ppermute | solution.py:311
  15.1 14.6 %collective-permute-start.3 = (bf16[4,256,256]{2,1,0:T(8,128)(2,1)S(1)}, bf16[4,256,256]{2,1,0:T(8,128)(2,1)S(1)}, u32[]{:S(2)}, u32[]{:S(2)}) collective-permute-start(bf16[4,256,256]{2,1,0:T(8,128)(2,1)S(1)} %get-tuple-element.42.x), channel_id=1, source_target_pairs={{1,2},{3,4},{5,6},{7,8},{9,10},{11,12},{13,14},{2,1},{4,3},{6,5},{... | collective-permute-start | bytes 1572872 | tf_op jit(solution)/shard_map/ppermute | solution.py:327
  18.4 11.3 %copy-start = (f32[8,256,256]{2,1,0:T(8,128)}, f32[8,256,256]{2,1,0:T(8,128)S(1)}, u32[]{:S(2)}) copy-start(f32[8,256,256]{2,1,0:T(8,128)S(1)} %get-tuple-element.41.amps) | copy-start | bytes 6291460
  18.4 11.3 %copy-start.2 = (f32[8,256,256]{2,1,0:T(8,128)}, f32[8,256,256]{2,1,0:T(8,128)S(1)}, u32[]{:S(2)}) copy-start(f32[8,256,256]{2,1,0:T(8,128)S(1)} %get-tuple-element.40.recip) | copy-start | bytes 6291460
  18.4 8.3 %collective-permute-start.4 = (bf16[2,256,256]{2,1,0:T(8,128)(2,1)S(1)}, bf16[2,256,256]{2,1,0:T(8,128)(2,1)S(1)}, u32[]{:S(2)}, u32[]{:S(2)}) collective-permute-start(bf16[2,256,256]{2,1,0:T(8,128)(2,1)S(1)} %get-tuple-element.43.ia), channel_id=1, source_target_pairs={{0,1},{1,0},{2,3},{3,2},{4,5},{5,4},{6,7},{7,6},{8,9},{9,8},{10,11... | collective-permute-start | bytes 786440 | tf_op jit(solution)/shard_map/ppermute | solution.py:311
  25.5 1.5 %collective-permute-start.5 = (bf16[2,256,256]{2,1,0:T(8,128)(2,1)S(1)}, bf16[2,256,256]{2,1,0:T(8,128)(2,1)S(1)}, u32[]{:S(2)}, u32[]{:S(2)}) collective-permute-start(bf16[2,256,256]{2,1,0:T(8,128)(2,1)S(1)} %get-tuple-element.44.ib), channel_id=1, source_target_pairs={{0,1},{1,0},{2,3},{3,2},{4,5},{5,4},{6,7},{7,6},{8,9},{9,8},{10,11... | collective-permute-start | bytes 786440 | tf_op jit(solution)/shard_map/ppermute | solution.py:311
  32.1 14.8 %all-to-all-start = ((f32[16,2,128]{2,1,0:T(2,128)}), f32[16,2,128]{2,1,0:T(2,128)S(1)}, u32[]{:S(2)}, u32[]{:S(2)}) async-start(f32[16,2,128]{2,1,0:T(2,128)} %bitcast), calls=%async_computation | async-start | bytes 32768 | tf_op jit(solution)/shard_map/all_to_all | solution.py:349
  40.3 1.6 %copy-start.1 = (f32[8,256,256]{2,1,0:T(8,128)S(1)}, f32[8,256,256]{2,1,0:T(8,128)}, u32[]{:S(2)}) copy-start(f32[8,256,256]{2,1,0:T(8,128)} %copy-done) | copy-start | bytes 6291460
  41.9 1.6 %copy-start.3 = (f32[8,256,256]{2,1,0:T(8,128)S(1)}, f32[8,256,256]{2,1,0:T(8,128)}, u32[]{:S(2)}) copy-start(f32[8,256,256]{2,1,0:T(8,128)} %copy-done.2) | copy-start | bytes 6291460

commit v11 on v8

--- a/solution.py
+++ b/solution.py
@@ -64,7 +64,11 @@
     for c in small:
         c.wait()
     dens = denominators(en, [gp[p] for p in slots], slots)
-    factors = [-lv[p].astype(F32) / dens[i] for i, p in enumerate(slots)]
+    factors = []
+    for i, p in enumerate(slots):
+        guess = pl.reciprocal(dens[i], approx=True)
+        guess = guess * (2.0 - dens[i] * guess)
+        factors.append(-lv[p].astype(F32) * (guess * (2.0 - dens[i] * guess)))
     for i in range(4):
         tiles[i].wait()
         out[i] = (buf[i].astype(F32) * factors[i]).astype(BF16)

time: 47.8 us -> 48 us (level)
  starting transfers between devices: 17.8 us -> 20.7 us
  Pallas kernels: 20.2 us -> 17.5 us
    pallas_call x1, Pallas kernels: 4.03 us -> 2.59 us  [on_device(): pl.pallas_call(rest_kernel, out_shape=[tiles2, tiles2] + [tiles8] * 3, in...]
    all_to_all x1, starting transfers between devices: 6.22 us -> 7.65 us  [on_device(): sums = lax.all_to_all(sums, 'row', 0, 0, tiled=True)]
    pallas_call x1, Pallas kernels: 4.59 us -> 3.16 us  [on_device(): pl.pallas_call(near_kernel_2, out_shape=[tiles8, pltpu.VMEM((8, 128), F32...]
    ppermute x4, starting transfers between devices: 10.2 us -> 11.7 us  [swap(): return [vmem(lax.ppermute(h, 'row', same_chip)) for h in halves]]
  transfers between devices with their start and end apart: 7 -> 7, of which waited for: 5 -> 5; matrix products, arithmetic and copies ran while one was open for 0% -> 0% of each run, Pallas kernels for 32% -> 26%
where the time goes in v11:
time: 48 us; the launch traced here: 47.6 us
  starting transfers between devices  20.7 us (43%)
  Pallas kernels  17.5 us (36%)
  waiting for transfers between devices  4.81 us (10%)
  local copies, waits for them, and re-layouts  3.19 us (7%)
  between operations  0.77 us (2%)
  other arithmetic  0.66 us (1%)
    ppermute x4, starting transfers between devices, swap(): return [vmem(lax.ppermute(h, 'row', same_chip)) for h in halves]  11.7 us
    all_to_all x1, starting transfers between devices, on_device(): sums = lax.all_to_all(sums, 'row', 0, 0, tiled=True)  7.65 us
    unnamed x8, local copies, waits for them, and re-layouts  3.19 us
    pallas_call x1, Pallas kernels, on_device(): pl.pallas_call(near_kernel_2, out_shape=[tiles8, pltpu.VMEM((8, 128), F32...  3.16 us
    ppermute x4, waiting for transfers between devices, swap(): return [vmem(lax.ppermute(h, 'row', same_chip)) for h in halves]  2.91 us
    pallas_call x1, Pallas kernels, on_device(): pl.pallas_call(second_kernel, out_shape=[tiles2, tiles2, pltpu.VMEM((8, v...  2.79 us
    pallas_call x1, Pallas kernels, on_device(): pl.pallas_call(rest_kernel, out_shape=[tiles2, tiles2] + [tiles8] * 3, in...  2.59 us
    pallas_call x1, Pallas kernels, on_device(): pl.pallas_call(near_kernel_1, out_shape=[tiles8] * 3 + [gathered, slabs],...  2.58 us
  transfers between devices with their start and end apart: 7, of which 5 were waited for; matrix products, arithmetic and copies ran while one was open for 0% of the time, Pallas kernels for 26%

profile of v11, /device:TPU:0, one launch (start us, length us, event | category | flops | bytes accessed | tf_op | source)
XLA Modules:
  0.0 47.6 jit_solution(5782571886599062222)
XLA Ops:
  0.6 1.5 %first.1.x = bf16[4,256,256]{2,1,0:T(8,128)(2,1)S(1)} custom-call(bf16[8,256,256]{2,1,0:T(8,128)(2,1)} %exch.3, f32[8,256]{1,0:T(8,128)} %energy.3, f32[8]{0:T(128)} %gap.3, s32[8]{0:T(128)} %live.3), custom_call_target="tpu_custom_call" | custom-call | flops 1000 | bytes 1000 | tf_op jit(solution)/shard_map/first/pallas_call | solution.py:294
  2.2 0.7 %collective-permute-start.2 = (bf16[4,256,256]{2,1,0:T(8,128)(2,1)S(1)}, bf16[4,256,256]{2,1,0:T(8,128)(2,1)S(1)}, u32[]{:S(2)}, u32[]{:S(2)}) collective-permute-start(bf16[4,256,256]{2,1,0:T(8,128)(2,1)S(1)} %first.1.x), channel_id=1, source_target_pairs={{1,2},{3,4},{5,6},{7,8},{9,10},{11,12},{13,14},{2,1},{4,3},{6,5},{... | collective-permute-start | bytes 1572872 | tf_op jit(solution)/shard_map/ppermute | solution.py:299
  2.9 2.8 %second.1 = (bf16[2,256,256]{2,1,0:T(8,128)(2,1)S(1)}, bf16[2,256,256]{2,1,0:T(8,128)(2,1)S(1)}, bf16[8,256,256]{2,1,0:T(8,128)(2,1)S(1)}, f32[8,256]{1,0:T(8,12...) custom-call(bf16[8,256,256]{2,1,0:T(8,128)(2,1)} %exch.3, f32[8,256]{1,0:T(8,128)} %energy.3, ...), custom_call_target="tpu_custom_call" | custom-call | flops 1000 | bytes 1000 | tf_op jit(solution)/shard_map/second/pallas_call | solution.py:300
  5.6 4.4 %collective-permute-start = (bf16[2,256,256]{2,1,0:T(8,128)(2,1)S(1)}, bf16[2,256,256]{2,1,0:T(8,128)(2,1)S(1)}, u32[]{:S(2)}, u32[]{:S(2)}) collective-permute-start(bf16[2,256,256]{2,1,0:T(8,128)(2,1)S(1)} %get-tuple-element.30.ia), channel_id=1, source_target_pairs={{0,1},{1,0},{2,3},{3,2},{4,5},{5,4},{6,7},{7,6},{8,9},{9,8},{10,11... | collective-permute-start | bytes 786440 | tf_op jit(solution)/shard_map/ppermute | solution.py:311
  10.0 0.1 collective-permute-start.1
  10.1 1.1 %collective-permute-done.iha = bf16[2,256,256]{2,1,0:T(8,128)(2,1)S(1)} collective-permute-done((bf16[2,256,256]{2,1,0:T(8,128)(2,1)S(1)}, bf16[2,256,256]{2,1,0:T(8,128)(2,1)S(1)}, u32[]{:S(2)}, u32[]{:S(2)}) %collective-permute-start) | collective-permute-done | bytes 262176 | tf_op jit(solution)/shard_map/ppermute | solution.py:311
  11.2 0.4 collective-permute-done.1.ihb
  11.5 2.6 %near1.1 = (f32[8,256,256]{2,1,0:T(8,128)S(1)}, f32[8,256,256]{2,1,0:T(8,128)S(1)}, f32[8,256,256]{2,1,0:T(8,128)S(1)}, bf16[12,256,256]{2,1,0:T(8,128)(2,1)S(1)}, bf16[8,8,256,256]{3,2,1,0:T(8,128)(2,1)S(1)}) custom-call(s32[300]{0:T(512)S(4)} %get-tuple-element.26.lists, f32[296]{0:T(512)S(4)} %get-tuple-element.27.coefs, ...), custom_call_target="tpu_custom_call", output_to_operand_aliasing={{4}: (10, {})} | custom-call | flops 1000 | bytes 1000 | tf_op jit(solution)/shard_map/near1/pallas_call | solution.py:316
  14.1 0.0 collective-permute-done.2.xh
  14.1 1.1 %across.1 = (bf16[4,256,256]{2,1,0:T(8,128)(2,1)S(1)}, f32[8,256,256]{2,1,0:T(8,128)S(1)}, f32[8,256,256]{2,1,0:T(8,128)S(1)}) custom-call(s32[300]{0:T(512)S(4)} %get-tuple-element.26.lists, f32[296]{0:T(512)S(4)} %get-tuple-element.27.coefs, bf16[8,8,256,256]{3,2,1,0:T(8,128)(2,1)S(1)} %get-tuple-element.33.inter, ...), custom_call_target="tpu_custom_call", output_to_operand_aliasing={{1}: (5, {}), {2}: (6, {})} | custom-call | flops 1000 | bytes 1000 | tf_op jit(solution)/shard_map/across/pallas_call | solution.py:322
  15.2 0.7 %collective-permute-start.3 = (bf16[4,256,256]{2,1,0:T(8,128)(2,1)S(1)}, bf16[4,256,256]{2,1,0:T(8,128)(2,1)S(1)}, u32[]{:S(2)}, u32[]{:S(2)}) collective-permute-start(bf16[4,256,256]{2,1,0:T(8,128)(2,1)S(1)} %get-tuple-element.42.x), channel_id=1, source_target_pairs={{1,2},{3,4},{5,6},{7,8},{9,10},{11,12},{13,14},{2,1},{4,3},{6,5},{... | collective-permute-start | bytes 1572872 | tf_op jit(solution)/shard_map/ppermute | solution.py:327
  15.9 2.6 %rest.1 = (bf16[2,256,256]{2,1,0:T(8,128)(2,1)S(1)}, bf16[2,256,256]{2,1,0:T(8,128)(2,1)S(1)}, f32[8,256,256]{2,1,0:T(8,128)S(1)}, f32[8,256,256]{2,1,0:T(8,128)S(1)}, f32[8,256,256]{2,1,0:T(8,128)S(1)}) custom-call(s32[300]{0:T(512)S(4)} %get-tuple-element.26.lists, ...), custom_call_target="tpu_custom_call", output_to_operand_aliasing={{2}: (7, {}), {3}: (8, {}), {4}: (9, {})} | custom-call | flops 1000 | bytes 1000 | tf_op jit(solution)/shard_map/rest/pallas_call | solution.py:328
  18.5 0.0 copy-start
  18.5 0.0 copy-start.2
  18.6 7.1 %collective-permute-start.4 = (bf16[2,256,256]{2,1,0:T(8,128)(2,1)S(1)}, bf16[2,256,256]{2,1,0:T(8,128)(2,1)S(1)}, u32[]{:S(2)}, u32[]{:S(2)}) collective-permute-start(bf16[2,256,256]{2,1,0:T(8,128)(2,1)S(1)} %get-tuple-element.43.ia), channel_id=1, source_target_pairs={{0,1},{1,0},{2,3},{3,2},{4,5},{5,4},{6,7},{7,6},{8,9},{9,8},{10,11... | collective-permute-start | bytes 786440 | tf_op jit(solution)/shard_map/ppermute | solution.py:311
  25.7 0.1 collective-permute-start.5
  25.8 1.1 %collective-permute-done.4.iha = bf16[2,256,256]{2,1,0:T(8,128)(2,1)S(1)} collective-permute-done((bf16[2,256,256]{2,1,0:T(8,128)(2,1)S(1)}, bf16[2,256,256]{2,1,0:T(8,128)(2,1)S(1)}, u32[]{:S(2)}, u32[]{:S(2)}) %collective-permute-start.4) | collective-permute-done | bytes 262176 | tf_op jit(solution)/shard_map/ppermute | solution.py:311
  26.9 0.4 collective-permute-done.5.ihb
  27.2 3.2 %near2.1 = (f32[8,256,256]{2,1,0:T(8,128)S(1)}, f32[8,128]{1,0:T(8,128)S(1)}) custom-call(s32[300]{0:T(512)S(4)} %get-tuple-element.26.lists, f32[296]{0:T(512)S(4)} %get-tuple-element.27.coefs, bf16[8,8,256,256]{3,2,1,0:T(8,128)(2,1)S(1)} %get-tuple-element.33.inter, ...), custom_call_target="tpu_custom_call", output_to_operand_aliasing={{0}: (11, {})} | custom-call | flops 1000 | bytes 1000 | tf_op jit(solution)/shard_map/near2/pallas_call | solution.py:333
  30.4 0.0 copy-done
  30.4 0.0 copy-done.2
  30.4 0.0 collective-permute-done.3.xh
  30.4 2.4 %last.1 = (f32[32,128]{1,0:T(8,128)}, f32[8,256,256]{2,1,0:T(8,128)S(1)}) custom-call(s32[300]{0:T(512)S(4)} %get-tuple-element.26.lists, f32[296]{0:T(512)S(4)} %get-tuple-element.27.coefs, bf16[8,8,256,256]{3,2,1,0:T(8,128)(2,1)S(1)} %get-tuple-element.33.inter, ...), custom_call_target="tpu_custom_call", output_to_operand_aliasing={{1}: (5, {})} | custom-call | flops 1000 | bytes 1000 | tf_op jit(solution)/shard_map/last/pallas_call | solution.py:338
  32.8 7.6 %all-to-all-start = ((f32[16,2,128]{2,1,0:T(2,128)}), f32[16,2,128]{2,1,0:T(2,128)S(1)}, u32[]{:S(2)}, u32[]{:S(2)}) async-start(f32[16,2,128]{2,1,0:T(2,128)} %bitcast), calls=%async_computation | async-start | bytes 32768 | tf_op jit(solution)/shard_map/all_to_all | solution.py:349
  40.5 0.0 copy-start.1
  40.5 1.6 %copy-done.1 = f32[8,256,256]{2,1,0:T(8,128)S(1)} copy-done((f32[8,256,256]{2,1,0:T(8,128)S(1)}, f32[8,256,256]{2,1,0:T(8,128)}, u32[]{:S(2)}) %copy-start.1) | copy-done | bytes 2097176
  42.1 0.0 copy-start.3
  42.1 1.6 %copy-done.3 = f32[8,256,256]{2,1,0:T(8,128)S(1)} copy-done((f32[8,256,256]{2,1,0:T(8,128)S(1)}, f32[8,256,256]{2,1,0:T(8,128)}, u32[]{:S(2)}) %copy-start.3) | copy-done | bytes 2097176
  43.7 1.4 %output.1 = f32[8,256,256]{2,1,0:T(8,128)} custom-call(s32[300]{0:T(512)S(4)} %get-tuple-element.26.lists, f32[8,256,256]{2,1,0:T(8,128)S(1)} %copy-done.3, f32[8,256,256]{2,1,0:T(8,128)S(1)} %copy-done.1, f32[8,256,256]{2,1,0:T(8,128)S(1)} %get-tuple-element.48.acc), custom_call_target="tpu_custom_call" | custom-call | flops 10000000 | bytes 10000000 | tf_op jit(solution)/shard_map/output/pallas_call | solution.py:343
  45.1 1.9 %all-to-all-done = f32[16,2,128]{2,1,0:T(2,128)S(1)} async-done(((f32[16,2,128]{2,1,0:T(2,128)}), f32[16,2,128]{2,1,0:T(2,128)S(1)}, u32[]{:S(2)}, u32[]{:S(2)}) %all-to-all-start) | async-done | bytes 16416 | tf_op jit(solution)/shard_map/all_to_all | solution.py:349
  47.0 0.1 reduce_sum.9
  47.1 0.5 %multiply_sqrt_fusion = f32[2]{0:T(128)} fusion(f32[2]{0:T(128)S(1)} %reduce_sum.9), kind=kLoop, calls=%fused_computation | loop fusion | flops 2 | bytes 16 | tf_op jit(solution)/shard_map/sqrt | solution.py:350
Async XLA Ops:
  2.2 12.0 %collective-permute-start.2 = (bf16[4,256,256]{2,1,0:T(8,128)(2,1)S(1)}, bf16[4,256,256]{2,1,0:T(8,128)(2,1)S(1)}, u32[]{:S(2)}, u32[]{:S(2)}) collective-permute-start(bf16[4,256,256]{2,1,0:T(8,128)(2,1)S(1)} %first.1.x), channel_id=1, source_target_pairs={{1,2},{3,4},{5,6},{7,8},{9,10},{11,12},{13,14},{2,1},{4,3},{6,5},{... | collective-permute-start | bytes 1572872 | tf_op jit(solution)/shard_map/ppermute | solution.py:299
  5.6 5.5 %collective-permute-start = (bf16[2,256,256]{2,1,0:T(8,128)(2,1)S(1)}, bf16[2,256,256]{2,1,0:T(8,128)(2,1)S(1)}, u32[]{:S(2)}, u32[]{:S(2)}) collective-permute-start(bf16[2,256,256]{2,1,0:T(8,128)(2,1)S(1)} %get-tuple-element.30.ia), channel_id=1, source_target_pairs={{0,1},{1,0},{2,3},{3,2},{4,5},{5,4},{6,7},{7,6},{8,9},{9,8},{10,11... | collective-permute-start | bytes 786440 | tf_op jit(solution)/shard_map/ppermute | solution.py:311
  10.0 1.5 %collective-permute-start.1 = (bf16[2,256,256]{2,1,0:T(8,128)(2,1)S(1)}, bf16[2,256,256]{2,1,0:T(8,128)(2,1)S(1)}, u32[]{:S(2)}, u32[]{:S(2)}) collective-permute-start(bf16[2,256,256]{2,1,0:T(8,128)(2,1)S(1)} %get-tuple-element.31.ib), channel_id=1, source_target_pairs={{0,1},{1,0},{2,3},{3,2},{4,5},{5,4},{6,7},{7,6},{8,9},{9,8},{10,11... | collective-permute-start | bytes 786440 | tf_op jit(solution)/shard_map/ppermute | solution.py:311
  15.2 15.2 %collective-permute-start.3 = (bf16[4,256,256]{2,1,0:T(8,128)(2,1)S(1)}, bf16[4,256,256]{2,1,0:T(8,128)(2,1)S(1)}, u32[]{:S(2)}, u32[]{:S(2)}) collective-permute-start(bf16[4,256,256]{2,1,0:T(8,128)(2,1)S(1)} %get-tuple-element.42.x), channel_id=1, source_target_pairs={{1,2},{3,4},{5,6},{7,8},{9,10},{11,12},{13,14},{2,1},{4,3},{6,5},{... | collective-permute-start | bytes 1572872 | tf_op jit(solution)/shard_map/ppermute | solution.py:327
  18.5 11.9 %copy-start = (f32[8,256,256]{2,1,0:T(8,128)}, f32[8,256,256]{2,1,0:T(8,128)S(1)}, u32[]{:S(2)}) copy-start(f32[8,256,256]{2,1,0:T(8,128)S(1)} %get-tuple-element.41.amps) | copy-start | bytes 6291460
  18.5 11.9 %copy-start.2 = (f32[8,256,256]{2,1,0:T(8,128)}, f32[8,256,256]{2,1,0:T(8,128)S(1)}, u32[]{:S(2)}) copy-start(f32[8,256,256]{2,1,0:T(8,128)S(1)} %get-tuple-element.40.recip) | copy-start | bytes 6291460
  18.6 8.3 %collective-permute-start.4 = (bf16[2,256,256]{2,1,0:T(8,128)(2,1)S(1)}, bf16[2,256,256]{2,1,0:T(8,128)(2,1)S(1)}, u32[]{:S(2)}, u32[]{:S(2)}) collective-permute-start(bf16[2,256,256]{2,1,0:T(8,128)(2,1)S(1)} %get-tuple-element.43.ia), channel_id=1, source_target_pairs={{0,1},{1,0},{2,3},{3,2},{4,5},{5,4},{6,7},{7,6},{8,9},{9,8},{10,11... | collective-permute-start | bytes 786440 | tf_op jit(solution)/shard_map/ppermute | solution.py:311
  25.7 1.5 %collective-permute-start.5 = (bf16[2,256,256]{2,1,0:T(8,128)(2,1)S(1)}, bf16[2,256,256]{2,1,0:T(8,128)(2,1)S(1)}, u32[]{:S(2)}, u32[]{:S(2)}) collective-permute-start(bf16[2,256,256]{2,1,0:T(8,128)(2,1)S(1)} %get-tuple-element.44.ib), channel_id=1, source_target_pairs={{0,1},{1,0},{2,3},{3,2},{4,5},{5,4},{6,7},{7,6},{8,9},{9,8},{10,11... | collective-permute-start | bytes 786440 | tf_op jit(solution)/shard_map/ppermute | solution.py:311
  32.8 14.2 %all-to-all-start = ((f32[16,2,128]{2,1,0:T(2,128)}), f32[16,2,128]{2,1,0:T(2,128)S(1)}, u32[]{:S(2)}, u32[]{:S(2)}) async-start(f32[16,2,128]{2,1,0:T(2,128)} %bitcast), calls=%async_computation | async-start | bytes 32768 | tf_op jit(solution)/shard_map/all_to_all | solution.py:349
  40.5 1.6 %copy-start.1 = (f32[8,256,256]{2,1,0:T(8,128)S(1)}, f32[8,256,256]{2,1,0:T(8,128)}, u32[]{:S(2)}) copy-start(f32[8,256,256]{2,1,0:T(8,128)} %copy-done) | copy-start | bytes 6291460
  42.1 1.6 %copy-start.3 = (f32[8,256,256]{2,1,0:T(8,128)S(1)}, f32[8,256,256]{2,1,0:T(8,128)}, u32[]{:S(2)}) copy-start(f32[8,256,256]{2,1,0:T(8,128)} %copy-done.2) | copy-start | bytes 6291460

commit v12 on v8

--- a/solution.py
+++ b/solution.py
@@ -13,7 +13,7 @@
 SM = pl.BlockSpec(memory_space=pltpu.SMEM)
 AN = pl.BlockSpec(memory_space=pl.ANY)
 CAP = 72
-LONG, SHORT = 16, 8
+LONG, SHORT = 24, 8
 COUNTS, LIVE = 4 * CAP, 4 * CAP + 4
 GAP = 4 * CAP
 MIB = 1 << 20

time: 47.8 us -> 47.8 us (level)
  transfers between devices with their start and end apart: 7 -> 7, of which waited for: 5 -> 5; matrix products, arithmetic and copies ran while one was open for 0% -> 0% of each run, Pallas kernels for 32% -> 33%
where the time goes in v12:
time: 47.8 us; the launch traced here: 47.5 us
  Pallas kernels  20.6 us (43%)
  starting transfers between devices  17.4 us (36%)
  waiting for transfers between devices  4.81 us (10%)
  local copies, waits for them, and re-layouts  3.19 us (7%)
  between operations  0.77 us (2%)
  other arithmetic  0.66 us (1%)
    ppermute x4, starting transfers between devices, swap(): return [vmem(lax.ppermute(h, 'row', same_chip)) for h in halves]  10.2 us
    all_to_all x1, starting transfers between devices, on_device(): sums = lax.all_to_all(sums, 'row', 0, 0, tiled=True)  5.83 us
    pallas_call x1, Pallas kernels, on_device(): pl.pallas_call(near_kernel_2, out_shape=[tiles8, pltpu.VMEM((8, 128), F32...  4.94 us
    pallas_call x1, Pallas kernels, on_device(): pl.pallas_call(rest_kernel, out_shape=[tiles2, tiles2] + [tiles8] * 3, in...  4.01 us
    unnamed x8, local copies, waits for them, and re-layouts  3.19 us
    ppermute x4, waiting for transfers between devices, swap(): return [vmem(lax.ppermute(h, 'row', same_chip)) for h in halves]  2.91 us
    pallas_call x1, Pallas kernels, on_device(): pl.pallas_call(second_kernel, out_shape=[tiles2, tiles2, pltpu.VMEM((8, v...  2.79 us
    pallas_call x1, Pallas kernels, on_device(): pl.pallas_call(near_kernel_1, out_shape=[tiles8] * 3 + [gathered, slabs],...  2.65 us
  transfers between devices with their start and end apart: 7, of which 5 were waited for; matrix products, arithmetic and copies ran while one was open for 0% of the time, Pallas kernels for 33%

profile of v12, /device:TPU:0, one launch (start us, length us, event | category | flops | bytes accessed | tf_op | source)
XLA Modules:
  0.0 47.5 jit_solution(12607672601121860860)
XLA Ops:
  0.6 1.4 %first.1.x = bf16[4,256,256]{2,1,0:T(8,128)(2,1)S(1)} custom-call(bf16[8,256,256]{2,1,0:T(8,128)(2,1)} %exch.3, f32[8,256]{1,0:T(8,128)} %energy.3, f32[8]{0:T(128)} %gap.3, s32[8]{0:T(128)} %live.3), custom_call_target="tpu_custom_call" | custom-call | flops 1000 | bytes 1000 | tf_op jit(solution)/shard_map/first/pallas_call | solution.py:290
  2.0 0.7 %collective-permute-start.2 = (bf16[4,256,256]{2,1,0:T(8,128)(2,1)S(1)}, bf16[4,256,256]{2,1,0:T(8,128)(2,1)S(1)}, u32[]{:S(2)}, u32[]{:S(2)}) collective-permute-start(bf16[4,256,256]{2,1,0:T(8,128)(2,1)S(1)} %first.1.x), channel_id=1, source_target_pairs={{1,2},{3,4},{5,6},{7,8},{9,10},{11,12},{13,14},{2,1},{4,3},{6,5},{... | collective-permute-start | bytes 1572872 | tf_op jit(solution)/shard_map/ppermute | solution.py:295
  2.7 2.8 %second.1 = (bf16[2,256,256]{2,1,0:T(8,128)(2,1)S(1)}, bf16[2,256,256]{2,1,0:T(8,128)(2,1)S(1)}, bf16[8,256,256]{2,1,0:T(8,128)(2,1)S(1)}, f32[8,256]{1,0:T(8,12...) custom-call(bf16[8,256,256]{2,1,0:T(8,128)(2,1)} %exch.3, f32[8,256]{1,0:T(8,128)} %energy.3, ...), custom_call_target="tpu_custom_call" | custom-call | flops 1000 | bytes 1000 | tf_op jit(solution)/shard_map/second/pallas_call | solution.py:296
  5.5 4.4 %collective-permute-start = (bf16[2,256,256]{2,1,0:T(8,128)(2,1)S(1)}, bf16[2,256,256]{2,1,0:T(8,128)(2,1)S(1)}, u32[]{:S(2)}, u32[]{:S(2)}) collective-permute-start(bf16[2,256,256]{2,1,0:T(8,128)(2,1)S(1)} %get-tuple-element.30.ia), channel_id=1, source_target_pairs={{0,1},{1,0},{2,3},{3,2},{4,5},{5,4},{6,7},{7,6},{8,9},{9,8},{10,11... | collective-permute-start | bytes 786440 | tf_op jit(solution)/shard_map/ppermute | solution.py:307
  9.9 0.1 collective-permute-start.1
  9.9 1.1 %collective-permute-done.iha = bf16[2,256,256]{2,1,0:T(8,128)(2,1)S(1)} collective-permute-done((bf16[2,256,256]{2,1,0:T(8,128)(2,1)S(1)}, bf16[2,256,256]{2,1,0:T(8,128)(2,1)S(1)}, u32[]{:S(2)}, u32[]{:S(2)}) %collective-permute-start) | collective-permute-done | bytes 262176 | tf_op jit(solution)/shard_map/ppermute | solution.py:307
  11.0 0.4 collective-permute-done.1.ihb
  11.4 2.6 %near1.1 = (f32[8,256,256]{2,1,0:T(8,128)S(1)}, f32[8,256,256]{2,1,0:T(8,128)S(1)}, f32[8,256,256]{2,1,0:T(8,128)S(1)}, bf16[12,256,256]{2,1,0:T(8,128)(2,1)S(1)}, bf16[8,8,256,256]{3,2,1,0:T(8,128)(2,1)S(1)}) custom-call(s32[300]{0:T(512)S(4)} %get-tuple-element.26.lists, f32[296]{0:T(512)S(4)} %get-tuple-element.27.coefs, ...), custom_call_target="tpu_custom_call", output_to_operand_aliasing={{4}: (10, {})} | custom-call | flops 1000 | bytes 1000 | tf_op jit(solution)/shard_map/near1/pallas_call | solution.py:312
  14.1 0.0 collective-permute-done.2.xh
  14.1 1.1 %across.1 = (bf16[4,256,256]{2,1,0:T(8,128)(2,1)S(1)}, f32[8,256,256]{2,1,0:T(8,128)S(1)}, f32[8,256,256]{2,1,0:T(8,128)S(1)}) custom-call(s32[300]{0:T(512)S(4)} %get-tuple-element.26.lists, f32[296]{0:T(512)S(4)} %get-tuple-element.27.coefs, bf16[8,8,256,256]{3,2,1,0:T(8,128)(2,1)S(1)} %get-tuple-element.33.inter, ...), custom_call_target="tpu_custom_call", output_to_operand_aliasing={{1}: (5, {}), {2}: (6, {})} | custom-call | flops 1000 | bytes 1000 | tf_op jit(solution)/shard_map/across/pallas_call | solution.py:318
  15.1 0.7 %collective-permute-start.3 = (bf16[4,256,256]{2,1,0:T(8,128)(2,1)S(1)}, bf16[4,256,256]{2,1,0:T(8,128)(2,1)S(1)}, u32[]{:S(2)}, u32[]{:S(2)}) collective-permute-start(bf16[4,256,256]{2,1,0:T(8,128)(2,1)S(1)} %get-tuple-element.42.x), channel_id=1, source_target_pairs={{1,2},{3,4},{5,6},{7,8},{9,10},{11,12},{13,14},{2,1},{4,3},{6,5},{... | collective-permute-start | bytes 1572872 | tf_op jit(solution)/shard_map/ppermute | solution.py:323
  15.8 4.0 %rest.1 = (bf16[2,256,256]{2,1,0:T(8,128)(2,1)S(1)}, bf16[2,256,256]{2,1,0:T(8,128)(2,1)S(1)}, f32[8,256,256]{2,1,0:T(8,128)S(1)}, f32[8,256,256]{2,1,0:T(8,128)S(1)}, f32[8,256,256]{2,1,0:T(8,128)S(1)}) custom-call(s32[300]{0:T(512)S(4)} %get-tuple-element.26.lists, ...), custom_call_target="tpu_custom_call", output_to_operand_aliasing={{2}: (7, {}), {3}: (8, {}), {4}: (9, {})} | custom-call | flops 1000 | bytes 1000 | tf_op jit(solution)/shard_map/rest/pallas_call | solution.py:324
  19.9 0.0 copy-start
  19.9 0.0 copy-start.2
  19.9 5.7 %collective-permute-start.4 = (bf16[2,256,256]{2,1,0:T(8,128)(2,1)S(1)}, bf16[2,256,256]{2,1,0:T(8,128)(2,1)S(1)}, u32[]{:S(2)}, u32[]{:S(2)}) collective-permute-start(bf16[2,256,256]{2,1,0:T(8,128)(2,1)S(1)} %get-tuple-element.43.ia), channel_id=1, source_target_pairs={{0,1},{1,0},{2,3},{3,2},{4,5},{5,4},{6,7},{7,6},{8,9},{9,8},{10,11... | collective-permute-start | bytes 786440 | tf_op jit(solution)/shard_map/ppermute | solution.py:307
  25.6 0.1 collective-permute-start.5
  25.7 1.1 %collective-permute-done.4.iha = bf16[2,256,256]{2,1,0:T(8,128)(2,1)S(1)} collective-permute-done((bf16[2,256,256]{2,1,0:T(8,128)(2,1)S(1)}, bf16[2,256,256]{2,1,0:T(8,128)(2,1)S(1)}, u32[]{:S(2)}, u32[]{:S(2)}) %collective-permute-start.4) | collective-permute-done | bytes 262176 | tf_op jit(solution)/shard_map/ppermute | solution.py:307
  26.7 0.4 collective-permute-done.5.ihb
  27.1 4.9 %near2.1 = (f32[8,256,256]{2,1,0:T(8,128)S(1)}, f32[8,128]{1,0:T(8,128)S(1)}) custom-call(s32[300]{0:T(512)S(4)} %get-tuple-element.26.lists, f32[296]{0:T(512)S(4)} %get-tuple-element.27.coefs, bf16[8,8,256,256]{3,2,1,0:T(8,128)(2,1)S(1)} %get-tuple-element.33.inter, ...), custom_call_target="tpu_custom_call", output_to_operand_aliasing={{0}: (11, {})} | custom-call | flops 1000 | bytes 1000 | tf_op jit(solution)/shard_map/near2/pallas_call | solution.py:329
  32.1 0.0 copy-done
  32.1 0.0 copy-done.2
  32.1 0.0 collective-permute-done.3.xh
  32.1 2.4 %last.1 = (f32[32,128]{1,0:T(8,128)}, f32[8,256,256]{2,1,0:T(8,128)S(1)}) custom-call(s32[300]{0:T(512)S(4)} %get-tuple-element.26.lists, f32[296]{0:T(512)S(4)} %get-tuple-element.27.coefs, bf16[8,8,256,256]{3,2,1,0:T(8,128)(2,1)S(1)} %get-tuple-element.33.inter, ...), custom_call_target="tpu_custom_call", output_to_operand_aliasing={{1}: (5, {})} | custom-call | flops 1000 | bytes 1000 | tf_op jit(solution)/shard_map/last/pallas_call | solution.py:334
  34.5 5.8 %all-to-all-start = ((f32[16,2,128]{2,1,0:T(2,128)}), f32[16,2,128]{2,1,0:T(2,128)S(1)}, u32[]{:S(2)}, u32[]{:S(2)}) async-start(f32[16,2,128]{2,1,0:T(2,128)} %bitcast), calls=%async_computation | async-start | bytes 32768 | tf_op jit(solution)/shard_map/all_to_all | solution.py:345
  40.3 0.0 copy-start.1
  40.3 1.6 %copy-done.1 = f32[8,256,256]{2,1,0:T(8,128)S(1)} copy-done((f32[8,256,256]{2,1,0:T(8,128)S(1)}, f32[8,256,256]{2,1,0:T(8,128)}, u32[]{:S(2)}) %copy-start.1) | copy-done | bytes 2097176
  41.9 0.0 copy-start.3
  41.9 1.6 %copy-done.3 = f32[8,256,256]{2,1,0:T(8,128)S(1)} copy-done((f32[8,256,256]{2,1,0:T(8,128)S(1)}, f32[8,256,256]{2,1,0:T(8,128)}, u32[]{:S(2)}) %copy-start.3) | copy-done | bytes 2097176
  43.5 1.4 %output.1 = f32[8,256,256]{2,1,0:T(8,128)} custom-call(s32[300]{0:T(512)S(4)} %get-tuple-element.26.lists, f32[8,256,256]{2,1,0:T(8,128)S(1)} %copy-done.3, f32[8,256,256]{2,1,0:T(8,128)S(1)} %copy-done.1, f32[8,256,256]{2,1,0:T(8,128)S(1)} %get-tuple-element.48.acc), custom_call_target="tpu_custom_call" | custom-call | flops 10000000 | bytes 10000000 | tf_op jit(solution)/shard_map/output/pallas_call | solution.py:339
  44.9 1.9 %all-to-all-done = f32[16,2,128]{2,1,0:T(2,128)S(1)} async-done(((f32[16,2,128]{2,1,0:T(2,128)}), f32[16,2,128]{2,1,0:T(2,128)S(1)}, u32[]{:S(2)}, u32[]{:S(2)}) %all-to-all-start) | async-done | bytes 16416 | tf_op jit(solution)/shard_map/all_to_all | solution.py:345
  46.8 0.1 reduce_sum.9
  47.0 0.5 %multiply_sqrt_fusion = f32[2]{0:T(128)} fusion(f32[2]{0:T(128)S(1)} %reduce_sum.9), kind=kLoop, calls=%fused_computation | loop fusion | flops 2 | bytes 16 | tf_op jit(solution)/shard_map/sqrt | solution.py:346
Async XLA Ops:
  2.0 12.1 %collective-permute-start.2 = (bf16[4,256,256]{2,1,0:T(8,128)(2,1)S(1)}, bf16[4,256,256]{2,1,0:T(8,128)(2,1)S(1)}, u32[]{:S(2)}, u32[]{:S(2)}) collective-permute-start(bf16[4,256,256]{2,1,0:T(8,128)(2,1)S(1)} %first.1.x), channel_id=1, source_target_pairs={{1,2},{3,4},{5,6},{7,8},{9,10},{11,12},{13,14},{2,1},{4,3},{6,5},{... | collective-permute-start | bytes 1572872 | tf_op jit(solution)/shard_map/ppermute | solution.py:295
  5.5 5.5 %collective-permute-start = (bf16[2,256,256]{2,1,0:T(8,128)(2,1)S(1)}, bf16[2,256,256]{2,1,0:T(8,128)(2,1)S(1)}, u32[]{:S(2)}, u32[]{:S(2)}) collective-permute-start(bf16[2,256,256]{2,1,0:T(8,128)(2,1)S(1)} %get-tuple-element.30.ia), channel_id=1, source_target_pairs={{0,1},{1,0},{2,3},{3,2},{4,5},{5,4},{6,7},{7,6},{8,9},{9,8},{10,11... | collective-permute-start | bytes 786440 | tf_op jit(solution)/shard_map/ppermute | solution.py:307
  9.9 1.5 %collective-permute-start.1 = (bf16[2,256,256]{2,1,0:T(8,128)(2,1)S(1)}, bf16[2,256,256]{2,1,0:T(8,128)(2,1)S(1)}, u32[]{:S(2)}, u32[]{:S(2)}) collective-permute-start(bf16[2,256,256]{2,1,0:T(8,128)(2,1)S(1)} %get-tuple-element.31.ib), channel_id=1, source_target_pairs={{0,1},{1,0},{2,3},{3,2},{4,5},{5,4},{6,7},{7,6},{8,9},{9,8},{10,11... | collective-permute-start | bytes 786440 | tf_op jit(solution)/shard_map/ppermute | solution.py:307
  15.1 17.0 %collective-permute-start.3 = (bf16[4,256,256]{2,1,0:T(8,128)(2,1)S(1)}, bf16[4,256,256]{2,1,0:T(8,128)(2,1)S(1)}, u32[]{:S(2)}, u32[]{:S(2)}) collective-permute-start(bf16[4,256,256]{2,1,0:T(8,128)(2,1)S(1)} %get-tuple-element.42.x), channel_id=1, source_target_pairs={{1,2},{3,4},{5,6},{7,8},{9,10},{11,12},{13,14},{2,1},{4,3},{6,5},{... | collective-permute-start | bytes 1572872 | tf_op jit(solution)/shard_map/ppermute | solution.py:323
  19.9 12.2 %copy-start = (f32[8,256,256]{2,1,0:T(8,128)}, f32[8,256,256]{2,1,0:T(8,128)S(1)}, u32[]{:S(2)}) copy-start(f32[8,256,256]{2,1,0:T(8,128)S(1)} %get-tuple-element.41.amps) | copy-start | bytes 6291460
  19.9 12.2 %copy-start.2 = (f32[8,256,256]{2,1,0:T(8,128)}, f32[8,256,256]{2,1,0:T(8,128)S(1)}, u32[]{:S(2)}) copy-start(f32[8,256,256]{2,1,0:T(8,128)S(1)} %get-tuple-element.40.recip) | copy-start | bytes 6291460
  19.9 6.9 %collective-permute-start.4 = (bf16[2,256,256]{2,1,0:T(8,128)(2,1)S(1)}, bf16[2,256,256]{2,1,0:T(8,128)(2,1)S(1)}, u32[]{:S(2)}, u32[]{:S(2)}) collective-permute-start(bf16[2,256,256]{2,1,0:T(8,128)(2,1)S(1)} %get-tuple-element.43.ia), channel_id=1, source_target_pairs={{0,1},{1,0},{2,3},{3,2},{4,5},{5,4},{6,7},{7,6},{8,9},{9,8},{10,11... | collective-permute-start | bytes 786440 | tf_op jit(solution)/shard_map/ppermute | solution.py:307
  25.6 1.5 %collective-permute-start.5 = (bf16[2,256,256]{2,1,0:T(8,128)(2,1)S(1)}, bf16[2,256,256]{2,1,0:T(8,128)(2,1)S(1)}, u32[]{:S(2)}, u32[]{:S(2)}) collective-permute-start(bf16[2,256,256]{2,1,0:T(8,128)(2,1)S(1)} %get-tuple-element.44.ib), channel_id=1, source_target_pairs={{0,1},{1,0},{2,3},{3,2},{4,5},{5,4},{6,7},{7,6},{8,9},{9,8},{10,11... | collective-permute-start | bytes 786440 | tf_op jit(solution)/shard_map/ppermute | solution.py:307
  34.5 12.3 %all-to-all-start = ((f32[16,2,128]{2,1,0:T(2,128)}), f32[16,2,128]{2,1,0:T(2,128)S(1)}, u32[]{:S(2)}, u32[]{:S(2)}) async-start(f32[16,2,128]{2,1,0:T(2,128)} %bitcast), calls=%async_computation | async-start | bytes 32768 | tf_op jit(solution)/shard_map/all_to_all | solution.py:345
  40.3 1.6 %copy-start.1 = (f32[8,256,256]{2,1,0:T(8,128)S(1)}, f32[8,256,256]{2,1,0:T(8,128)}, u32[]{:S(2)}) copy-start(f32[8,256,256]{2,1,0:T(8,128)} %copy-done) | copy-start | bytes 6291460
  41.9 1.6 %copy-start.3 = (f32[8,256,256]{2,1,0:T(8,128)S(1)}, f32[8,256,256]{2,1,0:T(8,128)}, u32[]{:S(2)}) copy-start(f32[8,256,256]{2,1,0:T(8,128)} %copy-done.2) | copy-start | bytes 6291460
